TPU v7x, 32 devices: a whole 2x2x4 slice. The times are simulated.
32 devices in a mesh: seq: 8 (over z, core), mp: 4 (over y, x).
Axes of the slice: x: 2, y: 2, z: 4, core: 2. Of those that a mesh axis runs over, the one named last changes fastest.
Arguments:
- fine_rows: bfloat16 [24576, 4096], P(('seq', 'mp')), may hold values from -6 to 6
- w_inputs: bfloat16 [4096, 4, 4096], P(None, None, 'mp'), may hold values from -0.375 to 0.375
- w_out: bfloat16 [4096, 4096], P('mp'), may hold values from -0.09375 to 0.09375
- head_gain: float32 [4096], P('mp'), may hold values from 0.1 to 1.9
- decay_log: float32 [32, 6144], P('mp', 'seq'), may hold values from -1 to 0, as said below
Outputs:
- fine_output: bfloat16 [24576, 4096], P(('seq', 'mp'))
Inputs may be any that keep to these rules, and one draw needn't show every extreme that they name: `decay_log`: entries are logarithms of decay factors, one for each head and coarse row.
All inputs are finite; a program needn't handle non-finite values.
Results may differ from a plain program's by a relative error of at most 0.018.
Values may be sent and summed in bfloat16 or wider, within the bound.
No kernel may reach another device: no remote copies, remote signals or barrier semaphores. Data moves between devices by JAX's collectives and lax.ppermute only.
A program may use at most 192 MiB of HBM per device.

v0:
```python
import jax
import jax.numpy as jnp
from jax import lax
from jax.sharding import PartitionSpec as P

D = 4096
ATTENDER_NUMBER = 32
SF = 4
CH = 128


EPSILON = 1e-05


def passed_along(value, axis, by):
    peers = lax.axis_size(axis)
    pairs = [(i, i + by) for i in range(peers) if 0 <= i + by < peers]
    return lax.ppermute(value, axis, pairs)


def body(fine_rows, w_inputs, w_out, head_gain, decay_log):
    model_width = fine_rows.shape[1]
    head_dim = D // ATTENDER_NUMBER
    local_heads = decay_log.shape[0]
    local_width = local_heads * head_dim
    rows_coarse = decay_log.shape[1]
    blocks = rows_coarse // CH
    fine_count = fine_rows.shape[0]
    tail_rows = fine_rows[fine_count - (SF - 1) :]
    before = passed_along(tail_rows, ("seq", "mp"), 1)
    widened = jnp.concatenate([before, fine_rows[: fine_count - (SF - 1)]], axis=0).astype(
        jnp.float32
    )
    pooled = jnp.mean(widened.reshape(-1, SF, model_width), axis=1).astype(jnp.bfloat16)
    weights_flat = w_inputs.reshape(model_width, 4 * local_width)
    projected = jnp.dot(
        lax.all_gather(pooled, "mp", axis=0, tiled=True),
        weights_flat,
        preferred_element_type=jnp.float32,
    )
    queries = (
        projected[:, :local_width].astype(jnp.bfloat16).reshape(blocks, CH, local_heads, head_dim)
    )
    key_rows = (
        projected[:, local_width : 2 * local_width]
        .astype(jnp.bfloat16)
        .reshape(blocks, CH, local_heads, head_dim)
    )
    values = (
        projected[:, 2 * local_width : 3 * local_width]
        .astype(jnp.bfloat16)
        .reshape(blocks, CH, local_heads, head_dim)
    )
    gate_values = projected[:, 3 * local_width :]
    cumulative = jnp.cumsum(decay_log.reshape(local_heads, blocks, CH), axis=2)
    gaps = cumulative[:, :, :, None] - cumulative[:, :, None, :]
    causal = jnp.arange(CH)[:, None] >= jnp.arange(CH)[None, :]
    weight = jnp.where(causal, jnp.exp(jnp.minimum(gaps, 0.0)), 0.0)
    scores = jnp.einsum("cthd,cshd->hcts", queries, key_rows, preferred_element_type=jnp.float32)
    scores = (scores * weight).astype(jnp.bfloat16)
    within = jnp.einsum("hcts,cshd->cthd", scores, values, preferred_element_type=jnp.float32)
    remaining = jnp.exp(cumulative[:, :, -1:] - cumulative)
    decayed_keys = (
        key_rows.astype(jnp.float32) * jnp.transpose(remaining, (1, 2, 0))[..., None]
    ).astype(jnp.bfloat16)
    block_states = jnp.einsum(
        "cshd,cshe->chde", decayed_keys, values, preferred_element_type=jnp.float32
    )
    block_decay = cumulative[:, :, -1]
    prefix_states = []
    prefix_decay = []
    running = jnp.zeros((local_heads, head_dim, head_dim), jnp.float32)
    decay_total = jnp.zeros((local_heads,), jnp.float32)
    for block_index in range(blocks):
        prefix_states.append(running)
        prefix_decay.append(decay_total)
        running = (
            jnp.exp(block_decay[:, block_index])[:, None, None] * running
            + block_states[block_index]
        )
        decay_total = decay_total + block_decay[:, block_index]
    shard_totals = lax.all_gather(decay_total[None, :], "seq", axis=0, tiled=True)
    my_rank = lax.axis_index("seq")
    running_ends = jnp.cumsum(shard_totals, axis=0)
    before_mine = lax.dynamic_slice_in_dim(running_ends - shard_totals, my_rank, 1, 0)
    shard_states = lax.all_gather(
        running[None].astype(jnp.bfloat16), "seq", axis=0, tiled=True
    ).astype(jnp.float32)
    row_count = shard_states.shape[0]
    span_sums = before_mine - running_ends
    device_rank = jnp.arange(row_count, dtype=jnp.int32)
    factor = jnp.where((device_rank < my_rank)[:, None], jnp.exp(jnp.minimum(span_sums, 0.0)), 0.0)
    incoming = jnp.zeros_like(running) + jnp.sum(factor[:, :, None, None] * shard_states, axis=0)
    entering = jnp.stack(
        [
            jnp.exp(prefix_decay[block_index])[:, None, None] * incoming
            + prefix_states[block_index]
            for block_index in range(blocks)
        ]
    )
    carried = jnp.einsum(
        "cthd,chde->cthe",
        queries,
        entering.astype(jnp.bfloat16),
        preferred_element_type=jnp.float32,
    )
    carried = carried * jnp.transpose(jnp.exp(cumulative), (1, 2, 0))[..., None]
    attended = (within + carried).reshape(rows_coarse, local_heads, head_dim)
    square_mean = jnp.mean(attended * attended, axis=2, keepdims=True)
    normed = (attended * lax.rsqrt(square_mean + EPSILON)).reshape(rows_coarse, local_width)
    gated_rows = (normed * head_gain * jax.nn.silu(gate_values)).astype(jnp.bfloat16)
    coarse = lax.psum_scatter(
        jnp.dot(gated_rows, w_out, preferred_element_type=jnp.float32).astype(jnp.bfloat16),
        "mp",
        scatter_dimension=0,
        tiled=True,
    ).astype(jnp.float32)
    upsampled = jnp.repeat(coarse, SF, axis=0)
    return (fine_rows.astype(jnp.float32) + upsampled).astype(jnp.bfloat16)


def solution(mesh):
    return jax.shard_map(
        body,
        mesh=mesh,
        in_specs=(
            P(("seq", "mp"), None),
            P(None, None, "mp"),
            P("mp", None),
            P("mp"),
            P("mp", "seq"),
        ),
        out_specs=P(("seq", "mp"), None),
        check_vma=False,
    )
```

profile of v0, /device:TPU:0, one launch (start us, length us, event | category | flops | bytes accessed | tf_op | source)
XLA Modules:
  0.0 327.0 jit_solution(3557057617605105759)
XLA Ops:
  6.5 0.9 slice.67
  7.4 4.8 %collective-permute-start = (bf16[3,4096]{1,0:T(4,128)(2,1)S(1)}, bf16[3,4096]{1,0:T(4,128)(2,1)S(1)}, u32[]{:S(2)}, u32[]{:S(2)}) collective-permute-start(bf16[3,4096]{1,0:T(4,128)(2,1)S(1)} %slice.67), channel_id=1, source_target_pairs={{0,1},{1,2},{2,3},{3,4},{4,5},{5,6},{6,7},{7,8},{8,9},{9,10},{10,1... | collective-permute-start | bytes 73736 | tf_op jit(solution)/shard_map/ppermute | solution.py:18
  12.3 1.6 collective-permute-done
  13.8 9.3 %maximum_convert_fusion = f32[768,4096]{1,0:T(8,128)} fusion(bf16[765,4096]{1,0:T(8,128)(2,1)} %bitcast.96, bf16[3,4096]{1,0:T(4,128)(2,1)S(1)} %collective-permute-done), kind=kLoop, calls=%fused_computation.2 | loop fusion | flops 12582912 | bytes 18874368 | tf_op jit(solution)/shard_map/convert_element_type | solution.py:31
  23.1 14.4 %reshape.289 = f32[192,4,4096]{2,1,0:T(4,128)} reshape(f32[768,4096]{1,0:T(8,128)} %maximum_convert_fusion) | data formatting | bytes 25165824 | tf_op jit(solution)/shard_map/convert_element_type | solution.py:31
  37.5 10.1 %reduce_sum.27 = f32[192,4096]{1,0:T(8,128)S(1)} reduce(f32[192,4,4096]{2,1,0:T(4,128)} %reshape.289, f32[]{:T(128)} %constant.9.clone.1), dimensions={1}, to_apply=%region_0.0 | reduce | flops 2359296 | bytes 15728644 | tf_op jit(solution)/shard_map/reduce_sum | solution.py:34
  47.6 1.4 multiply_convert_fusion.2
  49.0 0.2 all-gather.6.cloned.1.call-start
  49.2 1.7 reduce_window_sum.24
  51.0 0.1 copy.44
  51.2 0.1 copy.35
  51.3 23.4 %copy.45 = bf16[512,8,4,1024]{3,1,2,0:T(8,128)(2,1)} copy(bf16[512,8,4,1024]{3,2,1,0:T(4,128)(2,1)} %bitcast.94) | data formatting | bytes 67108864
  74.7 0.4 exponential_reduce_fusion
  75.1 46.3 %all-gather.4.cloned.1.call-done = bf16[768,4096]{1,0:T(8,128)(2,1)} async-done(((bf16[192,4096]{1,0:T(8,128)(2,1)}), bf16[768,4096]{1,0:T(8,128)(2,1)}) %all-gather.4.cloned.1.call-update) | async-done | bytes 6291472 | tf_op jit(solution)/shard_map/all_gather | solution.py:37
  121.4 33.5 %fusion.39 = (bf16[768,4096]{1,0:T(8,128)(2,1)S(1)}, f32[768,4096]{1,0:T(8,128)}) fusion(bf16[768,4096]{1,0:T(8,128)(2,1)} %all-gather.4.cloned.1.call-done, bf16[4096,4096]{1,0:T(8,128)(2,1)} %bitcast.95), kind=kOutput, calls=%fused_computation.85 | convolution fusion | flops 25772949504 | bytes 58720256 | tf_op jit(solution)/shard_map/dot_general | solution.py:36
  154.9 2.2 slice_bitcast_fusion.1
  157.2 0.4 copy.48
  157.6 1.8 copy.36
  159.4 0.4 copy.46
  159.9 0.9 copy-done.1
  160.8 0.6 fusion.5
  161.4 1.3 fusion.19
  162.8 0.6 dynamic-slice
  164.0 0.2 dynamic-update-slice
  164.3 17.0 %all-reduce = f32[64]{0:T(128)S(1)} all-reduce(f32[64]{0:T(128)S(1)} %dynamic-update-slice), channel_id=2, replica_groups=mesh['seq'=8,'mp'=4] {'seq'}, use_global_device_ids=true, to_apply=%add | all-reduce | flops 64 | bytes 512
  181.5 3.1 copy.47
  184.6 5.6 %fusion.4 = f32[6,8,128,128]{3,2,1,0:T(8,128)} fusion(bf16[6,128,8,128]{1,3,2,0:T(8,128)(2,1)} %copy.36, f32[8,6,128]{2,0,1:T(8,128)S(1)} %reduce_window_sum.24, pred[128,128]{1,0:T(8,128)(4,1)S(1)} %iota_compare_fusion, bf16[6,128,8,128]{3,2,1,0:T(8,128)(2,1)} %bitcast.101, bf16[6,128,8,128]{3,2,1,0:T(8,128)(2,1)} %bitcast.97), kind=kOutput, calls=%fused_computation.14 | convolution fusion | flops 406585344 | bytes 7905280 | tf_op jit(solution)/shard_map/hcts,cshd->cthd/dot_general | solution.py:61
  190.2 2.0 all-gather.6.cloned.1.call-done
  192.2 2.2 multiply_reduce_fusion
  194.5 0.2 fusion.34
  194.7 0.2 fusion.33
  194.9 0.2 fusion.32
  195.1 0.4 copy-done.3
  195.5 0.2 fusion.31
  195.6 0.2 fusion.30
  195.8 0.3 copy-done
  196.1 1.0 copy-done.6
  197.1 1.3 multiply_reduce_fusion.1
  198.4 0.6 rsqrt_bitcast_fusion
  199.0 0.9 copy.42
  199.9 2.4 copy.41
  202.2 0.9 mul.226
  203.1 1.0 copy-done.5
  204.1 12.9 %convolution_convert_fusion = bf16[768,4096]{1,0:T(8,128)(2,1)} fusion(bf16[1024,4096]{1,0:T(8,128)(2,1)} %param.7, f32[96,8,8,128]{3,2,1,0:T(8,128)S(1)} %bitcast.103, f32[96,8,8,128]{3,2,1,0:T(8,128)S(1)} %bitcast.102, f32[768,4096]{1,0:T(8,128)} %get-tuple-element.25, f32[1024]{0:T(1024)S(1)} %copy-done.8), kind=kOutput, calls=%fused_computation.1 | convolution fusion | flops 6451888128 | bytes 24121344 | tf_op jit(solution)/shard_map/dot_general | solution.py:113
  217.0 69.8 %reduce-scatter.2.cloned.1.call-done = bf16[192,4096]{1,0:T(8,128)(2,1)} async-done(((bf16[768,4096]{1,0:T(8,128)(2,1)}), bf16[192,4096]{1,0:T(8,128)(2,1)}) %reduce-scatter.2.cloned.1.call-update) | async-done | bytes 1572880 | tf_op jit(solution)/shard_map/reduce_scatter | solution.py:112
  286.8 7.5 %broadcast_in_dim.19 = f32[192,4,4096]{2,1,0:T(4,128)} broadcast(bf16[192,4096]{1,0:T(8,128)(2,1)} %reduce-scatter.2.cloned.1.call-done), dimensions={0,2} | broadcast | bytes 14155776 | tf_op jit(solution)/shard_map/broadcast_in_dim | solution.py:118
  294.3 14.7 %reshape.288 = f32[768,4096]{1,0:T(8,128)} reshape(f32[192,4,4096]{2,1,0:T(4,128)} %broadcast_in_dim.19) | data formatting | bytes 25165824 | tf_op jit(solution)/shard_map/reshape | solution.py:118
  309.0 11.5 %add_convert_fusion = bf16[768,4096]{1,0:T(8,128)(2,1)} fusion(f32[768,4096]{1,0:T(8,128)} %reshape.288, bf16[768,4096]{1,0:T(8,128)(2,1)} %param.5), kind=kLoop, calls=%fused_computation | loop fusion | flops 9437184 | bytes 25165824 | tf_op jit(solution)/shard_map/convert_element_type | solution.py:119
  (32 shorter events, 0.5 us)
Async XLA Ops:
  6.5 114.9 %all-gather.4.cloned.1.call-start = ((), (), s32[]{:S(2)}) async-start(), calls=%async_computation.1 | async-start | bytes 7864320 | tf_op jit(solution)/shard_map/all_gather | solution.py:37
  7.4 6.4 %collective-permute-start = (bf16[3,4096]{1,0:T(4,128)(2,1)S(1)}, bf16[3,4096]{1,0:T(4,128)(2,1)S(1)}, u32[]{:S(2)}, u32[]{:S(2)}) collective-permute-start(bf16[3,4096]{1,0:T(4,128)(2,1)S(1)} %slice.67), channel_id=1, source_target_pairs={{0,1},{1,2},{2,3},{3,4},{4,5},{5,6},{6,7},{7,8},{8,9},{9,10},{10,1... | collective-permute-start | bytes 73736 | tf_op jit(solution)/shard_map/ppermute | solution.py:18
  47.6 1.6 copy-start.7
  49.0 143.2 %all-gather.6.cloned.1.call-start = ((), (), s32[]{:S(2)}) async-start(), calls=%async_computation.2 | async-start | bytes 2359296 | tf_op jit(solution)/shard_map/all_gather | solution.py:86
  159.4 1.4 copy-start.1
  159.9 1.5 copy-start.2
  161.4 1.4 copy-start.9
  162.7 124.1 %reduce-scatter.2.cloned.1.call-start = ((), (), s32[]{:S(2)}) async-start(), calls=%async_computation.3 | async-start | bytes 7864320 | tf_op jit(solution)/shard_map/reduce_scatter | solution.py:112
  192.2 2.4 copy-start.4
  194.4 1.0 copy-start.3
  194.7 1.4 copy-start
  194.7 2.4 copy-start.6
  202.2 1.9 copy-start.5
  202.2 1.9 copy-start.8
Sparse Core Ops, SparseCore 0:
  49.1 72.2 all-gather.3
  162.8 29.3 all-gather.5
  217.2 69.6 reduce-scatter.1
where the time goes:
time: 328 us; the launch traced here: 327 us
  waiting for transfers between devices  120 us (37%)
  local copies, waits for them, and re-layouts  77.8 us (24%)
  matrix products  53.8 us (16%)
  other arithmetic  39.5 us (12%)
  blocking collectives  17 us (5%)
  between operations  14 us (4%)
  starting transfers between devices  5.11 us (2%)
    reduce_scatter x1, waiting for transfers between devices, body(): lax.psum_scatter(jnp.dot(gated_rows, w_out, preferred_element_type=jnp.fl...  69.8 us
    all_gather x1, waiting for transfers between devices, body(): lax.all_gather(pooled, 'mp', axis=0, tiled=True)  46.3 us
    unnamed x28, local copies, waits for them, and re-layouts  34 us
    dot_general x1, matrix products, body(): jnp.dot(lax.all_gather(pooled, 'mp', axis=0, tiled=True), weights_flat, p...  33.5 us
    unnamed x1, blocking collectives  17 us
    reshape x1, local copies, waits for them, and re-layouts, body(): upsampled = jnp.repeat(coarse, SF, axis=0)  14.7 us
    convert_element_type x1, local copies, waits for them, and re-layouts, body(): jnp.concatenate([before, fine_rows[:fine_count - (SF - 1)]], axis=0)  14.4 us
    dot_general x1, matrix products, body(): jnp.dot(gated_rows, w_out, preferred_element_type=jnp.float32)  12.9 us
  transfers between devices with their start and end apart: 4, of which 4 were waited for; matrix products, arithmetic and copies ran while one was open for 11% of the time, Pallas kernels for 0%

commit v1 on v0

--- a/solution.py
+++ b/solution.py
@@ -1,21 +1,519 @@
 import jax
 import jax.numpy as jnp
 from jax import lax
+from jax.experimental import pallas as pl
+from jax.experimental.pallas import tpu as pltpu
 from jax.sharding import PartitionSpec as P
 
 D = 4096
 ATTENDER_NUMBER = 32
 SF = 4
 CH = 128
+HD = D // ATTENDER_NUMBER
 
 
 EPSILON = 1e-05
+BF = jnp.bfloat16
+F32 = jnp.float32
+VMEM_LIMIT = 48 * 2**20
 
 
 def passed_along(value, axis, by):
     peers = lax.axis_size(axis)
     pairs = [(i, i + by) for i in range(peers) if 0 <= i + by < peers]
     return lax.ppermute(value, axis, pairs)
+
+
+def swapped(value, axis, bit):
+    peers = lax.axis_size(axis)
+    return lax.ppermute(value, axis, [(i, i ^ bit) for i in range(peers)])
+
+
+def params(**kw):
+    return pltpu.CompilerParams(vmem_limit_bytes=VMEM_LIMIT, **kw)
+
+
+def cost(flops, size):
+    return pl.CostEstimate(flops=int(flops), bytes_accessed=int(size), transcendentals=0)
+
+
+def dot(a, b):
+    return jnp.dot(a, b, preferred_element_type=F32)
+
+
+def dot_dims(a, b, da, db):
+    return lax.dot_general(a, b, (((da,), (db,)), ((), ())), preferred_element_type=F32)
+
+
+def pool_half(fine, tail, block, tail_block):
+    rows, width = fine.shape[0] // 2, fine.shape[1]
+    out_rows, cols = rows // SF, min(width, 1024)
+
+    def kernel(tail_ref, fine_ref, out_ref):
+        j = lax.broadcasted_iota(jnp.int32, (out_rows, rows), 0) * SF
+        i = lax.broadcasted_iota(jnp.int32, (out_rows, rows), 1)
+        main = jnp.where((i <= j) & (i > j - SF), 1.0 / SF, 0.0).astype(BF)
+        jt = lax.broadcasted_iota(jnp.int32, (out_rows, 16), 0) * SF
+        it = lax.broadcasted_iota(jnp.int32, (out_rows, 16), 1) - 16
+        ahead = jnp.where((it <= jt) & (it > jt - SF), 1.0 / SF, 0.0).astype(BF)
+        total = dot(main, fine_ref[...]) + dot(ahead, tail_ref[...])
+        out_ref[...] = total.astype(BF)
+
+    return pl.pallas_call(
+        kernel,
+        grid=(width // cols,),
+        in_specs=[
+            pl.BlockSpec((16, cols), lambda c: (tail_block, c)),
+            pl.BlockSpec((rows, cols), lambda c: (block, c)),
+        ],
+        out_specs=pl.BlockSpec((out_rows, cols), lambda c: (0, c)),
+        out_shape=jax.ShapeDtypeStruct((out_rows, width), BF),
+        compiler_params=params(),
+        cost_estimate=cost(2 * out_rows * rows * width, 2 * rows * width),
+    )(tail, fine)
+
+
+def project(pieces, weights, firsts, width):
+    piece_rows, depth = pieces[0].shape
+    count, rows, cols = len(pieces), len(pieces) * pieces[0].shape[0], 256
+    per = width // cols
+    ranges = len(firsts)
+
+    def kernel(*refs):
+        ins, w_ref, outs, held = refs[:count], refs[count], refs[count + 1 : count + 1 + ranges], refs[-1]
+        step = pl.program_id(0)
+
+        @pl.when(step == 0)
+        def _():
+            for n in range(count):
+                held[n * piece_rows : (n + 1) * piece_rows] = ins[n][...]
+
+        result = dot(held[...], w_ref[...])
+        for n in range(ranges):
+
+            @pl.when(step // per == n)
+            def _():
+                outs[n][...] = result.astype(outs[n].dtype)
+
+    def w_index(step):
+        block = firsts[0] // cols + step % per
+        for n in range(1, ranges):
+            block = jnp.where(step // per == n, firsts[n] // cols + step % per, block)
+        return (0, block)
+
+    def out_index(n):
+        return lambda step: (0, jnp.clip(step - n * per, 0, per - 1))
+
+    return pl.pallas_call(
+        kernel,
+        grid=(ranges * per,),
+        in_specs=[pl.BlockSpec((piece_rows, depth), lambda step: (0, 0))] * count
+        + [pl.BlockSpec((depth, cols), w_index)],
+        out_specs=[pl.BlockSpec((rows, cols), out_index(n)) for n in range(ranges)],
+        out_shape=[
+            jax.ShapeDtypeStruct((rows, width), F32 if n == ranges - 1 else BF) for n in range(ranges)
+        ],
+        scratch_shapes=[pltpu.VMEM((rows, depth), BF)],
+        compiler_params=params(),
+        cost_estimate=cost(2 * rows * depth * width * ranges, 2 * depth * width * ranges),
+    )(*pieces, weights)
+
+
+def natural_units(me):
+    x, y, d = me ^ 1, me ^ 2, me ^ 3
+    return [2 * me, 2 * me + 1, 2 * x, 2 * y + 1, 2 * x + 1, 2 * y, 2 * d, 2 * d + 1]
+
+
+def last_keys_and_state(me, pieces, weights, first, second, cum_columns, width):
+    unit, depth = pieces[0].shape
+    rows = 8 * unit
+    cols = 2 * HD
+    per = width // cols
+    heads = cum_columns.shape[1]
+
+    def kernel(me_ref, d0, d1, wk_ref, wv_ref, k1, v1, k2, v2, cum_ref, k_out, v_out, s_out, held, keys, vals):
+        step = pl.program_id(0)
+
+        @pl.when(step == 0)
+        def _():
+            held[:unit] = d0[...]
+            held[unit:] = d1[...]
+
+        k_last = dot(held[...], wk_ref[...]).astype(BF)
+        v_last = dot(held[...], wv_ref[...]).astype(BF)
+        k_out[...] = k_last
+        v_out[...] = v_last
+        order = natural_units(me_ref[0])
+        total = cum_ref[rows - 1 : rows, :]
+        lane = lax.broadcasted_iota(jnp.int32, (unit, heads), 1)
+        for n, natural in enumerate(order):
+            cum = cum_ref[pl.ds(pl.multiple_of(natural * unit, unit), unit), :]
+            left = jnp.exp(total - cum)
+            if n < 4:
+                part = k1[n * unit : (n + 1) * unit]
+            elif n < 6:
+                part = k2[(n - 4) * unit : (n - 3) * unit]
+            else:
+                part = k_last[(n - 6) * unit : (n - 5) * unit]
+            for h in range(2):
+                scale = jnp.sum(jnp.where(lane == 2 * step + h, left, 0.0), axis=1, keepdims=True)
+                keys[n * unit : (n + 1) * unit, h * HD : (h + 1) * HD] = (
+                    part[:, h * HD : (h + 1) * HD].astype(F32) * scale
+                ).astype(BF)
+        vals[: 4 * unit] = v1[...]
+        vals[4 * unit : 6 * unit] = v2[...]
+        vals[6 * unit :] = v_last
+        both = dot_dims(keys[...], vals[...], 0, 0)
+        for h in range(2):
+            s_out[h * HD : (h + 1) * HD] = both[h * HD : (h + 1) * HD, h * HD : (h + 1) * HD].astype(BF)
+
+    def column(block_rows, offset=0):
+        return pl.BlockSpec((block_rows, cols), lambda step, me: (0, offset + step))
+
+    whole = lambda step, me: (0, 0)
+    return pl.pallas_call(
+        kernel,
+        grid_spec=pltpu.PrefetchScalarGridSpec(
+            num_scalar_prefetch=1,
+            grid=(per,),
+            in_specs=[pl.BlockSpec((unit, depth), whole)] * 2
+            + [column(depth, per), column(depth, 2 * per)]
+            + [column(4 * unit), column(4 * unit), column(2 * unit), column(2 * unit)]
+            + [pl.BlockSpec((rows, heads), whole)],
+            out_specs=[column(2 * unit), column(2 * unit), pl.BlockSpec((cols, HD), lambda step, me: (step, 0))],
+            scratch_shapes=[
+                pltpu.VMEM((2 * unit, depth), BF),
+                pltpu.VMEM((rows, cols), BF),
+                pltpu.VMEM((rows, cols), BF),
+            ],
+        ),
+        out_shape=[
+            jax.ShapeDtypeStruct((2 * unit, width), BF),
+            jax.ShapeDtypeStruct((2 * unit, width), BF),
+            jax.ShapeDtypeStruct((width, HD), BF),
+        ],
+        compiler_params=params(),
+        cost_estimate=cost(4 * 2 * unit * depth * width, 4 * depth * width),
+    )(me, *pieces, weights, weights, first[1], first[2], second[1], second[2], cum_columns)
+
+
+def local_attention(me, firsts, seconds, lasts, gain, cum_columns, cum_rows, width):
+    unit = lasts[0].shape[0] // 2
+    rows = 8 * unit
+    cols = 2 * HD
+    heads = cum_columns.shape[1]
+    blocks = rows // CH
+
+    def kernel(
+        me_ref, q1, k1, v1, g1, q2, k2, v2, g2, q3, k3, v3, g3, gain_ref, cc_ref, cr_ref,
+        a1, s1, z1, a2, s2, z2, a3, s3, z3, q, k, v, a, s,
+    ):
+        step = pl.program_id(0)
+        order = natural_units(me_ref[0])
+        places = [pl.ds(pl.multiple_of(n * unit, unit), unit) for n in order]
+        for to, parts in ((q, (q1, q2, q3)), (k, (k1, k2, k3)), (v, (v1, v2, v3))):
+            for n, place in enumerate(places):
+                part, at = (parts[0], n) if n < 4 else (parts[1], n - 4) if n < 6 else (parts[2], n - 6)
+                to[place, :] = part[at * unit : (at + 1) * unit, :]
+        lane = lax.broadcasted_iota(jnp.int32, (rows, heads), 1)
+        sub = lax.broadcasted_iota(jnp.int32, (heads, rows), 0)
+        causal = lax.broadcasted_iota(jnp.int32, (CH, CH), 0) >= lax.broadcasted_iota(jnp.int32, (CH, CH), 1)
+        for h in range(2):
+            here = slice(h * HD, (h + 1) * HD)
+            column = jnp.sum(jnp.where(lane == 2 * step + h, cc_ref[...], 0.0), axis=1, keepdims=True)
+            row = jnp.sum(jnp.where(sub == 2 * step + h, cr_ref[...], 0.0), axis=0, keepdims=True)
+            s[:, here] = (q[:, here].astype(F32) * jnp.exp(column)).astype(BF)
+            state = jnp.zeros((HD, HD), F32)
+            for b in range(blocks):
+                t = slice(b * CH, (b + 1) * CH)
+                qb, kb, vb = q[t, here], k[t, here], v[t, here]
+                ct, cs = column[t], row[:, t]
+                before = column[b * CH - 1 : b * CH] if b else jnp.zeros((1, 1), F32)
+                end = column[(b + 1) * CH - 1 : (b + 1) * CH]
+                weight = jnp.where(causal, jnp.exp(jnp.minimum(ct - cs, 0.0)), 0.0)
+                scores = (dot_dims(qb, kb, 1, 1) * weight).astype(BF)
+                within = dot(scores, vb)
+                if b:
+                    within = within + dot(qb, state.astype(BF)) * jnp.exp(ct - before)
+                a[t, here] = within
+                if b < blocks - 1:
+                    decayed = (kb.astype(F32) * jnp.exp(end - ct)).astype(BF)
+                    state = jnp.exp(end - before) * state + dot_dims(decayed, vb, 0, 0)
+        for n, place in enumerate(places):
+            to_a, to_s, at = (a1, s1, n) if n < 4 else (a2, s2, n - 4) if n < 6 else (a3, s3, n - 6)
+            to_a[at * unit : (at + 1) * unit, :] = a[place, :]
+            to_s[at * unit : (at + 1) * unit, :] = s[place, :]
+        for g, z in ((g1, z1), (g2, z2), (g3, z3)):
+            gate = g[...]
+            z[...] = gain_ref[...] * (gate / (1.0 + jnp.exp(-gate)))
+
+    def column(block_rows):
+        return pl.BlockSpec((block_rows, cols), lambda step, me: (0, step))
+
+    whole = lambda step, me: (0, 0)
+    counts = (4 * unit, 2 * unit, 2 * unit)
+    outs = pl.pallas_call(
+        kernel,
+        grid_spec=pltpu.PrefetchScalarGridSpec(
+            num_scalar_prefetch=1,
+            grid=(width // cols,),
+            in_specs=[column(n) for n in counts for _ in range(4)]
+            + [column(1), pl.BlockSpec((rows, heads), whole), pl.BlockSpec((heads, rows), whole)],
+            out_specs=[column(n) for n in counts for _ in range(3)],
+            scratch_shapes=[pltpu.VMEM((rows, cols), BF)] * 3
+            + [pltpu.VMEM((rows, cols), F32), pltpu.VMEM((rows, cols), BF)],
+        ),
+        out_shape=[jax.ShapeDtypeStruct((n, width), t) for n in counts for t in (F32, BF, F32)],
+        compiler_params=params(),
+        cost_estimate=cost(10 * rows * CH * width, 30 * rows * width),
+    )(me, *firsts, *seconds, *lasts, gain, cum_columns, cum_rows)
+    return outs[:3], outs[3:6], outs[6:]
+
+
+def weighted_sum(terms, factors):
+    rows = terms[0].shape[0]
+    heads = rows // HD
+
+    def kernel(*refs):
+        ins, f_ref, out_ref = refs[: len(terms)], refs[len(terms)], refs[-1]
+        for h in range(heads):
+            here = slice(h * HD, (h + 1) * HD)
+            total = None
+            for n, ref in enumerate(ins):
+                term = ref[here].astype(F32) * f_ref[n, h : h + 1, :]
+                total = term if total is None else total + term
+            out_ref[here] = total.astype(BF)
+
+    return pl.pallas_call(
+        kernel,
+        out_shape=jax.ShapeDtypeStruct((rows, HD), BF),
+        compiler_params=params(),
+        cost_estimate=cost(2 * len(terms) * rows * HD, 2 * (len(terms) + 1) * rows * HD),
+    )(*terms, factors)
+
+
+def entering_state(state, totals):
+    peers = lax.axis_size("seq")
+    rank = lax.axis_index("seq")
+    heads = totals.shape[1]
+    half = heads // 2
+    core, chip = rank % 2, rank // 2
+    chips = peers // 2
+    one = jnp.ones((half, HD), F32)
+    own_half = lambda value: lax.dynamic_slice_in_dim(value, core * half, half, 0)
+    total_of = lambda r: lax.dynamic_index_in_dim(totals, jnp.clip(r, 0, peers - 1), 0, keepdims=False)
+    later = jnp.exp(own_half(total_of(2 * chip + 1)))
+    factors = jnp.stack([jnp.where(core == 0, later, one), jnp.where(core == 0, one, later)])
+    weights = []
+    passed = jnp.zeros((half, HD), F32)
+    for d in range(1, chips):
+        weights.append(jnp.where(chip >= d, jnp.exp(passed), 0.0))
+        passed = passed + own_half(total_of(2 * (chip - d)) + total_of(2 * (chip - d) + 1))
+    weights = jnp.stack(weights)
+    first_decay = jnp.exp(total_of(2 * chip))
+    final = jnp.stack(
+        [
+            jnp.where(core == 0, 1.0, first_decay),
+            jnp.where(core == 0, 0.0, jnp.ones_like(first_decay)),
+        ]
+    )
+    factors, weights, final = lax.optimization_barrier((factors, weights, final))
+
+    other = swapped(state, "seq", 1)
+    size = half * HD
+    mine = lax.dynamic_slice_in_dim(state, core * size, size, 0)
+    theirs = lax.dynamic_slice_in_dim(other, core * size, size, 0)
+    chip_state = weighted_sum([mine, theirs], factors)
+    arrived = [passed_along(chip_state, "seq", 2 * d) for d in range(1, chips)]
+    entering = weighted_sum(arrived, weights)
+    entering_other = swapped(entering, "seq", 1)
+    low = jnp.where(core == 0, entering, entering_other)
+    high = jnp.where(core == 0, entering_other, entering)
+    return weighted_sum([jnp.concatenate([low, high]), other], final)
+
+
+def output_terms(parts, incoming, w_out):
+    unit = parts[0][0].shape[0] // parts[0][4]
+    width, model = w_out.shape
+    cols = model // 4
+    heads = width // HD
+
+    def kernel(a0, s0, z0, a1, s1, z1, in_ref, w_ref, out_a, out_b, gated):
+        step = pl.program_id(0)
+
+        @pl.when(step == 0)
+        def _():
+            for n, (a, s, z) in enumerate(((a0, s0, z0), (a1, s1, z1))):
+                for h in range(heads):
+                    here = slice(h * HD, (h + 1) * HD)
+                    attended = a[:, here] + dot(s[:, here], in_ref[here])
+                    mean = jnp.mean(attended * attended, axis=1, keepdims=True)
+                    gated[n * unit : (n + 1) * unit, here] = (
+                        attended * lax.rsqrt(mean + EPSILON) * z[:, here]
+                    ).astype(BF)
+
+        result = dot(gated[...], w_ref[...]).astype(BF)
+
+        @pl.when(step < 2)
+        def _():
+            out_a[...] = result
+
+        @pl.when(step >= 2)
+        def _():
+            out_b[...] = result
+
+    specs, args = [], []
+    for a, s, z, block, _ in parts:
+        specs += [pl.BlockSpec((unit, width), lambda step, block=block: (block, 0))] * 3
+        args += [a, s, z]
+    return pl.pallas_call(
+        kernel,
+        grid=(4,),
+        in_specs=specs
+        + [
+            pl.BlockSpec((width, HD), lambda step: (0, 0)),
+            pl.BlockSpec((width, cols), lambda step: (0, step)),
+        ],
+        out_specs=[
+            pl.BlockSpec((2 * unit, cols), lambda step: (0, jnp.minimum(step, 1))),
+            pl.BlockSpec((2 * unit, cols), lambda step: (0, jnp.maximum(step - 2, 0))),
+        ],
+        out_shape=[jax.ShapeDtypeStruct((2 * unit, model // 2), BF)] * 2,
+        scratch_shapes=[pltpu.VMEM((2 * unit, width), BF)],
+        compiler_params=params(),
+        cost_estimate=cost(4 * unit * width * model, 2 * width * model),
+    )(*args, incoming, w_out)
+
+
+def merged(own, arrived, quarter):
+    rows, cols = own.shape[0], own.shape[1] // 2
+
+    def kernel(a, b, out):
+        out[...] = (a[...].astype(F32) + b[...].astype(F32)).astype(BF)
+
+    spec = pl.BlockSpec((rows, cols), lambda step: (0, quarter))
+    return pl.pallas_call(
+        kernel,
+        grid=(1,),
+        in_specs=[spec, spec],
+        out_specs=pl.BlockSpec((rows, cols), lambda step: (0, 0)),
+        out_shape=jax.ShapeDtypeStruct((rows, cols), BF),
+        compiler_params=params(),
+        cost_estimate=cost(rows * cols, 6 * rows * cols),
+    )(own, arrived)
+
+
+def add_coarse(fine, columns, previous=None):
+    rows, model = fine.shape
+    cols = model // 4
+    pieces = 3
+    tall = rows // pieces
+    coarse = tall // SF
+    quarters = [quarter for quarter, _ in columns]
+    flat = [term for _, terms in columns for term in terms]
+
+    def kernel(*refs):
+        fine_ref, terms, out_ref = refs[0], refs[1 : 1 + len(flat)], refs[-1]
+        r = lax.broadcasted_iota(jnp.int32, (tall, coarse), 0) // SF
+        c = lax.broadcasted_iota(jnp.int32, (tall, coarse), 1)
+        spread = jnp.where(r == c, 1.0, 0.0).astype(BF)
+        for n in range(len(columns)):
+
+            @pl.when(pl.program_id(0) == n)
+            def _():
+                total = fine_ref[...].astype(F32)
+                for term in terms[3 * n : 3 * n + 3]:
+                    total += dot(spread, term[...])
+                out_ref[...] = total.astype(BF)
+
+    def where(step):
+        return jnp.where(step == 0, quarters[0], quarters[1])
+
+    fine_spec = pl.BlockSpec((tall, cols), lambda step, piece: (piece, where(step)))
+    specs = [fine_spec]
+    for n, (_, terms) in enumerate(columns):
+        for _, block in terms:
+            last = pieces - 1
+            if n == 0:
+                index = lambda step, piece, block=block: (jnp.where(step == 0, piece, last), block)
+            else:
+                index = lambda step, piece, block=block: (jnp.where(step == 0, 0, piece), block)
+            specs.append(pl.BlockSpec((coarse, cols), index))
+    args = [fine] + [term for term, _ in flat]
+    aliases = {}
+    if previous is not None:
+        specs.append(pl.BlockSpec(memory_space=pl.ANY))
+        args.append(previous)
+        aliases = {len(args) - 1: 0}
+    return pl.pallas_call(
+        kernel,
+        grid=(2, pieces),
+        in_specs=specs,
+        out_specs=fine_spec,
+        out_shape=jax.ShapeDtypeStruct((rows, model), BF),
+        input_output_aliases=aliases,
+        compiler_params=params(),
+        cost_estimate=cost(6 * rows * coarse * cols, 4 * rows * cols),
+    )(*args)
+
+
+def body_square(fine_rows, w_inputs, w_out, head_gain, decay_log):
+    model = fine_rows.shape[1]
+    fine_count = fine_rows.shape[0]
+    heads, rows_coarse = decay_log.shape
+    width = heads * HD
+    me = lax.axis_index("mp")
+    place = jnp.reshape(me, (1,)).astype(jnp.int32)
+
+    before = passed_along(fine_rows[fine_count - 16 :], ("seq", "mp"), 1)
+    weights = w_inputs.reshape(model, 4 * width)
+    cum_rows = jnp.cumsum(decay_log, axis=1)
+    cum_columns = cum_rows.T
+    totals = lax.all_gather(
+        jnp.broadcast_to(cum_rows[:, -1:], (heads, HD))[None], "seq", axis=0, tiled=True
+    )
+
+    p1 = pool_half(fine_rows, fine_rows, 1, fine_count // 32 - 1)
+    p0 = pool_half(fine_rows, before, 0, 0)
+    y1 = swapped(p1, "mp", 2)
+    x0 = swapped(p0, "mp", 1)
+    y0 = swapped(p0, "mp", 2)
+    x1 = swapped(p1, "mp", 1)
+    d0 = swapped(x0, "mp", 2)
+    d1 = swapped(y1, "mp", 1)
+
+    everything = [0, width, 2 * width, 3 * width]
+    first = project([p0, p1, x0, y1], weights, everything, width)
+    second = project([x1, y0], weights, everything, width)
+    k_last, v_last, state = last_keys_and_state(place, [d0, d1], weights, first, second, cum_columns, width)
+    q_last, g_last = project([d0, d1], weights, [0, 3 * width], width)
+    a1, a2, a3 = local_attention(
+        place, first, second, [q_last, k_last, v_last, g_last], head_gain[None], cum_columns, cum_rows, width
+    )
+    incoming = entering_state(state, totals)
+
+    n = 4
+    far_a, far_b = output_terms([(*a3, 0, 2), (*a3, 1, 2)], incoming, w_out)
+    got_a = swapped(far_a, "mp", 1)
+    got_b = swapped(far_b, "mp", 2)
+    x_a, x_b = output_terms([(*a1, 2, n), (*a2, 0, 2)], incoming, w_out)
+    from_x_a = swapped(x_a, "mp", 1)
+    y_a, y_b = output_terms([(*a2, 1, 2), (*a1, 3, n)], incoming, w_out)
+    from_y_b = swapped(y_b, "mp", 2)
+    own_a, own_b = output_terms([(*a1, 0, n), (*a1, 1, n)], incoming, w_out)
+    from_x_b = [swapped(merged(x_b, got_b, q), "mp", 1) for q in range(2)]
+    from_y_a = [swapped(merged(y_a, got_a, q), "mp", 2) for q in range(2)]
+    out = None
+    for q in range(2):
+        out = add_coarse(
+            fine_rows,
+            [
+                (q, [(own_a, q), (from_x_a, q), (from_y_a[q], 0)]),
+                (2 + q, [(own_b, q), (from_y_b, q), (from_x_b[q], 0)]),
+            ],
+            out,
+        )
+    return out
 
 
 def body(fine_rows, w_inputs, w_out, head_gain, decay_log):
@@ -120,8 +618,9 @@
 
 
 def solution(mesh):
+    square = mesh.shape["mp"] == 4 and mesh.shape["seq"] % 2 == 0 and mesh.shape["seq"] > 2
     return jax.shard_map(
-        body,
+        body_square if square else body,
         mesh=mesh,
         in_specs=(
             P(("seq", "mp"), None),

time: 328 us -> 232 us (0.71)
  Pallas kernels: 0 us -> 125 us
  waiting for transfers between devices: 120 us -> 26.7 us
  matrix products: 53.8 us -> 0 us
  local copies, waits for them, and re-layouts: 77.8 us -> 32.1 us
  other arithmetic: 39.5 us -> 2.24 us
  starting transfers between devices: 5.11 us -> 26.2 us
  between operations: 14 us -> 1.12 us
    pallas_call x0 -> x20, Pallas kernels: none -> 125 us  [the longest x3 56.4 us: project(): pl.pallas_call(kernel, grid=(ranges * per,), in_specs=[pl.BlockSpec((piec...]
    reduce_scatter x1 -> x0, waiting for transfers between devices: 69.8 us -> none  [body(): lax.psum_scatter(jnp.dot(gated_rows, w_out, preferred_element_type=jnp.fl...]
    dot_general x5 -> x0, matrix products: 53.8 us -> none  [the longest x1 33.5 us: body(): jnp.dot(lax.all_gather(pooled, 'mp', axis=0, tiled=True), weights_flat, p...]
    all_gather x2 -> x0, waiting for transfers between devices: 48.4 us -> none  [the longest x1 46.3 us: body(): lax.all_gather(pooled, 'mp', axis=0, tiled=True)]
    convert_element_type x4 -> x0, other arithmetic: 23.4 us -> none  [the longest x1 11.5 us: body(): return (fine_rows.astype(jnp.float32) + upsampled).astype(jnp.bfloat16)]
    ppermute x0 -> x16, waiting for transfers between devices: none -> 22 us  [swapped(): return lax.ppermute(value, axis, [(i, i ^ bit) for i in range(peers)])]
    reshape x2 -> x0, local copies, waits for them, and re-layouts: 16.5 us -> none  [the longest x1 14.7 us: body(): upsampled = jnp.repeat(coarse, SF, axis=0)]
    convert_element_type x1 -> x0, local copies, waits for them, and re-layouts: 14.4 us -> none  [body(): jnp.concatenate([before, fine_rows[:fine_count - (SF - 1)]], axis=0)]
  transfers between devices with their start and end apart: 4 -> 20, of which waited for: 4 -> 7; matrix products, arithmetic and copies ran while one was open for 11% -> 12% of each run, Pallas kernels for 0% -> 45%
where the time goes in v1:
time: 232 us; the launch traced here: 229 us
  Pallas kernels  125 us (54%)
  local copies, waits for them, and re-layouts  32.1 us (14%)
  waiting for transfers between devices  26.7 us (12%)
  starting transfers between devices  26.2 us (11%)
  blocking collectives  15.5 us (7%)
    pallas_call x3, Pallas kernels, project(): pl.pallas_call(kernel, grid=(ranges * per,), in_specs=[pl.BlockSpec((piec...  56.4 us
    unnamed x52, local copies, waits for them, and re-layouts  29.2 us
    pallas_call x4, Pallas kernels, output_terms(): pl.pallas_call(kernel, grid=(4,), in_specs=specs + [pl.BlockSpec((width,...  23.6 us
    ppermute x16, waiting for transfers between devices, swapped(): return lax.ppermute(value, axis, [(i, i ^ bit) for i in range(peers)])  22 us
    unnamed x1, blocking collectives  15.5 us
    pallas_call x2, Pallas kernels, add_coarse(): pl.pallas_call(kernel, grid=(2, pieces), in_specs=specs, out_specs=fine_s...  13.5 us
    ppermute x16, starting transfers between devices, swapped(): return lax.ppermute(value, axis, [(i, i ^ bit) for i in range(peers)])  13.3 us
    ppermute x4, starting transfers between devices, passed_along(): return lax.ppermute(value, axis, pairs)  12.9 us
  transfers between devices with their start and end apart: 20, of which 7 were waited for; matrix products, arithmetic and copies ran while one was open for 12% of the time, Pallas kernels for 45%

profile of v1, /device:TPU:0, one launch (start us, length us, event | category | flops | bytes accessed | tf_op | source)
XLA Modules:
  0.0 228.8 jit_solution(12860173985414923094)
XLA Ops:
  0.0 0.9 slice.12
  0.9 4.8 %collective-permute-start = (bf16[16,4096]{1,0:T(8,128)(2,1)S(1)}, bf16[16,4096]{1,0:T(8,128)(2,1)S(1)}, u32[]{:S(2)}, u32[]{:S(2)}) collective-permute-start(bf16[16,4096]{1,0:T(8,128)(2,1)S(1)} %slice.12), channel_id=1, source_target_pairs={{0,1},{1,2},{2,3},{3,4},{4,5},{5,6},{6,7},{7,8},{8,9},{9,10},{10,1... | collective-permute-start | bytes 393224 | tf_op jit(solution)/shard_map/ppermute | solution.py:24
  5.8 4.4 %shard_map.56.refs_1_ = bf16[96,4096]{1,0:T(8,128)(2,1)} custom-call(bf16[768,4096]{1,0:T(8,128)(2,1)} %refs_0_.3, bf16[768,4096]{1,0:T(8,128)(2,1)} %refs_0_.3), custom_call_target="tpu_custom_call" | custom-call | flops 301989888 | bytes 3145728 | tf_op jit(solution)/shard_map/pallas_call | solution.py:62
  10.2 1.5 collective-permute-start.2
  11.7 22.8 %copy.15 = bf16[512,8,4,1024]{3,1,2,0:T(8,128)(2,1)} copy(bf16[512,8,4,1024]{3,2,1,0:T(4,128)(2,1)} %bitcast.30) | data formatting | bytes 67108864
  34.5 1.7 reduce-window.6
  36.6 4.4 %shard_map.55.refs_0_ = bf16[96,4096]{1,0:T(8,128)(2,1)} custom-call(bf16[16,4096]{1,0:T(8,128)(2,1)S(1)} %collective-permute-done.tail_ref, bf16[768,4096]{1,0:T(8,128)(2,1)} %refs_0_.3), custom_call_target="tpu_custom_call" | custom-call | flops 301989888 | bytes 3145728 | tf_op jit(solution)/shard_map/pallas_call | solution.py:62
  41.0 2.0 collective-permute-start.1
  43.3 0.6 dynamic-slice.12
  45.0 15.5 %all-reduce.1 = f32[64]{0:T(128)S(1)} all-reduce(f32[64]{0:T(128)S(1)} %dynamic-update-slice), channel_id=3, replica_groups=mesh['seq'=8,'mp'=4] {'seq'}, use_global_device_ids=true, to_apply=%add.1 | all-reduce | flops 64 | bytes 512
  60.9 0.5 collective-permute-start.4
  61.4 1.5 collective-permute-start.6
  63.2 25.2 %shard_map.57 = (bf16[384,1024]{1,0:T(8,128)(2,1)S(1)}, bf16[384,1024]{1,0:T(8,128)(2,1)S(1)}, bf16[384,1024]{1,0:T(8,128)(2,1)S(1)}, f32[384,1024]{1,0:T(8,128)}) custom-call(bf16[96,4096]{1,0:T(8,128)(2,1)} %shard_map.55.refs_0_, bf16[96,4096]{1,0:T(8,128)(2,1)} %shard_map.56.refs_1_, bf16[96,4096]{1,0:T(8,128)(2,1)} %collective-permute-done.1.refs_2_, ...), custom_call_target="tpu_custom_call" | custom-call | flops 12884901888 | bytes 33554432 | tf_op jit(solution)/shard_map/pallas_call | solution.py:107
  88.4 0.9 copy-done.10
  89.3 20.9 %shard_map.58 = (bf16[192,1024]{1,0:T(8,128)(2,1)S(1)}, bf16[192,1024]{1,0:T(8,128)(2,1)S(1)}, bf16[192,1024]{1,0:T(8,128)(2,1)S(1)}, f32[192,1024]{1,0:T(8,128)S(1)}) custom-call(bf16[96,4096]{1,0:T(8,128)(2,1)} %collective-permute-done.3.refs_0_, bf16[96,4096]{1,0:T(8,128)(2,1)S(1)} %collective-permute-done.4.refs_1_, bf16[4096,4096]{1,0:T(8,128)(2,1)} %bitcast.26), custom_call_target="tpu_custom_call" | custom-call | flops 6442450944 | bytes 33554432 | tf_op jit(solution)/shard_map/pallas_call | solution.py:107
  110.3 10.0 %shard_map.60 = (bf16[192,1024]{1,0:T(8,128)(2,1)S(1)}, bf16[192,1024]{1,0:T(8,128)(2,1)S(1)}, bf16[1024,128]{1,0:T(8,128)(2,1)}) custom-call(s32[1]{0:T(128)} %bitcast.me_ref, bf16[96,4096]{1,0:T(8,128)(2,1)S(1)} %collective-permute-done.5.refs_0_.d0, bf16[96,4096]{1,0:T(8,128)(2,1)S(1)} %collective-permute-done.6.refs_1_.d1, bf16[4096,4096]{1,0:T(8,128)(2,1)} %bitcast.27, ...), custom_call_target="tpu_custom_call" | custom-call | flops 3221225472 | bytes 16777216 | tf_op jit(solution)/shard_map/pallas_call | solution.py:174
  120.3 0.7 copy-done.15
  121.1 0.8 copy-done.17
  122.1 0.9 constant_dynamic-slice_fusion.8.refs_0_
  123.1 0.5 collective-permute-done.7.refs_1_
  123.6 4.1 %collective-permute-start.10 = (bf16[512,128]{1,0:T(8,128)(2,1)S(1)}, bf16[512,128]{1,0:T(8,128)(2,1)S(1)}, u32[]{:S(2)}, u32[]{:S(2)}) collective-permute-start(bf16[512,128]{1,0:T(8,128)(2,1)S(1)} %shard_map.62), channel_id=1, source_target_pairs={{0,24},{4,28},{1,25},{5,29},{2,26},{6,30},{3,27},{7,31}} | collective-permute-start | bytes 393224 | tf_op jit(solution)/shard_map/ppermute | solution.py:24
  127.7 1.3 collective-permute-start.8
  129.0 2.6 %collective-permute-start.9 = (bf16[512,128]{1,0:T(8,128)(2,1)S(1)}, bf16[512,128]{1,0:T(8,128)(2,1)S(1)}, u32[]{:S(2)}, u32[]{:S(2)}) collective-permute-start(bf16[512,128]{1,0:T(8,128)(2,1)S(1)} %shard_map.62), channel_id=1, source_target_pairs={{0,16},{4,20},{8,24},{12,28},{1,17},{5,21},{9,25},{13,29},{2,18},{... | collective-permute-start | bytes 393224 | tf_op jit(solution)/shard_map/ppermute | solution.py:24
  131.7 2.7 %collective-permute-done.8.refs_0_ = bf16[512,128]{1,0:T(8,128)(2,1)S(1)} collective-permute-done((bf16[512,128]{1,0:T(8,128)(2,1)S(1)}, bf16[512,128]{1,0:T(8,128)(2,1)S(1)}, u32[]{:S(2)}, u32[]{:S(2)}) %collective-permute-start.8) | collective-permute-done | bytes 131104 | tf_op jit(solution)/shard_map/ppermute | solution.py:24
  134.4 2.1 collective-permute-done.9.refs_1_
  136.6 10.3 %shard_map.59 = (bf16[192,1024]{1,0:T(8,128)(2,1)S(1)}, f32[192,1024]{1,0:T(8,128)S(1)}) custom-call(bf16[96,4096]{1,0:T(8,128)(2,1)S(1)} %collective-permute-done.5.refs_0_.d0, bf16[96,4096]{1,0:T(8,128)(2,1)S(1)} %collective-permute-done.6.refs_1_.d1, bf16[4096,4096]{1,0:T(8,128)(2,1)} %bitcast.29), custom_call_target="tpu_custom_call" | custom-call | flops 3221225472 | bytes 16777216 | tf_op jit(solution)/shard_map/pallas_call | solution.py:107
  147.0 0.9 copy-done.12
  147.9 12.1 %shard_map.61 = (f32[384,1024]{1,0:T(8,128)}, bf16[384,1024]{1,0:T(8,128)(2,1)S(1)}, f32[384,1024]{1,0:T(8,128)}, f32[192,1024]{1,0:T(8,128)S(1)}, bf16[192,1024...) custom-call(s32[1]{0:T(128)} %bitcast.me_ref, ...), custom_call_target="tpu_custom_call" | custom-call | flops 1006632960 | bytes 23592960 | tf_op jit(solution)/shard_map/pallas_call | solution.py:255
  160.1 1.1 copy-done.4
  161.3 1.1 copy-done.5
  162.4 6.0 %shard_map.68 = (bf16[192,2048]{1,0:T(8,128)(2,1)S(1)}, bf16[192,2048]{1,0:T(8,128)(2,1)S(1)}) custom-call(f32[192,1024]{1,0:T(8,128)S(1)} %copy-done.4, bf16[192,1024]{1,0:T(8,128)(2,1)S(1)} %get-tuple-element.64.s0.s1, f32[192,1024]{1,0:T(8,128)S(1)} %copy-done.5, f32[192,1024]{1,0:T(8,128)S(1)} %copy-done.4, ...), custom_call_target="tpu_custom_call" | custom-call | flops 1610612736 | bytes 8388608 | tf_op jit(solution)/shard_map/pallas_call | solution.py:369
  168.4 0.4 collective-permute-start.16
  168.8 1.7 collective-permute-start.13
  170.5 5.9 %shard_map.67 = (bf16[192,2048]{1,0:T(8,128)(2,1)S(1)}, bf16[192,2048]{1,0:T(8,128)(2,1)S(1)}) custom-call(f32[192,1024]{1,0:T(8,128)S(1)} %get-tuple-element.58.a1.a0, bf16[192,1024]{1,0:T(8,128)(2,1)S(1)} %get-tuple-element.59.s1.s0, f32[192,1024]{1,0:T(8,128)S(1)} %get-tuple-element.60.z1.z0, f32[384,1024]{1,0:T(8,128)S(1)} %copy-done, ...), custom_call_target="tpu_custom_call" | custom-call | flops 1610612736 | bytes 8388608 | tf_op jit(solution)/shard_map/pallas_call | solution.py:369
  176.4 0.7 collective-permute-start.15
  177.1 5.9 %shard_map.66 = (bf16[192,2048]{1,0:T(8,128)(2,1)S(1)}, bf16[192,2048]{1,0:T(8,128)(2,1)S(1)}) custom-call(f32[384,1024]{1,0:T(8,128)S(1)} %copy-done, bf16[384,1024]{1,0:T(8,128)(2,1)S(1)} %get-tuple-element.51.s0.s1, f32[384,1024]{1,0:T(8,128)} %get-tuple-element.52.z0.z1, f32[192,1024]{1,0:T(8,128)S(1)} %get-tuple-element.58.a1.a0, ...), custom_call_target="tpu_custom_call" | custom-call | flops 1610612736 | bytes 8388608 | tf_op jit(solution)/shard_map/pallas_call | solution.py:369
  183.0 1.4 collective-permute-start.12
  184.5 4.3 %collective-permute-done.16.b = bf16[192,2048]{1,0:T(8,128)(2,1)S(1)} collective-permute-done((bf16[192,2048]{1,0:T(8,128)(2,1)S(1)}, bf16[192,2048]{1,0:T(8,128)(2,1)S(1)}, u32[]{:S(2)}, u32[]{:S(2)}) %collective-permute-start.16) | collective-permute-done | bytes 786464 | tf_op jit(solution)/shard_map/ppermute | solution.py:29
  188.9 0.7 collective-permute-start.19
  189.7 1.5 collective-permute-start.18
  191.3 0.6 collective-permute-start.17
  192.0 13.7 %collective-permute-done.15.refs_5_ = bf16[192,2048]{1,0:T(8,128)(2,1)S(1)} collective-permute-done((bf16[192,2048]{1,0:T(8,128)(2,1)S(1)}, bf16[192,2048]{1,0:T(8,128)(2,1)S(1)}, u32[]{:S(2)}, u32[]{:S(2)}) %collective-permute-start.15) | collective-permute-done | bytes 786464 | tf_op jit(solution)/shard_map/ppermute | solution.py:29
  205.7 0.3 collective-permute-start.14
  206.0 5.9 %shard_map.65 = (bf16[192,2048]{1,0:T(8,128)(2,1)S(1)}, bf16[192,2048]{1,0:T(8,128)(2,1)S(1)}) custom-call(f32[384,1024]{1,0:T(8,128)S(1)} %copy-done, bf16[384,1024]{1,0:T(8,128)(2,1)S(1)} %get-tuple-element.51.s0.s1, f32[384,1024]{1,0:T(8,128)S(1)} %copy-done.1, f32[384,1024]{1,0:T(8,128)S(1)} %copy-done, bf16[384,1024]{1,0:T(8,128)(2,1)S(1)} %get-tuple-element.51.s0.s1, ...), custom_call_target="tpu_custom_call" | custom-call | flops 1610612736 | bytes 8388608 | tf_op jit(solution)/shard_map/pallas_call | solution.py:369
  211.9 2.6 %collective-permute-done.19.refs_6_ = bf16[192,1024]{1,0:T(8,128)(2,1)S(1)} collective-permute-done((bf16[192,1024]{1,0:T(8,128)(2,1)S(1)}, bf16[192,1024]{1,0:T(8,128)(2,1)S(1)}, u32[]{:S(2)}, u32[]{:S(2)}) %collective-permute-start.19) | collective-permute-done | bytes 393248 | tf_op jit(solution)/shard_map/ppermute | solution.py:29
  214.5 6.7 %shard_map.73.refs_7_ = bf16[768,4096]{1,0:T(8,128)(2,1)} custom-call(bf16[768,4096]{1,0:T(8,128)(2,1)} %refs_0_.3, bf16[192,2048]{1,0:T(8,128)(2,1)S(1)} %get-tuple-element.57.refs_1_, bf16[192,2048]{1,0:T(8,128)(2,1)S(1)} %collective-permute-done.12.refs_2_, bf16[192,1024]{1,0:T(8,128)(2,1)S(1)} %collective-permute-done.18.refs_3_, ...), custom_call_target="tpu_custom_call" | custom-call | flops 301989888 | bytes 3145728 | tf_op jit(solution)/shard_map/pallas_call | solution.py:448
  221.2 0.8 collective-permute-done.17.refs_6_
  222.0 6.7 %shard_map.74 = bf16[768,4096]{1,0:T(8,128)(2,1)} custom-call(bf16[768,4096]{1,0:T(8,128)(2,1)} %refs_0_.3, bf16[192,2048]{1,0:T(8,128)(2,1)S(1)} %get-tuple-element.57.refs_1_, bf16[192,2048]{1,0:T(8,128)(2,1)S(1)} %collective-permute-done.12.refs_2_, bf16[192,1024]{1,0:T(8,128)(2,1)S(1)} %collective-permute-done.14.refs_3_, ...), custom_call_target="tpu_custom_call", output_to_operand_aliasing={{}: (7, {})} | custom-call | flops 301989888 | bytes 3145728 | tf_op jit(solution)/shard_map/pallas_call | solution.py:448
  (91 shorter events, 3.0 us)
Async XLA Ops:
  0.9 35.7 %collective-permute-start = (bf16[16,4096]{1,0:T(8,128)(2,1)S(1)}, bf16[16,4096]{1,0:T(8,128)(2,1)S(1)}, u32[]{:S(2)}, u32[]{:S(2)}) collective-permute-start(bf16[16,4096]{1,0:T(8,128)(2,1)S(1)} %slice.12), channel_id=1, source_target_pairs={{0,1},{1,2},{2,3},{3,4},{4,5},{5,6},{6,7},{7,8},{8,9},{9,10},{10,1... | collective-permute-start | bytes 393224 | tf_op jit(solution)/shard_map/ppermute | solution.py:24
  10.2 51.2 %collective-permute-start.2 = (bf16[96,4096]{1,0:T(8,128)(2,1)}, bf16[96,4096]{1,0:T(8,128)(2,1)}, u32[]{:S(2)}, u32[]{:S(2)}) collective-permute-start(bf16[96,4096]{1,0:T(8,128)(2,1)} %shard_map.56.refs_1_), channel_id=1, source_target_pairs={{0,2},{1,3},{2,0},{3,1},{4,6},{5,7},{6,4},{7,5},{8,10},{9,11},{10,... | collective-permute-start | bytes 2359304 | tf_op jit(solution)/shard_map/ppermute | solution.py:29
  11.7 77.6 %collective-permute-start.3 = (bf16[96,4096]{1,0:T(8,128)(2,1)}, bf16[96,4096]{1,0:T(8,128)(2,1)}, u32[]{:S(2)}, u32[]{:S(2)}) collective-permute-start(bf16[96,4096]{1,0:T(8,128)(2,1)} %shard_map.56.refs_1_), channel_id=1, source_target_pairs={{0,1},{1,0},{2,3},{3,2},{4,5},{5,4},{6,7},{7,6},{8,9},{9,8},{10,11... | collective-permute-start | bytes 2359304 | tf_op jit(solution)/shard_map/ppermute | solution.py:29
  11.7 22.8 %copy-start.22 = (f32[8,768]{1,0:T(8,128)S(1)}, f32[8,768]{1,0:T(8,128)}, u32[]{:S(2)}) copy-start(f32[8,768]{1,0:T(8,128)} %param.9) | copy-start | bytes 73732
  34.5 8.9 %copy-start.23 = (u32[32]{0:T(128)S(1)}, u32[32]{0:T(128)}, u32[]{:S(2)}) copy-start(u32[32]{0:T(128)} %constant.101) | copy-start | bytes 388
  41.0 21.9 %collective-permute-start.1 = (bf16[96,4096]{1,0:T(8,128)(2,1)}, bf16[96,4096]{1,0:T(8,128)(2,1)}, u32[]{:S(2)}, u32[]{:S(2)}) collective-permute-start(bf16[96,4096]{1,0:T(8,128)(2,1)} %shard_map.55.refs_0_), channel_id=1, source_target_pairs={{0,1},{1,0},{2,3},{3,2},{4,5},{5,4},{6,7},{7,6},{8,9},{9,8},{10,11... | collective-permute-start | bytes 2359304 | tf_op jit(solution)/shard_map/ppermute | solution.py:29
  43.1 20.1 %copy-start.19 = (f32[8,768]{1,0:T(8,128)}, f32[8,768]{1,0:T(8,128)S(1)}, u32[]{:S(2)}) copy-start(f32[8,768]{1,0:T(8,128)S(1)} %get-tuple-element.73.cr_ref) | copy-start | bytes 73732
  60.9 28.4 %collective-permute-start.4 = (bf16[96,4096]{1,0:T(8,128)(2,1)}, bf16[96,4096]{1,0:T(8,128)(2,1)S(1)}, u32[]{:S(2)}, u32[]{:S(2)}) collective-permute-start(bf16[96,4096]{1,0:T(8,128)(2,1)} %shard_map.55.refs_0_), channel_id=1, source_target_pairs={{0,2},{1,3},{2,0},{3,1},{4,6},{5,7},{6,4},{7,5},{8,10},{9,11},{10,... | collective-permute-start | bytes 2359304 | tf_op jit(solution)/shard_map/ppermute | solution.py:29
  61.4 48.9 %collective-permute-start.6 = (bf16[96,4096]{1,0:T(8,128)(2,1)}, bf16[96,4096]{1,0:T(8,128)(2,1)S(1)}, u32[]{:S(2)}, u32[]{:S(2)}) collective-permute-start(bf16[96,4096]{1,0:T(8,128)(2,1)} %collective-permute-done.2.refs_3_), channel_id=1, source_target_pairs={{0,1},{1,0},{2,3},{3,2},{4,5},{5,4},{6,7},{7,6},{8,9},{9,8},{10,11... | collective-permute-start | bytes 2359304 | tf_op jit(solution)/shard_map/ppermute | solution.py:29
  62.9 47.4 %collective-permute-start.5 = (bf16[96,4096]{1,0:T(8,128)(2,1)}, bf16[96,4096]{1,0:T(8,128)(2,1)S(1)}, u32[]{:S(2)}, u32[]{:S(2)}) collective-permute-start(bf16[96,4096]{1,0:T(8,128)(2,1)} %collective-permute-done.1.refs_2_), channel_id=1, source_target_pairs={{0,2},{1,3},{2,0},{3,1},{4,6},{5,7},{6,4},{7,5},{8,10},{9,11},{10,... | collective-permute-start | bytes 2359304 | tf_op jit(solution)/shard_map/ppermute | solution.py:29
  88.4 0.9 copy-start.10
  89.3 21.0 %copy-start.2 = (bf16[384,1024]{1,0:T(8,128)(2,1)}, bf16[384,1024]{1,0:T(8,128)(2,1)S(1)}, u32[]{:S(2)}) copy-start(bf16[384,1024]{1,0:T(8,128)(2,1)S(1)} %get-tuple-element.39.k1) | copy-start | bytes 2359300
  89.3 21.0 %copy-start.3 = (bf16[384,1024]{1,0:T(8,128)(2,1)}, bf16[384,1024]{1,0:T(8,128)(2,1)S(1)}, u32[]{:S(2)}) copy-start(bf16[384,1024]{1,0:T(8,128)(2,1)S(1)} %get-tuple-element.40.v1) | copy-start | bytes 2359300
  110.2 10.1 %copy-start.6 = (bf16[192,1024]{1,0:T(8,128)(2,1)}, bf16[192,1024]{1,0:T(8,128)(2,1)S(1)}, u32[]{:S(2)}) copy-start(bf16[192,1024]{1,0:T(8,128)(2,1)S(1)} %get-tuple-element.43.k2) | copy-start | bytes 1179652
  110.2 10.1 %copy-start.8 = (bf16[192,1024]{1,0:T(8,128)(2,1)}, bf16[192,1024]{1,0:T(8,128)(2,1)S(1)}, u32[]{:S(2)}) copy-start(bf16[192,1024]{1,0:T(8,128)(2,1)S(1)} %get-tuple-element.44.v2) | copy-start | bytes 1179652
  110.2 10.1 %copy-start.11 = (f32[192,1024]{1,0:T(8,128)}, f32[192,1024]{1,0:T(8,128)S(1)}, u32[]{:S(2)}) copy-start(f32[192,1024]{1,0:T(8,128)S(1)} %get-tuple-element.45.g2) | copy-start | bytes 2359300
  110.2 10.1 %copy-start.13 = (bf16[192,1024]{1,0:T(8,128)(2,1)}, bf16[192,1024]{1,0:T(8,128)(2,1)S(1)}, u32[]{:S(2)}) copy-start(bf16[192,1024]{1,0:T(8,128)(2,1)S(1)} %get-tuple-element.42.q2) | copy-start | bytes 1179652
  120.3 0.8 copy-start.15
  121.1 0.8 copy-start.17
  121.8 1.7 collective-permute-start.7
  123.6 8.0 %collective-permute-start.10 = (bf16[512,128]{1,0:T(8,128)(2,1)S(1)}, bf16[512,128]{1,0:T(8,128)(2,1)S(1)}, u32[]{:S(2)}, u32[]{:S(2)}) collective-permute-start(bf16[512,128]{1,0:T(8,128)(2,1)S(1)} %shard_map.62), channel_id=1, source_target_pairs={{0,24},{4,28},{1,25},{5,29},{2,26},{6,30},{3,27},{7,31}} | collective-permute-start | bytes 393224 | tf_op jit(solution)/shard_map/ppermute | solution.py:24
  127.7 6.6 %collective-permute-start.8 = (bf16[512,128]{1,0:T(8,128)(2,1)S(1)}, bf16[512,128]{1,0:T(8,128)(2,1)S(1)}, u32[]{:S(2)}, u32[]{:S(2)}) collective-permute-start(bf16[512,128]{1,0:T(8,128)(2,1)S(1)} %shard_map.62), channel_id=1, source_target_pairs={{0,8},{4,12},{8,16},{12,20},{16,24},{20,28},{1,9},{5,13},{9,17},{1... | collective-permute-start | bytes 393224 | tf_op jit(solution)/shard_map/ppermute | solution.py:24
  129.0 7.4 %collective-permute-start.9 = (bf16[512,128]{1,0:T(8,128)(2,1)S(1)}, bf16[512,128]{1,0:T(8,128)(2,1)S(1)}, u32[]{:S(2)}, u32[]{:S(2)}) collective-permute-start(bf16[512,128]{1,0:T(8,128)(2,1)S(1)} %shard_map.62), channel_id=1, source_target_pairs={{0,16},{4,20},{8,24},{12,28},{1,17},{5,21},{9,25},{13,29},{2,18},{... | collective-permute-start | bytes 393224 | tf_op jit(solution)/shard_map/ppermute | solution.py:24
  136.5 11.3 %copy-start.7 = (bf16[192,1024]{1,0:T(8,128)(2,1)S(1)}, bf16[192,1024]{1,0:T(8,128)(2,1)}, u32[]{:S(2)}) copy-start(bf16[192,1024]{1,0:T(8,128)(2,1)} %copy-done.6) | copy-start | bytes 1179652
  136.5 11.3 %copy-start.9 = (bf16[192,1024]{1,0:T(8,128)(2,1)S(1)}, bf16[192,1024]{1,0:T(8,128)(2,1)}, u32[]{:S(2)}) copy-start(bf16[192,1024]{1,0:T(8,128)(2,1)} %copy-done.8) | copy-start | bytes 1179652
  136.5 11.3 %copy-start.14 = (bf16[192,1024]{1,0:T(8,128)(2,1)S(1)}, bf16[192,1024]{1,0:T(8,128)(2,1)}, u32[]{:S(2)}) copy-start(bf16[192,1024]{1,0:T(8,128)(2,1)} %copy-done.13) | copy-start | bytes 1179652
  136.5 11.3 %copy-start.16 = (bf16[192,1024]{1,0:T(8,128)(2,1)S(1)}, bf16[192,1024]{1,0:T(8,128)(2,1)}, u32[]{:S(2)}) copy-start(bf16[192,1024]{1,0:T(8,128)(2,1)} %copy-done.15) | copy-start | bytes 1179652
  136.5 11.3 %copy-start.18 = (bf16[192,1024]{1,0:T(8,128)(2,1)S(1)}, bf16[192,1024]{1,0:T(8,128)(2,1)}, u32[]{:S(2)}) copy-start(bf16[192,1024]{1,0:T(8,128)(2,1)} %copy-done.17) | copy-start | bytes 1179652
  136.5 11.3 %copy-start.20 = (f32[8,768]{1,0:T(8,128)S(1)}, f32[8,768]{1,0:T(8,128)}, u32[]{:S(2)}) copy-start(f32[8,768]{1,0:T(8,128)} %copy-done.19) | copy-start | bytes 73732
  136.6 11.3 %copy-start.21 = (f32[1024]{0:T(1024)S(1)}, f32[1024]{0:T(1024)}, u32[]{:S(2)}) copy-start(f32[1024]{0:T(1024)} %param.8) | copy-start | bytes 12292
  136.6 23.4 %collective-permute-start.11 = (bf16[512,128]{1,0:T(8,128)(2,1)S(1)}, bf16[512,128]{1,0:T(8,128)(2,1)S(1)}, u32[]{:S(2)}, u32[]{:S(2)}) collective-permute-start(bf16[512,128]{1,0:T(8,128)(2,1)S(1)} %shard_map.63), channel_id=1, source_target_pairs={{0,4},{4,0},{8,12},{12,8},{16,20},{20,16},{24,28},{28,24},{1,5},{5... | collective-permute-start | bytes 393224 | tf_op jit(solution)/shard_map/ppermute | solution.py:29
  146.9 0.9 copy-start.12
  160.1 1.1 copy-start.4
  161.2 1.1 copy-start.5
  162.4 8.1 %copy-start = (f32[384,1024]{1,0:T(8,128)S(1)}, f32[384,1024]{1,0:T(8,128)}, u32[]{:S(2)}) copy-start(f32[384,1024]{1,0:T(8,128)} %get-tuple-element.50.a0.a1) | copy-start | bytes 4718596
  168.4 20.4 %collective-permute-start.16 = (bf16[192,2048]{1,0:T(8,128)(2,1)S(1)}, bf16[192,2048]{1,0:T(8,128)(2,1)S(1)}, u32[]{:S(2)}, u32[]{:S(2)}) collective-permute-start(bf16[192,2048]{1,0:T(8,128)(2,1)S(1)} %get-tuple-element.70), channel_id=1, source_target_pairs={{0,2},{1,3},{2,0},{3,1},{4,6},{5,7},{6,4},{7,5},{8,10},{9,11},{10,... | collective-permute-start | bytes 2359304 | tf_op jit(solution)/shard_map/ppermute | solution.py:29
  168.8 20.9 %collective-permute-start.13 = (bf16[192,2048]{1,0:T(8,128)(2,1)S(1)}, bf16[192,2048]{1,0:T(8,128)(2,1)S(1)}, u32[]{:S(2)}, u32[]{:S(2)}) collective-permute-start(bf16[192,2048]{1,0:T(8,128)(2,1)S(1)} %get-tuple-element.66), channel_id=1, source_target_pairs={{0,1},{1,0},{2,3},{3,2},{4,5},{5,4},{6,7},{7,6},{8,9},{9,8},{10,11... | collective-permute-start | bytes 2359304 | tf_op jit(solution)/shard_map/ppermute | solution.py:29
  176.4 29.2 %collective-permute-start.15 = (bf16[192,2048]{1,0:T(8,128)(2,1)S(1)}, bf16[192,2048]{1,0:T(8,128)(2,1)S(1)}, u32[]{:S(2)}, u32[]{:S(2)}) collective-permute-start(bf16[192,2048]{1,0:T(8,128)(2,1)S(1)} %get-tuple-element.68), channel_id=1, source_target_pairs={{0,2},{1,3},{2,0},{3,1},{4,6},{5,7},{6,4},{7,5},{8,10},{9,11},{10,... | collective-permute-start | bytes 2359304 | tf_op jit(solution)/shard_map/ppermute | solution.py:29
  183.0 23.0 %copy-start.1 = (f32[384,1024]{1,0:T(8,128)S(1)}, f32[384,1024]{1,0:T(8,128)}, u32[]{:S(2)}) copy-start(f32[384,1024]{1,0:T(8,128)} %get-tuple-element.52.z0.z1) | copy-start | bytes 4718596
  183.0 28.8 %collective-permute-start.12 = (bf16[192,2048]{1,0:T(8,128)(2,1)S(1)}, bf16[192,2048]{1,0:T(8,128)(2,1)S(1)}, u32[]{:S(2)}, u32[]{:S(2)}) collective-permute-start(bf16[192,2048]{1,0:T(8,128)(2,1)S(1)} %get-tuple-element.61), channel_id=1, source_target_pairs={{0,1},{1,0},{2,3},{3,2},{4,5},{5,4},{6,7},{7,6},{8,9},{9,8},{10,11... | collective-permute-start | bytes 2359304 | tf_op jit(solution)/shard_map/ppermute | solution.py:29
  188.9 25.5 %collective-permute-start.19 = (bf16[192,1024]{1,0:T(8,128)(2,1)S(1)}, bf16[192,1024]{1,0:T(8,128)(2,1)S(1)}, u32[]{:S(2)}, u32[]{:S(2)}) collective-permute-start(bf16[192,1024]{1,0:T(8,128)(2,1)S(1)} %shard_map.72), channel_id=1, source_target_pairs={{0,1},{1,0},{2,3},{3,2},{4,5},{5,4},{6,7},{7,6},{8,9},{9,8},{10,11... | collective-permute-start | bytes 1179656 | tf_op jit(solution)/shard_map/ppermute | solution.py:29
  189.7 24.7 %collective-permute-start.18 = (bf16[192,1024]{1,0:T(8,128)(2,1)S(1)}, bf16[192,1024]{1,0:T(8,128)(2,1)S(1)}, u32[]{:S(2)}, u32[]{:S(2)}) collective-permute-start(bf16[192,1024]{1,0:T(8,128)(2,1)S(1)} %shard_map.71), channel_id=1, source_target_pairs={{0,2},{1,3},{2,0},{3,1},{4,6},{5,7},{6,4},{7,5},{8,10},{9,11},{10,... | collective-permute-start | bytes 1179656 | tf_op jit(solution)/shard_map/ppermute | solution.py:29
  191.3 30.7 %collective-permute-start.17 = (bf16[192,1024]{1,0:T(8,128)(2,1)S(1)}, bf16[192,1024]{1,0:T(8,128)(2,1)S(1)}, u32[]{:S(2)}, u32[]{:S(2)}) collective-permute-start(bf16[192,1024]{1,0:T(8,128)(2,1)S(1)} %shard_map.70), channel_id=1, source_target_pairs={{0,1},{1,0},{2,3},{3,2},{4,5},{5,4},{6,7},{7,6},{8,9},{9,8},{10,11... | collective-permute-start | bytes 1179656 | tf_op jit(solution)/shard_map/ppermute | solution.py:29
  205.7 16.4 %collective-permute-start.14 = (bf16[192,1024]{1,0:T(8,128)(2,1)S(1)}, bf16[192,1024]{1,0:T(8,128)(2,1)S(1)}, u32[]{:S(2)}, u32[]{:S(2)}) collective-permute-start(bf16[192,1024]{1,0:T(8,128)(2,1)S(1)} %shard_map.69), channel_id=1, source_target_pairs={{0,2},{1,3},{2,0},{3,1},{4,6},{5,7},{6,4},{7,5},{8,10},{9,11},{10,... | collective-permute-start | bytes 1179656 | tf_op jit(solution)/shard_map/ppermute | solution.py:29

commit v2 on v0

--- a/solution.py
+++ b/solution.py
@@ -1,21 +1,641 @@
 import jax
 import jax.numpy as jnp
 from jax import lax
+from jax.experimental import pallas as pl
+from jax.experimental.pallas import tpu as pltpu
 from jax.sharding import PartitionSpec as P
 
 D = 4096
 ATTENDER_NUMBER = 32
 SF = 4
 CH = 128
+HD = D // ATTENDER_NUMBER
 
 
 EPSILON = 1e-05
+BF = jnp.bfloat16
+F32 = jnp.float32
+MIB = 2**20
+SMALL = 14 * MIB
+ANY = pl.BlockSpec(memory_space=pl.ANY)
+VMEM = pl.BlockSpec(memory_space=pltpu.VMEM)
+SMEM = pl.BlockSpec(memory_space=pltpu.SMEM)
 
 
 def passed_along(value, axis, by):
     peers = lax.axis_size(axis)
     pairs = [(i, i + by) for i in range(peers) if 0 <= i + by < peers]
     return lax.ppermute(value, axis, pairs)
+
+
+def swapped(value, axis, bit):
+    peers = lax.axis_size(axis)
+    return lax.ppermute(value, axis, [(i, i ^ bit) for i in range(peers)])
+
+
+def params(limit):
+    return pltpu.CompilerParams(vmem_limit_bytes=limit)
+
+
+def in_vmem(*arrays):
+    return [pltpu.with_memory_space_constraint(array, pltpu.VMEM) for array in arrays]
+
+
+def cost(flops, size):
+    return pl.CostEstimate(flops=int(flops), bytes_accessed=int(size), transcendentals=0)
+
+
+def dot(a, b):
+    return jnp.dot(a, b, preferred_element_type=F32)
+
+
+def dot_dims(a, b, da, db):
+    return lax.dot_general(a, b, (((da,), (db,)), ((), ())), preferred_element_type=F32)
+
+
+def pool_half(fine, tail, first, tail_first):
+    rows, width = fine.shape[0] // 2, fine.shape[1]
+    out_rows, parts = rows // SF, 4
+    cols = width // parts
+
+    def kernel(tail_ref, fine_ref, out_ref, ahead_rows, main_rows, pooled, tail_sem, fine_sems, out_sems):
+        here = [pl.ds(n * cols, cols) for n in range(parts)]
+        tail_copy = pltpu.make_async_copy(tail_ref.at[pl.ds(tail_first, 16)], ahead_rows, tail_sem)
+        copies = [
+            pltpu.make_async_copy(fine_ref.at[pl.ds(first, rows), c], main_rows.at[:, c], fine_sems.at[n])
+            for n, c in enumerate(here)
+        ]
+        tail_copy.start()
+        for copy in copies:
+            copy.start()
+        j = lax.broadcasted_iota(jnp.int32, (out_rows, rows), 0) * SF
+        i = lax.broadcasted_iota(jnp.int32, (out_rows, rows), 1)
+        main = jnp.where((i <= j) & (i > j - SF), 1.0 / SF, 0.0).astype(BF)
+        jt = lax.broadcasted_iota(jnp.int32, (out_rows, 16), 0) * SF
+        it = lax.broadcasted_iota(jnp.int32, (out_rows, 16), 1) - 16
+        ahead = jnp.where((it <= jt) & (it > jt - SF), 1.0 / SF, 0.0).astype(BF)
+        tail_copy.wait()
+        outs = []
+        for n, c in enumerate(here):
+            copies[n].wait()
+            total = dot(main, main_rows[:, c]) + dot(ahead, ahead_rows[:, c])
+            pooled[:, c] = total.astype(BF)
+            outs.append(pltpu.make_async_copy(pooled.at[:, c], out_ref.at[:, c], out_sems.at[n]))
+            outs[n].start()
+        for copy in outs:
+            copy.wait()
+
+    return pl.pallas_call(
+        kernel,
+        in_specs=[ANY, ANY],
+        out_specs=ANY,
+        out_shape=jax.ShapeDtypeStruct((out_rows, width), BF),
+        scratch_shapes=[
+            pltpu.VMEM((16, width), BF),
+            pltpu.VMEM((rows, width), BF),
+            pltpu.VMEM((out_rows, width), BF),
+            pltpu.SemaphoreType.DMA,
+            pltpu.SemaphoreType.DMA((parts,)),
+            pltpu.SemaphoreType.DMA((parts,)),
+        ],
+        compiler_params=params(58 * MIB),
+        cost_estimate=cost(2 * out_rows * rows * width, 2 * rows * width),
+    )(tail, fine)
+
+
+def prepare(raw, *after):
+    depth, kinds, width = raw.shape
+    lanes = 128
+    tiles = width // lanes
+    per = kinds * tiles
+    rows = raw.reshape(depth, kinds, tiles, lanes).transpose(0, 2, 1, 3).reshape(depth * per, lanes)
+    bk, slots, size = 256, 4, 8 * per
+    steps = depth // bk
+
+    def kernel(raw_ref, *refs):
+        w_refs, (buf, sems) = refs[-2 - kinds : -2], refs[-2:]
+
+
+        def fetch(step, slot):
+            return pltpu.make_async_copy(
+                raw_ref.at[pl.ds(pl.multiple_of(step * bk * per, bk * per), bk * per)], buf.at[slot], sems.at[slot]
+            )
+
+        for n in range(slots):
+            fetch(n, n).start()
+        to = lax.broadcasted_iota(jnp.int32, (size, size), 0)
+        of = lax.broadcasted_iota(jnp.int32, (size, size), 1)
+        order = jnp.where(of == (to % 8) * per + to // 8, 1.0, 0.0).astype(BF)
+
+        def loop(step, carry):
+            slot = lax.rem(step, slots)
+            fetch(step, slot).wait()
+
+            def sixteen(i, carry):
+                start = pl.multiple_of(i * 2 * size, 2 * size)
+                low, high = buf[slot, pl.ds(start, size)], buf[slot, pl.ds(start + size, size)]
+                moved = dot(order, jnp.concatenate([low, high], axis=1))
+                k = pl.ds(pl.multiple_of(step * bk + i * 16, 16), 16)
+                for q in range(per):
+                    eight = moved[q * 8 : (q + 1) * 8]
+                    w_refs[q % kinds][k, (q // kinds) * lanes : (q // kinds + 1) * lanes] = jnp.concatenate(
+                        [eight[:, :lanes], eight[:, lanes:]], axis=0
+                    ).astype(BF)
+                return carry
+
+            lax.fori_loop(0, bk // 16, sixteen, 0, unroll=4)
+
+            @pl.when(step + slots < steps)
+            def _():
+                fetch(step + slots, slot).start()
+
+            return carry
+
+        lax.fori_loop(0, steps, loop, 0)
+
+    return pl.pallas_call(
+        kernel,
+        in_specs=[ANY] * (1 + len(after)),
+        out_specs=[VMEM] * kinds,
+        out_shape=[pltpu.VMEM((depth, width), BF)] * kinds,
+        scratch_shapes=[pltpu.VMEM((slots, bk * per, lanes), BF), pltpu.SemaphoreType.DMA((slots,))],
+        compiler_params=params(10 * MIB),
+        cost_estimate=cost(2 * depth * kinds * width * size, 4 * depth * kinds * width),
+    )(rows, *after)
+
+
+def project(pieces, weights, types):
+    unit, depth = pieces[0].shape
+    rows, width, cols = 2 * unit, weights[0].shape[1], 512
+    count = len(weights)
+
+    def kernel(d0, d1, *refs):
+        w_refs, outs, held = refs[:count], refs[count : 2 * count], refs[-1]
+        held[:unit] = d0[...]
+        held[unit:] = d1[...]
+        for n in range(count):
+            for c in range(0, width, cols):
+                outs[n][:, c : c + cols] = dot(held[...], w_refs[n][:, c : c + cols]).astype(types[n])
+
+    return in_vmem(
+        *pl.pallas_call(
+            kernel,
+            in_specs=[VMEM] * (2 + count),
+            out_specs=[VMEM] * count,
+            out_shape=[pltpu.VMEM((rows, width), t) for t in types],
+            scratch_shapes=[pltpu.VMEM((rows, depth), BF)],
+            compiler_params=params(5 * MIB),
+            cost_estimate=cost(2 * rows * depth * width * count, 2 * rows * (depth + width)),
+        )(*pieces, *weights)
+    )
+
+
+def natural_units(me):
+    x, y, d = me ^ 1, me ^ 2, me ^ 3
+    return [2 * me, 2 * me + 1, 2 * x + 1, 2 * y + 1, 2 * x, 2 * y, 2 * d, 2 * d + 1]
+
+
+def known_state(me, groups, cum_columns, width):
+    unit = groups[0][0].shape[0] // 2
+    rows, heads = cum_columns.shape
+
+    def kernel(me_ref, *refs):
+        ks, vs, cum_ref = refs[0:3], refs[3:6], refs[6]
+        s_out, left_out, left, keys, vals = refs[7:]
+        total = cum_ref[rows - 1 : rows, :]
+        for n, natural in enumerate(natural_units(me_ref[0])):
+            cum = cum_ref[pl.ds(pl.multiple_of(natural * unit, unit), unit), :]
+            left[n * unit : (n + 1) * unit, :] = jnp.exp(total - cum)
+        left_out[...] = left[6 * unit :, :]
+        for pair in range(heads // 2):
+            here = slice(pair * 2 * HD, (pair + 1) * 2 * HD)
+            for g in range(3):
+                span = slice(2 * unit * g, 2 * unit * (g + 1))
+                vals[span] = vs[g][:, here]
+                for h in range(2):
+                    lane = slice((2 * pair + h) * HD, (2 * pair + h + 1) * HD)
+                    keys[span, h * HD : (h + 1) * HD] = (
+                        ks[g][:, lane].astype(F32) * left[span, 2 * pair + h : 2 * pair + h + 1]
+                    ).astype(BF)
+            both = dot_dims(keys[...], vals[...], 0, 0)
+            for h in range(2):
+                s_out[(2 * pair + h) * HD : (2 * pair + h + 1) * HD] = both[
+                    h * HD : (h + 1) * HD, h * HD : (h + 1) * HD
+                ]
+
+    return pl.pallas_call(
+        kernel,
+        in_specs=[SMEM] + [VMEM] * 7,
+        out_specs=[VMEM] * 2,
+        out_shape=[pltpu.VMEM((width, HD), F32), pltpu.VMEM((2 * unit, heads), F32)],
+        scratch_shapes=[
+            pltpu.VMEM((rows, heads), F32),
+            pltpu.VMEM((6 * unit, 2 * HD), BF),
+            pltpu.VMEM((6 * unit, 2 * HD), BF),
+        ],
+        compiler_params=params(4 * MIB),
+        cost_estimate=cost(8 * rows * HD * width, 8 * rows * width),
+    )(me, *[g[1] for g in groups], *[g[2] for g in groups], cum_columns)
+
+
+def last_keys_and_state(pieces, w_k, w_v, known, left):
+    unit, depth = pieces[0].shape
+    rows, width, cols = 2 * unit, w_k.shape[1], 512
+    here_heads = cols // HD
+
+    def kernel(d0, d1, wk_ref, wv_ref, known_ref, left_ref, k_out, v_out, s_out, held, keys):
+        held[:unit] = d0[...]
+        held[unit:] = d1[...]
+        for c in range(0, width, cols):
+            k_part = dot(held[...], wk_ref[:, c : c + cols]).astype(BF)
+            v_part = dot(held[...], wv_ref[:, c : c + cols]).astype(BF)
+            k_out[:, c : c + cols] = k_part
+            v_out[:, c : c + cols] = v_part
+            first = c // HD
+            for h in range(here_heads):
+                keys[:, h * HD : (h + 1) * HD] = (
+                    k_part[:, h * HD : (h + 1) * HD].astype(F32) * left_ref[:, first + h : first + h + 1]
+                ).astype(BF)
+            for pair in range(here_heads // 2):
+                span = slice(pair * 2 * HD, (pair + 1) * 2 * HD)
+                both = dot_dims(keys[:, span], v_part[:, span], 0, 0)
+                for h in range(2):
+                    head = slice((first + 2 * pair + h) * HD, (first + 2 * pair + h + 1) * HD)
+                    s_out[head] = (known_ref[head] + both[h * HD : (h + 1) * HD, h * HD : (h + 1) * HD]).astype(BF)
+
+    return pl.pallas_call(
+        kernel,
+        in_specs=[VMEM] * 6,
+        out_specs=[VMEM] * 3,
+        out_shape=[
+            pltpu.VMEM((rows, width), BF),
+            pltpu.VMEM((rows, width), BF),
+            jax.ShapeDtypeStruct((width, HD), BF),
+        ],
+        scratch_shapes=[pltpu.VMEM((rows, depth), BF), pltpu.VMEM((rows, cols), BF)],
+        compiler_params=params(5 * MIB),
+        cost_estimate=cost(4 * rows * depth * width, 4 * rows * (depth + width)),
+    )(*pieces, w_k, w_v, known, left)
+
+
+def local_attention(me, groups, w_out, cum_columns, cum_rows, width):
+    unit = groups[0][0].shape[0] // 2
+    rows, heads = cum_columns.shape
+    cols = 2 * HD
+    blocks = rows // CH
+
+    def kernel(me_ref, *refs):
+        ins, (cc_ref, cr_ref, w_ref), outs, w_kept, done = refs[:12], refs[12:15], refs[15:23], refs[23], refs[24]
+        q, k, v, a, s, w_sem = refs[25:]
+        done[...] = jnp.zeros_like(done)
+        w_copy = pltpu.make_async_copy(w_ref, w_kept, w_sem)
+        w_copy.start()
+        order = natural_units(me_ref[0])
+        places = [pl.ds(pl.multiple_of(n * unit, unit), unit) for n in order]
+        causal = lax.broadcasted_iota(jnp.int32, (CH, CH), 0) >= lax.broadcasted_iota(jnp.int32, (CH, CH), 1)
+        lane = lax.broadcasted_iota(jnp.int32, (rows, heads), 1)
+        sub = lax.broadcasted_iota(jnp.int32, (heads, rows), 0)
+
+        def loop(pair, carry):
+            lanes = pl.ds(pl.multiple_of(pair * cols, cols), cols)
+            for kind, to in enumerate((q, k, v)):
+                for n, place in enumerate(places):
+                    at = (n % 2) * unit
+                    to[place, :] = ins[3 * (n // 2) + kind][at : at + unit, lanes]
+            for h in range(2):
+                here = slice(h * HD, (h + 1) * HD)
+                column = jnp.sum(jnp.where(lane == 2 * pair + h, cc_ref[...], 0.0), axis=1, keepdims=True)
+                row = jnp.sum(jnp.where(sub == 2 * pair + h, cr_ref[...], 0.0), axis=0, keepdims=True)
+                s[:, here] = (q[:, here].astype(F32) * jnp.exp(column)).astype(BF)
+                state = jnp.zeros((HD, HD), F32)
+                for b in range(blocks):
+                    t = slice(b * CH, (b + 1) * CH)
+                    qb, kb, vb = q[t, here], k[t, here], v[t, here]
+                    ct, cs = column[t], row[:, t]
+                    before = column[b * CH - 1 : b * CH] if b else jnp.zeros((1, 1), F32)
+                    end = column[(b + 1) * CH - 1 : (b + 1) * CH]
+                    weight = jnp.where(causal, jnp.exp(jnp.minimum(ct - cs, 0.0)), 0.0)
+                    scores = (dot_dims(qb, kb, 1, 1) * weight).astype(BF)
+                    within = dot(scores, vb)
+                    if b:
+                        within = within + dot(qb, state.astype(BF)) * jnp.exp(ct - before)
+                    a[t, here] = within
+                    if b < blocks - 1:
+                        decayed = (kb.astype(F32) * jnp.exp(end - ct)).astype(BF)
+                        state = jnp.exp(end - before) * state + dot_dims(decayed, vb, 0, 0)
+            for n, place in enumerate(places):
+                at = (n % 2) * unit
+                outs[2 * (n // 2)][at : at + unit, lanes] = a[place, :]
+                outs[2 * (n // 2) + 1][at : at + unit, lanes] = s[place, :]
+            return carry
+
+        lax.fori_loop(0, heads // 2, loop, 0)
+        w_copy.wait()
+
+    outs = pl.pallas_call(
+        kernel,
+        in_specs=[SMEM] + [VMEM] * 14 + [ANY],
+        out_specs=[VMEM] * 10,
+        out_shape=[pltpu.VMEM((2 * unit, width), t) for _ in range(4) for t in (F32, BF)]
+        + [pltpu.VMEM(w_out.shape, BF), jax.ShapeDtypeStruct((8, HD), F32)],
+        scratch_shapes=[pltpu.VMEM((rows, cols), BF)] * 3
+        + [pltpu.VMEM((rows, cols), F32), pltpu.VMEM((rows, cols), BF), pltpu.SemaphoreType.DMA],
+        compiler_params=params(SMALL),
+        cost_estimate=cost(10 * rows * CH * width, 8 * rows * width),
+    )(me, *[part for group in groups for part in group[:3]], cum_columns, cum_rows, w_out)
+    *kept, done = outs
+    kept = in_vmem(*kept)
+    return [kept[2 * g : 2 * g + 2] for g in range(4)], kept[8], done
+
+
+def decay_sums(decay_log):
+    heads, rows = decay_log.shape
+
+    def kernel(d_ref, rows_ref, columns_ref, total_ref):
+        earlier = lax.broadcasted_iota(jnp.int32, (CH, CH), 0) <= lax.broadcasted_iota(jnp.int32, (CH, CH), 1)
+        ones = jnp.where(earlier, 1.0, 0.0)
+        ahead = jnp.zeros((heads, 1), F32)
+        for b in range(rows // CH):
+            here = slice(b * CH, (b + 1) * CH)
+            sums = ahead + jnp.dot(
+                d_ref[:, here], ones, preferred_element_type=F32, precision=lax.Precision.HIGHEST
+            )
+            rows_ref[:, here] = sums
+            columns_ref[here, :] = sums.T
+            ahead = sums[:, CH - 1 :]
+        total_ref[...] = jnp.broadcast_to(ahead, (heads, HD))
+
+    return pl.pallas_call(
+        kernel,
+        in_specs=[VMEM],
+        out_specs=[VMEM] * 3,
+        out_shape=[jax.ShapeDtypeStruct(shape, F32) for shape in ((heads, rows), (rows, heads), (heads, HD))],
+        compiler_params=params(SMALL),
+        cost_estimate=cost(12 * heads * rows * CH, 12 * heads * rows),
+    )(decay_log)
+
+
+def combined(core, pick, terms, factors, rows, after=()):
+    heads = rows // HD
+
+    def kernel(core_ref, *refs):
+        ins, f_ref, out_ref = refs[: len(terms)], refs[len(terms)], refs[-1]
+        for h in range(heads):
+            total = None
+            for n, ref in enumerate(ins):
+                at = pick(n, core_ref[0], h) * HD
+                term = ref[pl.ds(pl.multiple_of(at, HD), HD)].astype(F32) * f_ref[n, h : h + 1, :]
+                total = term if total is None else total + term
+            out_ref[h * HD : (h + 1) * HD] = total.astype(BF)
+
+    return pl.pallas_call(
+        kernel,
+        in_specs=[SMEM] + [VMEM] * (len(terms) + 1) + [ANY] * len(after),
+        out_specs=VMEM,
+        out_shape=jax.ShapeDtypeStruct((rows, HD), BF),
+        compiler_params=params(3 * MIB),
+        cost_estimate=cost(2 * len(terms) * rows * HD, 2 * (len(terms) + 1) * rows * HD),
+    )(core, *terms, factors, *after)
+
+
+def state_factors(total):
+    chips = lax.axis_size("seq") // 2
+    rank = lax.axis_index("seq")
+    core, chip = rank % 2, rank // 2
+    heads = total.shape[0]
+    half = heads // 2
+    first = core == 0
+    other = swapped(total, "seq", 1)
+    own_half = lambda value: lax.dynamic_slice_in_dim(value, core * half, half, 0)
+    one = jnp.ones((half, HD), F32)
+    later = jnp.exp(own_half(jnp.where(first, other, total)))
+    joining = jnp.stack([jnp.where(first, later, one), jnp.where(first, one, later)])
+    chip_total = own_half(total + other)
+    weights = []
+    passed = jnp.zeros((half, HD), F32)
+    for d in range(1, chips):
+        weights.append(jnp.where(chip >= d, jnp.exp(passed), 0.0))
+        if d < chips - 1:
+            passed = passed + passed_along(chip_total, "seq", 2 * d)
+    nothing = jnp.zeros((heads, HD), F32)
+    decay = jnp.where(first, 1.0, jnp.exp(other))
+    final = jnp.stack(
+        [
+            jnp.where(first, jnp.concatenate([decay[:half], nothing[half:]]), jnp.concatenate([nothing[:half], decay[half:]])),
+            jnp.where(first, jnp.concatenate([nothing[:half], decay[half:]]), jnp.concatenate([decay[:half], nothing[half:]])),
+            jnp.where(first, nothing, 1.0),
+        ]
+    )
+    return joining, jnp.stack(weights), final
+
+
+def state_of_chip(core, state, other, joining):
+    half = state.shape[0] // 2
+    heads = half // HD
+    return combined(core, lambda n, c, h: c * heads + h, [state, other], joining, half)
+
+
+def entering_state(core, chip_states, other, weights, final, after):
+    half = chip_states[0].shape[0]
+    heads = half // HD
+    entering = combined(core, lambda n, c, h: h, chip_states, weights, half, [after])
+    entering_other = swapped(entering, "seq", 1)
+    return combined(
+        core, lambda n, c, h: h if n == 2 else h % heads, [entering, entering_other, other], final, 2 * half
+    )
+
+
+def output_terms(parts, gain, incoming, w_out):
+    unit = parts[0][0].shape[0] // 2
+    width, model = w_out.shape
+    cols = model // 4
+    heads = width // HD
+
+    def kernel(a0, s0, z0, a1, s1, z1, gain_ref, in_ref, w_ref, out_a, out_b, gated, kept, out_sems):
+        for n, (a, s, z) in enumerate(((a0, s0, z0), (a1, s1, z1))):
+            span = slice(parts[n][3] * unit, (parts[n][3] + 1) * unit)
+            for h in range(heads):
+                here = slice(h * HD, (h + 1) * HD)
+                attended = a[span, here] + dot(s[span, here], in_ref[here])
+                mean = jnp.mean(attended * attended, axis=1, keepdims=True)
+                gate = z[span, here]
+                gated[n * unit : (n + 1) * unit, here] = (
+                    attended * lax.rsqrt(mean + EPSILON) * gain_ref[:, here] * (gate / (1.0 + jnp.exp(-gate)))
+                ).astype(BF)
+        outs = []
+        for n in range(4):
+            kept[n] = dot(gated[...], w_ref[:, n * cols : (n + 1) * cols]).astype(BF)
+            target = out_a if n < 2 else out_b
+            outs.append(pltpu.make_async_copy(kept.at[n], target.at[:, pl.ds((n % 2) * cols, cols)], out_sems.at[n]))
+            outs[n].start()
+        for copy in outs:
+            copy.wait()
+
+    args = [array for part in parts for array in part[:3]]
+    return pl.pallas_call(
+        kernel,
+        in_specs=[VMEM] * 9,
+        out_specs=[ANY] * 2,
+        out_shape=[jax.ShapeDtypeStruct((2 * unit, model // 2), BF)] * 2,
+        scratch_shapes=[
+            pltpu.VMEM((2 * unit, width), BF),
+            pltpu.VMEM((4, 2 * unit, cols), BF),
+            pltpu.SemaphoreType.DMA((4,)),
+        ],
+        compiler_params=params(SMALL),
+        cost_estimate=cost(4 * unit * width * model, 4 * unit * model),
+    )(*args, gain, incoming, w_out)
+
+
+def merged(own, arrived, widths, after):
+    rows = own.shape[0]
+    firsts = [sum(widths[:n]) for n in range(len(widths))]
+
+    def kernel(a, b, after_ref, *outs):
+        for first, width, out in zip(firsts, widths, outs):
+            here = slice(first, first + width)
+            out[...] = (a[:, here].astype(F32) + b[:, here].astype(F32)).astype(BF)
+
+    return pl.pallas_call(
+        kernel,
+        in_specs=[VMEM] * 2 + [ANY],
+        out_specs=[VMEM] * len(widths),
+        out_shape=[jax.ShapeDtypeStruct((rows, width), BF) for width in widths],
+        compiler_params=params(SMALL),
+        cost_estimate=cost(rows * own.shape[1], 6 * rows * own.shape[1]),
+    )(own, arrived, after)
+
+
+def add_coarse(fine, columns, width, previous=None):
+    rows, model = fine.shape
+    pieces = 3
+    tall = rows // pieces
+    coarse = tall // SF
+    flat = [term for _, terms in columns for term in terms]
+
+    def kernel(fine_ref, *refs):
+        terms, out_ref = refs[: len(flat)], refs[len(flat) + (previous is not None)]
+        fine_buf, term_buf, kept, fine_sems, term_sems, out_sems = refs[-6:]
+        term_copies, fine_copies, outs = [], [], []
+        for n, (first, _) in enumerate(columns):
+            for m in range(3):
+                source = terms[3 * n + m].at[:, pl.ds(flat[3 * n + m][1], width)]
+                copy = pltpu.make_async_copy(source, term_buf.at[3 * n + m], term_sems.at[3 * n + m])
+                copy.start()
+                term_copies.append(copy)
+            for piece in range(pieces):
+                place = (pl.ds(piece * tall, tall), pl.ds(first, width))
+                at = pieces * n + piece
+                copy = pltpu.make_async_copy(fine_ref.at[place], fine_buf.at[at], fine_sems.at[at])
+                copy.start()
+                fine_copies.append(copy)
+                outs.append(pltpu.make_async_copy(kept.at[at], out_ref.at[place], out_sems.at[at]))
+        r = lax.broadcasted_iota(jnp.int32, (tall, coarse), 0) // SF
+        c = lax.broadcasted_iota(jnp.int32, (tall, coarse), 1)
+        spread = jnp.where(r == c, 1.0, 0.0).astype(BF)
+        for n in range(len(columns)):
+            for m in range(3):
+                term_copies[3 * n + m].wait()
+            for piece in range(pieces):
+                at = pieces * n + piece
+                fine_copies[at].wait()
+                total = fine_buf[at].astype(F32)
+                for m in range(3):
+                    total += dot(spread, term_buf[3 * n + m, piece * coarse : (piece + 1) * coarse])
+                kept[at] = total.astype(BF)
+                outs[at].start()
+        for copy in outs:
+            copy.wait()
+
+    args = [fine] + [term for term, _ in flat]
+    aliases = {}
+    if previous is not None:
+        args.append(previous)
+        aliases = {len(args) - 1: 0}
+    count = pieces * len(columns)
+    return pl.pallas_call(
+        kernel,
+        in_specs=[ANY] * len(args),
+        out_specs=ANY,
+        out_shape=jax.ShapeDtypeStruct((rows, model), BF),
+        input_output_aliases=aliases,
+        scratch_shapes=[
+            pltpu.VMEM((count, tall, width), BF),
+            pltpu.VMEM((len(flat), rows // SF, width), BF),
+            pltpu.VMEM((count, tall, width), BF),
+            pltpu.SemaphoreType.DMA((count,)),
+            pltpu.SemaphoreType.DMA((len(flat),)),
+            pltpu.SemaphoreType.DMA((count,)),
+        ],
+        compiler_params=params(24 * MIB),
+        cost_estimate=cost(12 * rows * coarse * width, 8 * rows * width),
+    )(*args)
+
+
+def body_square(fine_rows, w_inputs, w_out, head_gain, decay_log):
+    model = fine_rows.shape[1]
+    fine_count = fine_rows.shape[0]
+    heads, rows_coarse = decay_log.shape
+    width = heads * HD
+    place = jnp.reshape(lax.axis_index("mp"), (1,)).astype(jnp.int32)
+    core = jnp.reshape(lax.axis_index("seq") % 2, (1,)).astype(jnp.int32)
+
+    before = passed_along(fine_rows[fine_count - 16 :], ("seq", "mp"), 1)
+    p1 = pool_half(fine_rows, fine_rows, fine_count // 2, fine_count // 2 - 16)
+    x1 = swapped(p1, "mp", 1)
+    y1 = swapped(p1, "mp", 2)
+    p0 = pool_half(fine_rows, before, 0, 0)
+    x0 = swapped(p0, "mp", 1)
+    y0 = swapped(p0, "mp", 2)
+    cum_rows, cum_columns, total = decay_sums(decay_log)
+    joining, state_weights, final = state_factors(total)
+    w_q, w_k, w_v, w_g = weights = in_vmem(*prepare(w_inputs, p0, joining, state_weights, final))
+    d1 = swapped(y1, "mp", 1)
+    d0 = swapped(x0, "mp", 2)
+
+    types = [BF, BF, BF, F32]
+    first = project([p0, p1], weights, types)
+    second = project([x1, y1], weights, types)
+    third = project([x0, y0], weights, types)
+    known, left = in_vmem(*known_state(place, [first, second, third], cum_columns, width))
+    k_last, v_last, state = last_keys_and_state([d0, d1], w_k, w_v, known, left)
+    k_last, v_last = in_vmem(k_last, v_last)
+    other = swapped(state, "seq", 1)
+    q_last, g_last = project([d0, d1], [w_q, w_g], [BF, F32])
+    chip_state = state_of_chip(core, state, other, joining)
+    chip_states = [passed_along(chip_state, "seq", 2 * d) for d in range(1, lax.axis_size("seq") // 2)]
+    groups, w_kept, attended = local_attention(
+        place, [first, second, third, [q_last, k_last, v_last]], pltpu.with_memory_space_constraint(w_out, pltpu.HBM), cum_columns, cum_rows, width
+    )
+    own, second, third, last = [(*group, gate) for group, gate in zip(groups, (first[3], second[3], third[3], g_last))]
+    incoming = entering_state(core, chip_states, other, state_weights, final, attended)
+
+    gain = head_gain[None]
+    terms = lambda parts: output_terms(parts, gain, incoming, w_kept)
+    far_a, far_b = terms([(*last, 0), (*last, 1)])
+    got_a = swapped(far_a, "mp", 1)
+    got_b = swapped(far_b, "mp", 2)
+    x_a, x_b = terms([(*third, 0), (*second, 0)])
+    from_x_a = swapped(x_a, "mp", 1)
+    y_a, y_b = terms([(*third, 1), (*second, 1)])
+    from_y_b = swapped(y_b, "mp", 2)
+    own_a, own_b = terms([(*own, 0), (*own, 1)])
+    half = model // 2
+    widths = (half - half // 4, half // 4)
+    from_x_b = [swapped(part, "mp", 1) for part in merged(x_b, got_b, widths, own_a)]
+    from_y_a = [swapped(part, "mp", 2) for part in merged(y_a, got_a, widths, own_a)]
+    out = None
+    for n, at in enumerate((0, widths[0])):
+        out = add_coarse(
+            fine_rows,
+            [
+                (at, [(own_a, at), (from_x_a, at), (from_y_a[n], 0)]),
+                (half + at, [(own_b, at), (from_y_b, at), (from_x_b[n], 0)]),
+            ],
+            widths[n],
+            out,
+        )
+    return out
 
 
 def body(fine_rows, w_inputs, w_out, head_gain, decay_log):
@@ -120,8 +740,9 @@
 
 
 def solution(mesh):
+    square = mesh.shape["mp"] == 4 and mesh.shape["seq"] % 2 == 0 and mesh.shape["seq"] > 2
     return jax.shard_map(
-        body,
+        body_square if square else body,
         mesh=mesh,
         in_specs=(
             P(("seq", "mp"), None),

time: 328 us -> 187 us (0.57)
  Pallas kernels: 0 us -> 91.4 us
  waiting for transfers between devices: 120 us -> 45.9 us
  local copies, waits for them, and re-layouts: 77.8 us -> 6.97 us
  matrix products: 53.8 us -> 0 us
  other arithmetic: 39.5 us -> 0.25 us
  starting transfers between devices: 5.11 us -> 38.6 us
  blocking collectives: 17 us -> 0 us
  between operations: 14 us -> 0.61 us
    pallas_call x0 -> x22, Pallas kernels: none -> 91.4 us  [the longest x4 23.6 us: project(): pl.pallas_call(kernel, in_specs=[VMEM] * (2 + count), out_specs=[VMEM] *...]
    reduce_scatter x1 -> x0, waiting for transfers between devices: 69.8 us -> none  [body(): lax.psum_scatter(jnp.dot(gated_rows, w_out, preferred_element_type=jnp.fl...]
    dot_general x5 -> x0, matrix products: 53.8 us -> none  [the longest x1 33.5 us: body(): jnp.dot(lax.all_gather(pooled, 'mp', axis=0, tiled=True), weights_flat, p...]
    all_gather x2 -> x0, waiting for transfers between devices: 48.4 us -> none  [the longest x1 46.3 us: body(): lax.all_gather(pooled, 'mp', axis=0, tiled=True)]
    ppermute x0 -> x17, waiting for transfers between devices: none -> 38.7 us  [swapped(): return lax.ppermute(value, axis, [(i, i ^ bit) for i in range(peers)])]
    unnamed x28 -> x20, local copies, waits for them, and re-layouts: 34 us -> 5.96 us
    convert_element_type x4 -> x0, other arithmetic: 23.4 us -> none  [the longest x1 11.5 us: body(): return (fine_rows.astype(jnp.float32) + upsampled).astype(jnp.bfloat16)]
    ppermute x0 -> x17, starting transfers between devices: none -> 18.8 us  [swapped(): return lax.ppermute(value, axis, [(i, i ^ bit) for i in range(peers)])]
  transfers between devices with their start and end apart: 4 -> 23, of which waited for: 4 -> 9; matrix products, arithmetic and copies ran while one was open for 11% -> 1% of each run, Pallas kernels for 0% -> 43%
where the time goes in v2:
time: 187 us; the launch traced here: 184 us
  Pallas kernels  91.4 us (49%)
  waiting for transfers between devices  45.9 us (25%)
  starting transfers between devices  38.6 us (21%)
  local copies, waits for them, and re-layouts  6.97 us (4%)
    ppermute x17, waiting for transfers between devices, swapped(): return lax.ppermute(value, axis, [(i, i ^ bit) for i in range(peers)])  38.7 us
    pallas_call x4, Pallas kernels, project(): pl.pallas_call(kernel, in_specs=[VMEM] * (2 + count), out_specs=[VMEM] *...  23.6 us
    pallas_call x1, Pallas kernels, prepare(): pl.pallas_call(kernel, in_specs=[ANY] * (1 + len(after)), out_specs=[VMEM...  22.2 us
    ppermute x6, starting transfers between devices, passed_along(): return lax.ppermute(value, axis, pairs)  19.7 us
    ppermute x17, starting transfers between devices, swapped(): return lax.ppermute(value, axis, [(i, i ^ bit) for i in range(peers)])  18.8 us
    pallas_call x4, Pallas kernels, output_terms(): pl.pallas_call(kernel, in_specs=[VMEM] * 9, out_specs=[ANY] * 2, out_shap...  11.9 us
    pallas_call x2, Pallas kernels, add_coarse(): pl.pallas_call(kernel, in_specs=[ANY] * len(args), out_specs=ANY, out_sha...  10.2 us
    pallas_call x1, Pallas kernels, local_attention(): pl.pallas_call(kernel, in_specs=[SMEM] + [VMEM] * 14 + [ANY], out_specs=[...  9.23 us
  transfers between devices with their start and end apart: 23, of which 9 were waited for; matrix products, arithmetic and copies ran while one was open for 1% of the time, Pallas kernels for 43%

profile of v2, /device:TPU:0, one launch (start us, length us, event | category | flops | bytes accessed | tf_op | source)
XLA Modules:
  0.0 183.7 jit_solution(16138713088144086503)
XLA Ops:
  0.0 0.7 copy-done.5
  0.7 0.8 shard_map.57
  1.5 0.5 collective-permute-start.1
  2.0 3.7 %shard_map.56.d1 = bf16[96,4096]{1,0:T(8,128)(2,1)} custom-call(bf16[768,4096]{1,0:T(8,128)(2,1)} %fine_ref.7, bf16[768,4096]{1,0:T(8,128)(2,1)} %fine_ref.7), custom_call_target="tpu_custom_call" | custom-call | flops 301989888 | bytes 3145728 | tf_op jit(solution)/shard_map/pallas_call | solution.py:88
  5.7 2.6 %collective-permute-start.4 = (bf16[96,4096]{1,0:T(8,128)(2,1)}, bf16[96,4096]{1,0:T(8,128)(2,1)S(1)}, u32[]{:S(2)}, u32[]{:S(2)}) collective-permute-start(bf16[96,4096]{1,0:T(8,128)(2,1)} %shard_map.56.d1), channel_id=1, source_target_pairs={{0,1},{1,0},{2,3},{3,2},{4,5},{5,4},{6,7},{7,6},{8,9},{9,8},{10,11... | collective-permute-start | bytes 2359304 | tf_op jit(solution)/shard_map/ppermute | solution.py:33
  8.3 1.5 collective-permute-start.5
  9.8 0.9 slice.10
  10.7 2.4 %collective-permute-start = (bf16[16,4096]{1,0:T(8,128)(2,1)S(1)}, bf16[16,4096]{1,0:T(8,128)(2,1)S(1)}, u32[]{:S(2)}, u32[]{:S(2)}) collective-permute-start(bf16[16,4096]{1,0:T(8,128)(2,1)S(1)} %slice.10), channel_id=1, source_target_pairs={{0,1},{1,2},{2,3},{3,4},{4,5},{5,6},{6,7},{7,8},{8,9},{9,10},{10,1... | collective-permute-start | bytes 393224 | tf_op jit(solution)/shard_map/ppermute | solution.py:28
  13.4 3.5 %collective-permute-start.2 = (f32[4,128]{1,0:T(4,128)S(1)}, f32[4,128]{1,0:T(4,128)S(1)}, u32[]{:S(2)}, u32[]{:S(2)}) collective-permute-start(f32[4,128]{1,0:T(4,128)S(1)} %constant_dynamic-slice_fusion), channel_id=1, source_target_pairs={{0,8},{4,12},{8,16},{12,20},{16,24},{20,28},{1,9},{5,13},{9,17},{1... | collective-permute-start | bytes 6152 | tf_op jit(solution)/shard_map/ppermute | solution.py:28
  16.9 4.5 %collective-permute-start.3 = (f32[4,128]{1,0:T(4,128)S(1)}, f32[4,128]{1,0:T(4,128)S(1)}, u32[]{:S(2)}, u32[]{:S(2)}) collective-permute-start(f32[4,128]{1,0:T(4,128)S(1)} %constant_dynamic-slice_fusion), channel_id=1, source_target_pairs={{0,16},{4,20},{8,24},{12,28},{1,17},{5,21},{9,25},{13,29},{2,18},{... | collective-permute-start | bytes 6152 | tf_op jit(solution)/shard_map/ppermute | solution.py:28
  21.5 1.2 collective-permute-done.3
  22.8 6.0 %collective-permute-done.tail_ref = bf16[16,4096]{1,0:T(8,128)(2,1)S(1)} collective-permute-done((bf16[16,4096]{1,0:T(8,128)(2,1)S(1)}, bf16[16,4096]{1,0:T(8,128)(2,1)S(1)}, u32[]{:S(2)}, u32[]{:S(2)}) %collective-permute-start) | collective-permute-done | bytes 131104 | tf_op jit(solution)/shard_map/ppermute | solution.py:28
  28.8 0.6 copy-done.6
  29.4 3.7 %shard_map.55.refs_0_.d0 = bf16[96,4096]{1,0:T(8,128)(2,1)} custom-call(bf16[16,4096]{1,0:T(8,128)(2,1)} %copy-done.6, bf16[768,4096]{1,0:T(8,128)(2,1)} %fine_ref.7), custom_call_target="tpu_custom_call" | custom-call | flops 301989888 | bytes 3145728 | tf_op jit(solution)/shard_map/pallas_call | solution.py:88
  33.1 2.5 %collective-permute-start.6 = (bf16[96,4096]{1,0:T(8,128)(2,1)}, bf16[96,4096]{1,0:T(8,128)(2,1)S(1)}, u32[]{:S(2)}, u32[]{:S(2)}) collective-permute-start(bf16[96,4096]{1,0:T(8,128)(2,1)} %shard_map.55.refs_0_.d0), channel_id=1, source_target_pairs={{0,1},{1,0},{2,3},{3,2},{4,5},{5,4},{6,7},{7,6},{8,9},{9,8},{10,11... | collective-permute-start | bytes 2359304 | tf_op jit(solution)/shard_map/ppermute | solution.py:33
  35.6 1.5 collective-permute-start.7
  37.1 1.2 copy-done.2
  38.3 22.2 %shard_map.58 = (bf16[4096,1024]{1,0:T(8,128)(2,1)S(1)}, bf16[4096,1024]{1,0:T(8,128)(2,1)S(1)}, bf16[4096,1024]{1,0:T(8,128)(2,1)S(1)}, bf16[4096,1024]{1,0:T(8,128)(2,1)S(1)}) custom-call(bf16[131072,128]{1,0:T(8,128)(2,1)} %bitcast.28, bf16[96,4096]{1,0:T(8,128)(2,1)S(1)} %copy-done.2, f32[2,4,128]{2,1,0:T(4,128)S(1)} %pad_maximum_fusion.1.refs_1_.refs_2_, ...), custom_call_target="tpu_custom_call" | custom-call | flops 8589934592 | bytes 67108864 | tf_op jit(solution)/shard_map/pallas_call | solution.py:156
  60.5 6.7 %shard_map.59 = (bf16[192,1024]{1,0:T(8,128)(2,1)S(1)}, bf16[192,1024]{1,0:T(8,128)(2,1)S(1)}, bf16[192,1024]{1,0:T(8,128)(2,1)S(1)}, f32[192,1024]{1,0:T(8,128)S(1)}) custom-call(bf16[96,4096]{1,0:T(8,128)(2,1)S(1)} %copy-done.2, bf16[96,4096]{1,0:T(8,128)(2,1)S(1)} %copy-done.3, bf16[4096,1024]{1,0:T(8,128)(2,1)S(1)} %get-tuple-element.54.refs_0_, ...), custom_call_target="tpu_custom_call" | custom-call | flops 6442450944 | bytes 1966080 | tf_op jit(solution)/shard_map/pallas_call | solution.py:181
  67.9 6.7 %shard_map.60 = (bf16[192,1024]{1,0:T(8,128)(2,1)S(1)}, bf16[192,1024]{1,0:T(8,128)(2,1)S(1)}, bf16[192,1024]{1,0:T(8,128)(2,1)S(1)}, f32[192,1024]{1,0:T(8,128)S(1)}) custom-call(bf16[96,4096]{1,0:T(8,128)(2,1)S(1)} %collective-permute-done.4.d0, bf16[96,4096]{1,0:T(8,128)(2,1)S(1)} %collective-permute-done.5.d1, ...), custom_call_target="tpu_custom_call" | custom-call | flops 6442450944 | bytes 1966080 | tf_op jit(solution)/shard_map/pallas_call | solution.py:181
  74.6 6.9 %shard_map.61 = (bf16[192,1024]{1,0:T(8,128)(2,1)S(1)}, bf16[192,1024]{1,0:T(8,128)(2,1)S(1)}, bf16[192,1024]{1,0:T(8,128)(2,1)S(1)}, f32[192,1024]{1,0:T(8,128)S(1)}) custom-call(bf16[96,4096]{1,0:T(8,128)(2,1)S(1)} %collective-permute-done.6.d0, bf16[96,4096]{1,0:T(8,128)(2,1)S(1)} %collective-permute-done.7.d1, ...), custom_call_target="tpu_custom_call" | custom-call | flops 6442450944 | bytes 1966080 | tf_op jit(solution)/shard_map/pallas_call | solution.py:181
  81.5 1.6 shard_map.63
  83.1 2.8 %collective-permute-done.9.d1 = bf16[96,4096]{1,0:T(8,128)(2,1)S(1)} collective-permute-done((bf16[96,4096]{1,0:T(8,128)(2,1)S(1)}, bf16[96,4096]{1,0:T(8,128)(2,1)S(1)}, u32[]{:S(2)}, u32[]{:S(2)}) %collective-permute-start.9) | collective-permute-done | bytes 786464 | tf_op jit(solution)/shard_map/ppermute | solution.py:33
  86.1 3.4 %copy-done.1 = bf16[4096,1024]{1,0:T(8,128)(2,1)S(1)} copy-done((bf16[4096,1024]{1,0:T(8,128)(2,1)S(1)}, bf16[4096,1024]{1,0:T(8,128)(2,1)}, u32[]{:S(2)}) %copy-start.1) | copy-done | bytes 8388632
  89.5 3.9 %shard_map.64 = (bf16[192,1024]{1,0:T(8,128)(2,1)S(1)}, bf16[192,1024]{1,0:T(8,128)(2,1)S(1)}, bf16[1024,128]{1,0:T(8,128)(2,1)S(1)}) custom-call(bf16[96,4096]{1,0:T(8,128)(2,1)S(1)} %collective-permute-done.8.d0, bf16[96,4096]{1,0:T(8,128)(2,1)S(1)} %collective-permute-done.9.d1, bf16[4096,1024]{1,0:T(8,128)(2,1)S(1)} %copy-done.1, ...), custom_call_target="tpu_custom_call" | custom-call | flops 3221225472 | bytes 3932160 | tf_op jit(solution)/shard_map/pallas_call | solution.py:266
  93.5 1.5 collective-permute-done.10.refs_1_.refs_2_
  95.1 3.5 %collective-permute-start.11 = (bf16[512,128]{1,0:T(8,128)(2,1)S(1)}, bf16[512,128]{1,0:T(8,128)(2,1)S(1)}, u32[]{:S(2)}, u32[]{:S(2)}) collective-permute-start(bf16[512,128]{1,0:T(8,128)(2,1)S(1)} %shard_map.66), channel_id=1, source_target_pairs={{0,8},{4,12},{8,16},{12,20},{16,24},{20,28},{1,9},{5,13},{9,17},{1... | collective-permute-start | bytes 393224 | tf_op jit(solution)/shard_map/ppermute | solution.py:28
  98.6 4.5 %collective-permute-start.12 = (bf16[512,128]{1,0:T(8,128)(2,1)S(1)}, bf16[512,128]{1,0:T(8,128)(2,1)S(1)}, u32[]{:S(2)}, u32[]{:S(2)}) collective-permute-start(bf16[512,128]{1,0:T(8,128)(2,1)S(1)} %shard_map.66), channel_id=1, source_target_pairs={{0,16},{4,20},{8,24},{12,28},{1,17},{5,21},{9,25},{13,29},{2,18},{... | collective-permute-start | bytes 393224 | tf_op jit(solution)/shard_map/ppermute | solution.py:28
  103.1 1.3 collective-permute-start.13
  104.4 3.4 %shard_map.62 = (bf16[192,1024]{1,0:T(8,128)(2,1)S(1)}, f32[192,1024]{1,0:T(8,128)S(1)}) custom-call(bf16[96,4096]{1,0:T(8,128)(2,1)S(1)} %collective-permute-done.8.d0, bf16[96,4096]{1,0:T(8,128)(2,1)S(1)} %collective-permute-done.9.d1, bf16[4096,1024]{1,0:T(8,128)(2,1)S(1)} %get-tuple-element.54.refs_0_, ...), custom_call_target="tpu_custom_call" | custom-call | flops 3221225472 | bytes 1966080 | tf_op jit(solution)/shard_map/pallas_call | solution.py:181
  107.9 9.2 %shard_map.65 = (f32[192,1024]{1,0:T(8,128)S(1)}, bf16[192,1024]{1,0:T(8,128)(2,1)S(1)}, f32[192,1024]{1,0:T(8,128)S(1)}, bf16[192,1024]{1,0:T(8,128)(2,1)S(1)},...) custom-call(s32[1]{0:T(128)} %bitcast.me_ref, ...), custom_call_target="tpu_custom_call" | custom-call | flops 1006632960 | bytes 6291456 | tf_op jit(solution)/shard_map/pallas_call | solution.py:335
  117.3 1.3 collective-permute-done.14.refs_1_
  118.8 3.0 %shard_map.72 = (bf16[192,2048]{1,0:T(8,128)(2,1)S(1)}, bf16[192,2048]{1,0:T(8,128)(2,1)S(1)}) custom-call(f32[192,1024]{1,0:T(8,128)S(1)} %get-tuple-element.89.a0.a1, bf16[192,1024]{1,0:T(8,128)(2,1)S(1)} %get-tuple-element.90.s0.s1, f32[192,1024]{1,0:T(8,128)S(1)} %get-tuple-element.91.z0.z1, f32[192,1024]{1,0:T(8,128)S(1)} %get-tuple-element.89.a0.a1, ...), custom_call_target="tpu_custom_call" | custom-call | flops 1610612736 | bytes 1572864 | tf_op jit(solution)/shard_map/pallas_call | solution.py:475
  121.8 1.6 collective-permute-start.16
  123.3 0.5 collective-permute-start.19
  123.9 3.0 %shard_map.70 = (bf16[192,2048]{1,0:T(8,128)(2,1)S(1)}, bf16[192,2048]{1,0:T(8,128)(2,1)S(1)}) custom-call(f32[192,1024]{1,0:T(8,128)S(1)} %get-tuple-element.81.a0, bf16[192,1024]{1,0:T(8,128)(2,1)S(1)} %get-tuple-element.82.s0, f32[192,1024]{1,0:T(8,128)S(1)} %get-tuple-element.83.z0, f32[192,1024]{1,0:T(8,128)S(1)} %get-tuple-element.84.a1, ...), custom_call_target="tpu_custom_call" | custom-call | flops 1610612736 | bytes 1572864 | tf_op jit(solution)/shard_map/pallas_call | solution.py:475
  126.8 1.7 collective-permute-start.15
  128.6 3.0 %shard_map.71 = (bf16[192,2048]{1,0:T(8,128)(2,1)S(1)}, bf16[192,2048]{1,0:T(8,128)(2,1)S(1)}) custom-call(f32[192,1024]{1,0:T(8,128)S(1)} %get-tuple-element.81.a0, bf16[192,1024]{1,0:T(8,128)(2,1)S(1)} %get-tuple-element.82.s0, f32[192,1024]{1,0:T(8,128)S(1)} %get-tuple-element.83.z0, f32[192,1024]{1,0:T(8,128)S(1)} %get-tuple-element.84.a1, ...), custom_call_target="tpu_custom_call" | custom-call | flops 1610612736 | bytes 1572864 | tf_op jit(solution)/shard_map/pallas_call | solution.py:475
  131.5 0.4 collective-permute-start.18
  132.0 3.0 %shard_map.69 = (bf16[192,2048]{1,0:T(8,128)(2,1)S(1)}, bf16[192,2048]{1,0:T(8,128)(2,1)S(1)}) custom-call(f32[192,1024]{1,0:T(8,128)S(1)} %get-tuple-element.74.a0.a1, bf16[192,1024]{1,0:T(8,128)(2,1)S(1)} %get-tuple-element.75.s0.s1, f32[192,1024]{1,0:T(8,128)S(1)} %get-tuple-element.76.z0.z1, f32[192,1024]{1,0:T(8,128)S(1)} %get-tuple-element.74.a0.a1, ...), custom_call_target="tpu_custom_call" | custom-call | flops 1610612736 | bytes 1572864 | tf_op jit(solution)/shard_map/pallas_call | solution.py:475
  135.0 7.3 %collective-permute-done.16.b = bf16[192,2048]{1,0:T(8,128)(2,1)S(1)} collective-permute-done((bf16[192,2048]{1,0:T(8,128)(2,1)S(1)}, bf16[192,2048]{1,0:T(8,128)(2,1)S(1)}, u32[]{:S(2)}, u32[]{:S(2)}) %collective-permute-start.16) | collective-permute-done | bytes 786464 | tf_op jit(solution)/shard_map/ppermute | solution.py:33
  142.4 1.7 collective-permute-start.21
  144.8 1.5 collective-permute-start.17
  146.2 12.8 %collective-permute-done.15.refs_1_ = bf16[192,2048]{1,0:T(8,128)(2,1)S(1)} collective-permute-done((bf16[192,2048]{1,0:T(8,128)(2,1)S(1)}, bf16[192,2048]{1,0:T(8,128)(2,1)S(1)}, u32[]{:S(2)}, u32[]{:S(2)}) %collective-permute-start.15) | collective-permute-done | bytes 786464 | tf_op jit(solution)/shard_map/ppermute | solution.py:33
  159.1 1.5 collective-permute-start.20
  160.6 12.6 %collective-permute-done.21.refs_2_ = bf16[192,1536]{1,0:T(8,128)(2,1)S(1)} collective-permute-done((bf16[192,1536]{1,0:T(8,128)(2,1)S(1)}, bf16[192,1536]{1,0:T(8,128)(2,1)S(1)}, u32[]{:S(2)}, u32[]{:S(2)}) %collective-permute-start.21) | collective-permute-done | bytes 589856 | tf_op jit(solution)/shard_map/ppermute | solution.py:33
  173.3 6.5 %shard_map.75.refs_6_ = bf16[768,4096]{1,0:T(8,128)(2,1)} custom-call(bf16[768,4096]{1,0:T(8,128)(2,1)S(1)} %bitcast.23, bf16[192,2048]{1,0:T(8,128)(2,1)S(1)} %get-tuple-element.80.after_ref.refs_0_, bf16[192,2048]{1,0:T(8,128)(2,1)S(1)} %collective-permute-done.15.refs_1_, bf16[192,1536]{1,0:T(8,128)(2,1)S(1)} %collective-permute-done.21.refs_2_, ...), custom_call_target="tpu_custom_call" | custom-call | flops 905969664 | bytes 9437184 | tf_op jit(solution)/shard_map/pallas_call | solution.py:556
  179.8 3.7 %shard_map.76 = bf16[768,4096]{1,0:T(8,128)(2,1)} custom-call(bf16[768,4096]{1,0:T(8,128)(2,1)S(1)} %bitcast.23, bf16[192,2048]{1,0:T(8,128)(2,1)S(1)} %get-tuple-element.80.after_ref.refs_0_, bf16[192,2048]{1,0:T(8,128)(2,1)S(1)} %collective-permute-done.15.refs_1_, ...), custom_call_target="tpu_custom_call", output_to_operand_aliasing={{}: (7, {})} | custom-call | flops 301989888 | bytes 3145728 | tf_op jit(solution)/shard_map/pallas_call | solution.py:556
  (53 shorter events, 2.5 us)
Async XLA Ops:
  0.0 0.7 copy-start.5
  0.7 12.6 %copy-start.7 = (pred[8]{0:T(512)(128)(4,1)S(1)}, pred[8]{0:T(512)(128)(4,1)}, u32[]{:S(2)}) copy-start(pred[8]{0:T(512)(128)(4,1)} %constant.51.clone.1) | copy-start | bytes 28
  1.5 11.8 %collective-permute-start.1 = (f32[8,128]{1,0:T(8,128)S(1)}, f32[8,128]{1,0:T(8,128)S(1)}, u32[]{:S(2)}, u32[]{:S(2)}) collective-permute-start(f32[8,128]{1,0:T(8,128)S(1)} %get-tuple-element.53), channel_id=1, source_target_pairs={{0,4},{4,0},{8,12},{12,8},{16,20},{20,16},{24,28},{28,24},{1,5},{5... | collective-permute-start | bytes 12296 | tf_op jit(solution)/shard_map/ppermute | solution.py:33
  5.7 62.2 %collective-permute-start.4 = (bf16[96,4096]{1,0:T(8,128)(2,1)}, bf16[96,4096]{1,0:T(8,128)(2,1)S(1)}, u32[]{:S(2)}, u32[]{:S(2)}) collective-permute-start(bf16[96,4096]{1,0:T(8,128)(2,1)} %shard_map.56.d1), channel_id=1, source_target_pairs={{0,1},{1,0},{2,3},{3,2},{4,5},{5,4},{6,7},{7,6},{8,9},{9,8},{10,11... | collective-permute-start | bytes 2359304 | tf_op jit(solution)/shard_map/ppermute | solution.py:33
  8.3 58.9 %collective-permute-start.5 = (bf16[96,4096]{1,0:T(8,128)(2,1)}, bf16[96,4096]{1,0:T(8,128)(2,1)S(1)}, u32[]{:S(2)}, u32[]{:S(2)}) collective-permute-start(bf16[96,4096]{1,0:T(8,128)(2,1)} %shard_map.56.d1), channel_id=1, source_target_pairs={{0,2},{1,3},{2,0},{3,1},{4,6},{5,7},{6,4},{7,5},{8,10},{9,11},{10,... | collective-permute-start | bytes 2359304 | tf_op jit(solution)/shard_map/ppermute | solution.py:33
  10.7 18.0 %collective-permute-start = (bf16[16,4096]{1,0:T(8,128)(2,1)S(1)}, bf16[16,4096]{1,0:T(8,128)(2,1)S(1)}, u32[]{:S(2)}, u32[]{:S(2)}) collective-permute-start(bf16[16,4096]{1,0:T(8,128)(2,1)S(1)} %slice.10), channel_id=1, source_target_pairs={{0,1},{1,2},{2,3},{3,4},{4,5},{5,6},{6,7},{7,8},{8,9},{9,10},{10,1... | collective-permute-start | bytes 393224 | tf_op jit(solution)/shard_map/ppermute | solution.py:28
  13.4 8.1 %collective-permute-start.2 = (f32[4,128]{1,0:T(4,128)S(1)}, f32[4,128]{1,0:T(4,128)S(1)}, u32[]{:S(2)}, u32[]{:S(2)}) collective-permute-start(f32[4,128]{1,0:T(4,128)S(1)} %constant_dynamic-slice_fusion), channel_id=1, source_target_pairs={{0,8},{4,12},{8,16},{12,20},{16,24},{20,28},{1,9},{5,13},{9,17},{1... | collective-permute-start | bytes 6152 | tf_op jit(solution)/shard_map/ppermute | solution.py:28
  16.9 5.8 %collective-permute-start.3 = (f32[4,128]{1,0:T(4,128)S(1)}, f32[4,128]{1,0:T(4,128)S(1)}, u32[]{:S(2)}, u32[]{:S(2)}) collective-permute-start(f32[4,128]{1,0:T(4,128)S(1)} %constant_dynamic-slice_fusion), channel_id=1, source_target_pairs={{0,16},{4,20},{8,24},{12,28},{1,17},{5,21},{9,25},{13,29},{2,18},{... | collective-permute-start | bytes 6152 | tf_op jit(solution)/shard_map/ppermute | solution.py:28
  28.8 0.6 copy-start.6
  33.1 34.6 %collective-permute-start.6 = (bf16[96,4096]{1,0:T(8,128)(2,1)}, bf16[96,4096]{1,0:T(8,128)(2,1)S(1)}, u32[]{:S(2)}, u32[]{:S(2)}) collective-permute-start(bf16[96,4096]{1,0:T(8,128)(2,1)} %shard_map.55.refs_0_.d0), channel_id=1, source_target_pairs={{0,1},{1,0},{2,3},{3,2},{4,5},{5,4},{6,7},{7,6},{8,9},{9,8},{10,11... | collective-permute-start | bytes 2359304 | tf_op jit(solution)/shard_map/ppermute | solution.py:33
  35.6 38.9 %collective-permute-start.7 = (bf16[96,4096]{1,0:T(8,128)(2,1)}, bf16[96,4096]{1,0:T(8,128)(2,1)S(1)}, u32[]{:S(2)}, u32[]{:S(2)}) collective-permute-start(bf16[96,4096]{1,0:T(8,128)(2,1)} %shard_map.55.refs_0_.d0), channel_id=1, source_target_pairs={{0,2},{1,3},{2,0},{3,1},{4,6},{5,7},{6,4},{7,5},{8,10},{9,11},{10,... | collective-permute-start | bytes 2359304 | tf_op jit(solution)/shard_map/ppermute | solution.py:33
  37.1 1.2 copy-start.2
  38.3 22.2 %copy-start.3 = (bf16[96,4096]{1,0:T(8,128)(2,1)S(1)}, bf16[96,4096]{1,0:T(8,128)(2,1)}, u32[]{:S(2)}) copy-start(bf16[96,4096]{1,0:T(8,128)(2,1)} %shard_map.56.d1) | copy-start | bytes 2359300
  60.5 14.0 %copy-start = (bf16[4096,1024]{1,0:T(8,128)(2,1)}, bf16[4096,1024]{1,0:T(8,128)(2,1)S(1)}, u32[]{:S(2)}) copy-start(bf16[4096,1024]{1,0:T(8,128)(2,1)S(1)} %get-tuple-element.55.refs_1_.wk_ref) | copy-start | bytes 25165828
  67.2 18.7 %collective-permute-start.9 = (bf16[96,4096]{1,0:T(8,128)(2,1)S(1)}, bf16[96,4096]{1,0:T(8,128)(2,1)S(1)}, u32[]{:S(2)}, u32[]{:S(2)}) collective-permute-start(bf16[96,4096]{1,0:T(8,128)(2,1)S(1)} %collective-permute-done.5.d1), channel_id=1, source_target_pairs={{0,1},{1,0},{2,3},{3,2},{4,5},{5,4},{6,7},{7,6},{8,9},{9,8},{10,11... | collective-permute-start | bytes 2359304 | tf_op jit(solution)/shard_map/ppermute | solution.py:33
  67.7 18.5 %collective-permute-start.8 = (bf16[96,4096]{1,0:T(8,128)(2,1)S(1)}, bf16[96,4096]{1,0:T(8,128)(2,1)S(1)}, u32[]{:S(2)}, u32[]{:S(2)}) collective-permute-start(bf16[96,4096]{1,0:T(8,128)(2,1)S(1)} %collective-permute-done.6.d0), channel_id=1, source_target_pairs={{0,2},{1,3},{2,0},{3,1},{4,6},{5,7},{6,4},{7,5},{8,10},{9,11},{10,... | collective-permute-start | bytes 2359304 | tf_op jit(solution)/shard_map/ppermute | solution.py:33
  86.1 3.4 %copy-start.1 = (bf16[4096,1024]{1,0:T(8,128)(2,1)S(1)}, bf16[4096,1024]{1,0:T(8,128)(2,1)}, u32[]{:S(2)}) copy-start(bf16[4096,1024]{1,0:T(8,128)(2,1)} %copy-done) | copy-start | bytes 25165828
  93.4 1.6 collective-permute-start.10
  95.1 22.0 %collective-permute-start.11 = (bf16[512,128]{1,0:T(8,128)(2,1)S(1)}, bf16[512,128]{1,0:T(8,128)(2,1)S(1)}, u32[]{:S(2)}, u32[]{:S(2)}) collective-permute-start(bf16[512,128]{1,0:T(8,128)(2,1)S(1)} %shard_map.66), channel_id=1, source_target_pairs={{0,8},{4,12},{8,16},{12,20},{16,24},{20,28},{1,9},{5,13},{9,17},{1... | collective-permute-start | bytes 393224 | tf_op jit(solution)/shard_map/ppermute | solution.py:28
  98.6 18.5 %collective-permute-start.12 = (bf16[512,128]{1,0:T(8,128)(2,1)S(1)}, bf16[512,128]{1,0:T(8,128)(2,1)S(1)}, u32[]{:S(2)}, u32[]{:S(2)}) collective-permute-start(bf16[512,128]{1,0:T(8,128)(2,1)S(1)} %shard_map.66), channel_id=1, source_target_pairs={{0,16},{4,20},{8,24},{12,28},{1,17},{5,21},{9,25},{13,29},{2,18},{... | collective-permute-start | bytes 393224 | tf_op jit(solution)/shard_map/ppermute | solution.py:28
  103.1 14.0 %collective-permute-start.13 = (bf16[512,128]{1,0:T(8,128)(2,1)S(1)}, bf16[512,128]{1,0:T(8,128)(2,1)S(1)}, u32[]{:S(2)}, u32[]{:S(2)}) collective-permute-start(bf16[512,128]{1,0:T(8,128)(2,1)S(1)} %shard_map.66), channel_id=1, source_target_pairs={{0,24},{4,28},{1,25},{5,29},{2,26},{6,30},{3,27},{7,31}} | collective-permute-start | bytes 393224 | tf_op jit(solution)/shard_map/ppermute | solution.py:28
  107.9 10.9 %copy-start.4 = (f32[1024]{0:T(1024)S(1)}, f32[1024]{0:T(1024)}, u32[]{:S(2)}) copy-start(f32[1024]{0:T(1024)} %param.8) | copy-start | bytes 12292
  117.2 1.4 collective-permute-start.14
  121.8 20.4 %collective-permute-start.16 = (bf16[192,2048]{1,0:T(8,128)(2,1)S(1)}, bf16[192,2048]{1,0:T(8,128)(2,1)S(1)}, u32[]{:S(2)}, u32[]{:S(2)}) collective-permute-start(bf16[192,2048]{1,0:T(8,128)(2,1)S(1)} %get-tuple-element.92), channel_id=1, source_target_pairs={{0,1},{1,0},{2,3},{3,2},{4,5},{5,4},{6,7},{7,6},{8,9},{9,8},{10,11... | collective-permute-start | bytes 2359304 | tf_op jit(solution)/shard_map/ppermute | solution.py:33
  123.3 20.8 %collective-permute-start.19 = (bf16[192,2048]{1,0:T(8,128)(2,1)S(1)}, bf16[192,2048]{1,0:T(8,128)(2,1)S(1)}, u32[]{:S(2)}, u32[]{:S(2)}) collective-permute-start(bf16[192,2048]{1,0:T(8,128)(2,1)S(1)} %get-tuple-element.97), channel_id=1, source_target_pairs={{0,2},{1,3},{2,0},{3,1},{4,6},{5,7},{6,4},{7,5},{8,10},{9,11},{10,... | collective-permute-start | bytes 2359304 | tf_op jit(solution)/shard_map/ppermute | solution.py:33
  126.8 32.2 %collective-permute-start.15 = (bf16[192,2048]{1,0:T(8,128)(2,1)S(1)}, bf16[192,2048]{1,0:T(8,128)(2,1)S(1)}, u32[]{:S(2)}, u32[]{:S(2)}) collective-permute-start(bf16[192,2048]{1,0:T(8,128)(2,1)S(1)} %get-tuple-element.87), channel_id=1, source_target_pairs={{0,1},{1,0},{2,3},{3,2},{4,5},{5,4},{6,7},{7,6},{8,9},{9,8},{10,11... | collective-permute-start | bytes 2359304 | tf_op jit(solution)/shard_map/ppermute | solution.py:33
  131.5 29.1 %collective-permute-start.18 = (bf16[192,2048]{1,0:T(8,128)(2,1)S(1)}, bf16[192,2048]{1,0:T(8,128)(2,1)S(1)}, u32[]{:S(2)}, u32[]{:S(2)}) collective-permute-start(bf16[192,2048]{1,0:T(8,128)(2,1)S(1)} %get-tuple-element.95), channel_id=1, source_target_pairs={{0,2},{1,3},{2,0},{3,1},{4,6},{5,7},{6,4},{7,5},{8,10},{9,11},{10,... | collective-permute-start | bytes 2359304 | tf_op jit(solution)/shard_map/ppermute | solution.py:33
  132.0 41.3 %slice-start = ((s8[6291456]{0:T(1024)(128)(4,1)}), s8[4194304]{0:T(1024)(128)(4,1)S(1)}, s32[]{:S(2)}) async-start(s8[6291456]{0:T(1024)(128)(4,1)} %bitcast.22), calls=%async_computation | async-start | bytes 8388608
  132.0 41.3 %slice-start.1 = ((s8[6291456]{0:T(1024)(128)(4,1)}), s8[2097152]{0:T(1024)(128)(4,1)S(1)}, s32[]{:S(2)}) async-start(s8[6291456]{0:T(1024)(128)(4,1)} %bitcast.22), calls=%async_computation.1 | async-start | bytes 4194304
  142.4 30.8 %collective-permute-start.21 = (bf16[192,1536]{1,0:T(8,128)(2,1)S(1)}, bf16[192,1536]{1,0:T(8,128)(2,1)S(1)}, u32[]{:S(2)}, u32[]{:S(2)}) collective-permute-start(bf16[192,1536]{1,0:T(8,128)(2,1)S(1)} %get-tuple-element.99), channel_id=1, source_target_pairs={{0,2},{1,3},{2,0},{3,1},{4,6},{5,7},{6,4},{7,5},{8,10},{9,11},{10,... | collective-permute-start | bytes 1769480 | tf_op jit(solution)/shard_map/ppermute | solution.py:33
  144.3 28.9 %collective-permute-start.22 = (bf16[192,1536]{1,0:T(8,128)(2,1)S(1)}, bf16[192,1536]{1,0:T(8,128)(2,1)S(1)}, u32[]{:S(2)}, u32[]{:S(2)}) collective-permute-start(bf16[192,1536]{1,0:T(8,128)(2,1)S(1)} %get-tuple-element.100), channel_id=1, source_target_pairs={{0,1},{1,0},{2,3},{3,2},{4,5},{5,4},{6,7},{7,6},{8,9},{9,8},{10,11... | collective-permute-start | bytes 1769480 | tf_op jit(solution)/shard_map/ppermute | solution.py:33
  144.8 35.0 %collective-permute-start.17 = (bf16[192,512]{1,0:T(8,128)(2,1)S(1)}, bf16[192,512]{1,0:T(8,128)(2,1)S(1)}, u32[]{:S(2)}, u32[]{:S(2)}) collective-permute-start(bf16[192,512]{1,0:T(8,128)(2,1)S(1)} %get-tuple-element.93), channel_id=1, source_target_pairs={{0,2},{1,3},{2,0},{3,1},{4,6},{5,7},{6,4},{7,5},{8,10},{9,11},{10,... | collective-permute-start | bytes 589832 | tf_op jit(solution)/shard_map/ppermute | solution.py:33
  159.1 20.7 %collective-permute-start.20 = (bf16[192,512]{1,0:T(8,128)(2,1)S(1)}, bf16[192,512]{1,0:T(8,128)(2,1)S(1)}, u32[]{:S(2)}, u32[]{:S(2)}) collective-permute-start(bf16[192,512]{1,0:T(8,128)(2,1)S(1)} %get-tuple-element.98), channel_id=1, source_target_pairs={{0,1},{1,0},{2,3},{3,2},{4,5},{5,4},{6,7},{7,6},{8,9},{9,8},{10,11... | collective-permute-start | bytes 589832 | tf_op jit(solution)/shard_map/ppermute | solution.py:33

commit v3 on v2

--- a/solution.py
+++ b/solution.py
@@ -53,97 +53,125 @@
     return lax.dot_general(a, b, (((da,), (db,)), ((), ())), preferred_element_type=F32)
 
 
-def pool_half(fine, tail, first, tail_first):
+def pool(fine, before):
     rows, width = fine.shape[0] // 2, fine.shape[1]
     out_rows, parts = rows // SF, 4
     cols = width // parts
-
-    def kernel(tail_ref, fine_ref, out_ref, ahead_rows, main_rows, pooled, tail_sem, fine_sems, out_sems):
-        here = [pl.ds(n * cols, cols) for n in range(parts)]
-        tail_copy = pltpu.make_async_copy(tail_ref.at[pl.ds(tail_first, 16)], ahead_rows, tail_sem)
-        copies = [
-            pltpu.make_async_copy(fine_ref.at[pl.ds(first, rows), c], main_rows.at[:, c], fine_sems.at[n])
-            for n, c in enumerate(here)
-        ]
-        tail_copy.start()
-        for copy in copies:
-            copy.start()
+    jobs = [(half, n) for half in (1, 0) for n in range(parts)]
+
+    def kernel(before_ref, fine_ref, low_ref, high_ref, ahead_rows, main_rows, pooled, before_sem, fine_sems, out_sems):
+        before_copy = pltpu.make_async_copy(before_ref, ahead_rows, before_sem)
+        copies = []
+        for half, n in jobs:
+            c = pl.ds(n * cols, cols)
+            copies.append(
+                pltpu.make_async_copy(
+                    fine_ref.at[pl.ds(half * rows, rows), c],
+                    main_rows.at[pl.ds(half * rows, rows), c],
+                    fine_sems.at[half * parts + n],
+                )
+            )
+            copies[-1].start()
+        before_copy.start()
         j = lax.broadcasted_iota(jnp.int32, (out_rows, rows), 0) * SF
         i = lax.broadcasted_iota(jnp.int32, (out_rows, rows), 1)
         main = jnp.where((i <= j) & (i > j - SF), 1.0 / SF, 0.0).astype(BF)
         jt = lax.broadcasted_iota(jnp.int32, (out_rows, 16), 0) * SF
         it = lax.broadcasted_iota(jnp.int32, (out_rows, 16), 1) - 16
         ahead = jnp.where((it <= jt) & (it > jt - SF), 1.0 / SF, 0.0).astype(BF)
-        tail_copy.wait()
         outs = []
-        for n, c in enumerate(here):
-            copies[n].wait()
-            total = dot(main, main_rows[:, c]) + dot(ahead, ahead_rows[:, c])
-            pooled[:, c] = total.astype(BF)
-            outs.append(pltpu.make_async_copy(pooled.at[:, c], out_ref.at[:, c], out_sems.at[n]))
-            outs[n].start()
+        for job, (half, n) in enumerate(jobs):
+            c = slice(n * cols, (n + 1) * cols)
+            if half == 1:
+                copies[job].wait()
+                copies[parts + n].wait()
+            elif n == 0:
+                before_copy.wait()
+            tail = main_rows[rows - 16 : rows, c] if half == 1 else ahead_rows[:, c]
+            total = dot(main, main_rows[half * rows : (half + 1) * rows, c]) + dot(ahead, tail)
+            pooled[half, :, c] = total.astype(BF)
+            target = high_ref if half == 1 else low_ref
+            outs.append(
+                pltpu.make_async_copy(pooled.at[half, :, pl.ds(n * cols, cols)], target.at[:, pl.ds(n * cols, cols)], out_sems.at[half * parts + n])
+            )
+            outs[-1].start()
         for copy in outs:
             copy.wait()
 
     return pl.pallas_call(
         kernel,
         in_specs=[ANY, ANY],
-        out_specs=ANY,
-        out_shape=jax.ShapeDtypeStruct((out_rows, width), BF),
+        out_specs=[ANY, ANY],
+        out_shape=[jax.ShapeDtypeStruct((out_rows, width), BF)] * 2,
         scratch_shapes=[
             pltpu.VMEM((16, width), BF),
-            pltpu.VMEM((rows, width), BF),
-            pltpu.VMEM((out_rows, width), BF),
+            pltpu.VMEM((2 * rows, width), BF),
+            pltpu.VMEM((2, out_rows, width), BF),
             pltpu.SemaphoreType.DMA,
-            pltpu.SemaphoreType.DMA((parts,)),
-            pltpu.SemaphoreType.DMA((parts,)),
+            pltpu.SemaphoreType.DMA((2 * parts,)),
+            pltpu.SemaphoreType.DMA((2 * parts,)),
         ],
         compiler_params=params(58 * MIB),
-        cost_estimate=cost(2 * out_rows * rows * width, 2 * rows * width),
-    )(tail, fine)
-
-
-def prepare(raw, *after):
+        cost_estimate=cost(4 * out_rows * rows * width, 4 * rows * width),
+    )(before, fine)
+
+
+def held_back(array, after):
+    def kernel(array_ref, after_ref, out_ref):
+        pass
+
+    return pl.pallas_call(
+        kernel,
+        in_specs=[ANY, ANY],
+        out_specs=ANY,
+        out_shape=jax.ShapeDtypeStruct(array.shape, array.dtype),
+        input_output_aliases={0: 0},
+        compiler_params=params(MIB),
+        cost_estimate=cost(1, 1),
+    )(array, after)
+
+
+def prepare(raw, part, parts, *after):
     depth, kinds, width = raw.shape
     lanes = 128
     tiles = width // lanes
-    per = kinds * tiles
-    rows = raw.reshape(depth, kinds, tiles, lanes).transpose(0, 2, 1, 3).reshape(depth * per, lanes)
-    bk, slots, size = 256, 4, 8 * per
+    per = kinds * tiles // parts
+    group = 256 // per
+    rows = raw.reshape(depth, kinds, tiles, lanes).transpose(0, 2, 1, 3).reshape(depth, parts * per, lanes)
+    bk, slots, wide = 256, 4, 4
     steps = depth // bk
 
     def kernel(raw_ref, *refs):
         w_refs, (buf, sems) = refs[-2 - kinds : -2], refs[-2:]
 
-
         def fetch(step, slot):
             return pltpu.make_async_copy(
-                raw_ref.at[pl.ds(pl.multiple_of(step * bk * per, bk * per), bk * per)], buf.at[slot], sems.at[slot]
+                raw_ref.at[pl.ds(pl.multiple_of(step * bk, bk), bk), pl.ds(part * per, per)], buf.at[slot], sems.at[slot]
             )
 
         for n in range(slots):
             fetch(n, n).start()
-        to = lax.broadcasted_iota(jnp.int32, (size, size), 0)
-        of = lax.broadcasted_iota(jnp.int32, (size, size), 1)
-        order = jnp.where(of == (to % 8) * per + to // 8, 1.0, 0.0).astype(BF)
+        to = lax.broadcasted_iota(jnp.int32, (256, 256), 0)
+        of = lax.broadcasted_iota(jnp.int32, (256, 256), 1)
+        order = jnp.where(of == (to % group) * per + to // group, 1.0, 0.0).astype(BF)
 
         def loop(step, carry):
             slot = lax.rem(step, slots)
             fetch(step, slot).wait()
 
-            def sixteen(i, carry):
-                start = pl.multiple_of(i * 2 * size, 2 * size)
-                low, high = buf[slot, pl.ds(start, size)], buf[slot, pl.ds(start + size, size)]
-                moved = dot(order, jnp.concatenate([low, high], axis=1))
-                k = pl.ds(pl.multiple_of(step * bk + i * 16, 16), 16)
-                for q in range(per):
-                    eight = moved[q * 8 : (q + 1) * 8]
-                    w_refs[q % kinds][k, (q // kinds) * lanes : (q // kinds + 1) * lanes] = jnp.concatenate(
-                        [eight[:, :lanes], eight[:, lanes:]], axis=0
-                    ).astype(BF)
+            def some(i, carry):
+                start = pl.multiple_of(i * wide * group, wide * group)
+                blocks = [buf[slot, pl.ds(start + u * group, group)].reshape(256, lanes) for u in range(wide)]
+                moved = dot(order, jnp.concatenate(blocks, axis=1))
+                first = pl.multiple_of(step * bk + i * wide * group, wide * group)
+                for u in range(wide):
+                    for q in range(per):
+                        w_refs[q % kinds][pl.ds(first + u * group, group), (q // kinds) * lanes : (q // kinds + 1) * lanes] = (
+                            moved[q * group : (q + 1) * group, u * lanes : (u + 1) * lanes].astype(BF)
+                        )
                 return carry
 
-            lax.fori_loop(0, bk // 16, sixteen, 0, unroll=4)
+            lax.fori_loop(0, bk // (wide * group), some, 0, unroll=True)
 
             @pl.when(step + slots < steps)
             def _():
@@ -153,40 +181,43 @@
 
         lax.fori_loop(0, steps, loop, 0)
 
-    return pl.pallas_call(
-        kernel,
-        in_specs=[ANY] * (1 + len(after)),
-        out_specs=[VMEM] * kinds,
-        out_shape=[pltpu.VMEM((depth, width), BF)] * kinds,
-        scratch_shapes=[pltpu.VMEM((slots, bk * per, lanes), BF), pltpu.SemaphoreType.DMA((slots,))],
-        compiler_params=params(10 * MIB),
-        cost_estimate=cost(2 * depth * kinds * width * size, 4 * depth * kinds * width),
-    )(rows, *after)
-
-
-def project(pieces, weights, types):
+    return in_vmem(
+        *pl.pallas_call(
+            kernel,
+            in_specs=[ANY] * (1 + len(after)),
+            out_specs=[VMEM] * kinds,
+            out_shape=[pltpu.VMEM((depth, width // parts), BF)] * kinds,
+            scratch_shapes=[pltpu.VMEM((slots, bk, per, lanes), BF), pltpu.SemaphoreType.DMA((slots,))],
+            compiler_params=params(8 * MIB),
+            cost_estimate=cost(2 * depth * kinds * width * 256 // parts, 4 * depth * kinds * width // parts),
+        )(rows, *after)
+    )
+
+
+def project(pieces, weights, types, *after):
     unit, depth = pieces[0].shape
-    rows, width, cols = 2 * unit, weights[0].shape[1], 512
-    count = len(weights)
+    rows, cols, parts = 2 * unit, weights[0][0].shape[1], len(weights[0])
+    count, width = len(weights), parts * weights[0][0].shape[1]
 
     def kernel(d0, d1, *refs):
-        w_refs, outs, held = refs[:count], refs[count : 2 * count], refs[-1]
+        w_refs, outs, held = refs[: count * parts], refs[-1 - count : -1], refs[-1]
         held[:unit] = d0[...]
         held[unit:] = d1[...]
         for n in range(count):
-            for c in range(0, width, cols):
-                outs[n][:, c : c + cols] = dot(held[...], w_refs[n][:, c : c + cols]).astype(types[n])
+            for c in range(parts):
+                here = slice(c * cols, (c + 1) * cols)
+                outs[n][:, here] = dot(held[...], w_refs[n * parts + c][...]).astype(types[n])
 
     return in_vmem(
         *pl.pallas_call(
             kernel,
-            in_specs=[VMEM] * (2 + count),
+            in_specs=[VMEM] * (2 + count * parts) + [ANY] * len(after),
             out_specs=[VMEM] * count,
             out_shape=[pltpu.VMEM((rows, width), t) for t in types],
             scratch_shapes=[pltpu.VMEM((rows, depth), BF)],
             compiler_params=params(5 * MIB),
             cost_estimate=cost(2 * rows * depth * width * count, 2 * rows * (depth + width)),
-        )(*pieces, *weights)
+        )(*pieces, *[part for array in weights for part in array], *after)
     )
 
 
@@ -238,17 +269,22 @@
     )(me, *[g[1] for g in groups], *[g[2] for g in groups], cum_columns)
 
 
-def last_keys_and_state(pieces, w_k, w_v, known, left):
+def last_keys_and_state(pieces, w_k, w_v, known, left, width):
     unit, depth = pieces[0].shape
-    rows, width, cols = 2 * unit, w_k.shape[1], 512
+    rows, cols, parts = 2 * unit, w_k[0].shape[1], len(w_k)
     here_heads = cols // HD
 
-    def kernel(d0, d1, wk_ref, wv_ref, known_ref, left_ref, k_out, v_out, s_out, held, keys):
+    def kernel(d0, d1, *refs):
+        wk_refs, wv_refs, (known_ref, left_ref, k_out, v_out, s_out, held, keys) = (
+            refs[:parts],
+            refs[parts : 2 * parts],
+            refs[2 * parts :],
+        )
         held[:unit] = d0[...]
         held[unit:] = d1[...]
         for c in range(0, width, cols):
-            k_part = dot(held[...], wk_ref[:, c : c + cols]).astype(BF)
-            v_part = dot(held[...], wv_ref[:, c : c + cols]).astype(BF)
+            k_part = dot(held[...], wk_refs[c // cols][...]).astype(BF)
+            v_part = dot(held[...], wv_refs[c // cols][...]).astype(BF)
             k_out[:, c : c + cols] = k_part
             v_out[:, c : c + cols] = v_part
             first = c // HD
@@ -265,7 +301,7 @@
 
     return pl.pallas_call(
         kernel,
-        in_specs=[VMEM] * 6,
+        in_specs=[VMEM] * (4 + 2 * parts),
         out_specs=[VMEM] * 3,
         out_shape=[
             pltpu.VMEM((rows, width), BF),
@@ -275,13 +311,14 @@
         scratch_shapes=[pltpu.VMEM((rows, depth), BF), pltpu.VMEM((rows, cols), BF)],
         compiler_params=params(5 * MIB),
         cost_estimate=cost(4 * rows * depth * width, 4 * rows * (depth + width)),
-    )(*pieces, w_k, w_v, known, left)
+    )(*pieces, *w_k, *w_v, known, left)
 
 
 def local_attention(me, groups, w_out, cum_columns, cum_rows, width):
     unit = groups[0][0].shape[0] // 2
     rows, heads = cum_columns.shape
-    cols = 2 * HD
+    together = 4 if heads % 4 == 0 else 2
+    cols = together * HD
     blocks = rows // CH
 
     def kernel(me_ref, *refs):
@@ -302,10 +339,10 @@
                 for n, place in enumerate(places):
                     at = (n % 2) * unit
                     to[place, :] = ins[3 * (n // 2) + kind][at : at + unit, lanes]
-            for h in range(2):
+            for h in range(together):
                 here = slice(h * HD, (h + 1) * HD)
-                column = jnp.sum(jnp.where(lane == 2 * pair + h, cc_ref[...], 0.0), axis=1, keepdims=True)
-                row = jnp.sum(jnp.where(sub == 2 * pair + h, cr_ref[...], 0.0), axis=0, keepdims=True)
+                column = jnp.sum(jnp.where(lane == together * pair + h, cc_ref[...], 0.0), axis=1, keepdims=True)
+                row = jnp.sum(jnp.where(sub == together * pair + h, cr_ref[...], 0.0), axis=0, keepdims=True)
                 s[:, here] = (q[:, here].astype(F32) * jnp.exp(column)).astype(BF)
                 state = jnp.zeros((HD, HD), F32)
                 for b in range(blocks):
@@ -329,7 +366,7 @@
                 outs[2 * (n // 2) + 1][at : at + unit, lanes] = s[place, :]
             return carry
 
-        lax.fori_loop(0, heads // 2, loop, 0)
+        lax.fori_loop(0, heads // together, loop, 0)
         w_copy.wait()
 
     outs = pl.pallas_call(
@@ -348,10 +385,10 @@
     return [kept[2 * g : 2 * g + 2] for g in range(4)], kept[8], done
 
 
-def decay_sums(decay_log):
+def decay_sums(decay_log, after):
     heads, rows = decay_log.shape
 
-    def kernel(d_ref, rows_ref, columns_ref, total_ref):
+    def kernel(d_ref, after_ref, rows_ref, columns_ref, total_ref):
         earlier = lax.broadcasted_iota(jnp.int32, (CH, CH), 0) <= lax.broadcasted_iota(jnp.int32, (CH, CH), 1)
         ones = jnp.where(earlier, 1.0, 0.0)
         ahead = jnp.zeros((heads, 1), F32)
@@ -367,12 +404,12 @@
 
     return pl.pallas_call(
         kernel,
-        in_specs=[VMEM],
+        in_specs=[VMEM, ANY],
         out_specs=[VMEM] * 3,
         out_shape=[jax.ShapeDtypeStruct(shape, F32) for shape in ((heads, rows), (rows, heads), (heads, HD))],
         compiler_params=params(SMALL),
         cost_estimate=cost(12 * heads * rows * CH, 12 * heads * rows),
-    )(decay_log)
+    )(decay_log, after)
 
 
 def combined(core, pick, terms, factors, rows, after=()):
@@ -530,19 +567,18 @@
                 copy.start()
                 fine_copies.append(copy)
                 outs.append(pltpu.make_async_copy(kept.at[at], out_ref.at[place], out_sems.at[at]))
-        r = lax.broadcasted_iota(jnp.int32, (tall, coarse), 0) // SF
-        c = lax.broadcasted_iota(jnp.int32, (tall, coarse), 1)
+        r = lax.broadcasted_iota(jnp.int32, (tall, 3 * coarse), 0) // SF
+        c = lax.broadcasted_iota(jnp.int32, (tall, 3 * coarse), 1) % coarse
         spread = jnp.where(r == c, 1.0, 0.0).astype(BF)
         for n in range(len(columns)):
             for m in range(3):
                 term_copies[3 * n + m].wait()
             for piece in range(pieces):
                 at = pieces * n + piece
+                here = slice(piece * coarse, (piece + 1) * coarse)
+                added = dot(spread, jnp.concatenate([term_buf[3 * n + m, here] for m in range(3)], axis=0))
                 fine_copies[at].wait()
-                total = fine_buf[at].astype(F32)
-                for m in range(3):
-                    total += dot(spread, term_buf[3 * n + m, piece * coarse : (piece + 1) * coarse])
-                kept[at] = total.astype(BF)
+                kept[at] = (fine_buf[at].astype(F32) + added).astype(BF)
                 outs[at].start()
         for copy in outs:
             copy.wait()
@@ -581,24 +617,28 @@
     core = jnp.reshape(lax.axis_index("seq") % 2, (1,)).astype(jnp.int32)
 
     before = passed_along(fine_rows[fine_count - 16 :], ("seq", "mp"), 1)
-    p1 = pool_half(fine_rows, fine_rows, fine_count // 2, fine_count // 2 - 16)
+    p0, p1 = pool(fine_rows, before)
     x1 = swapped(p1, "mp", 1)
     y1 = swapped(p1, "mp", 2)
-    p0 = pool_half(fine_rows, before, 0, 0)
     x0 = swapped(p0, "mp", 1)
     y0 = swapped(p0, "mp", 2)
-    cum_rows, cum_columns, total = decay_sums(decay_log)
+    cum_rows, cum_columns, total = decay_sums(decay_log, p0)
     joining, state_weights, final = state_factors(total)
-    w_q, w_k, w_v, w_g = weights = in_vmem(*prepare(w_inputs, p0, joining, state_weights, final))
+    parts = 2
+    weights = [prepare(w_inputs, 0, parts, p0, joining, state_weights, final)]
+    for part in range(1, parts):
+        weights.append(prepare(w_inputs, part, parts, p0))
+    w_q, w_k, w_v, w_g = weights = list(zip(*weights))
     d1 = swapped(y1, "mp", 1)
+
+    types = [BF, BF, BF, F32]
+    first = project([p0, p1], weights, types, y1)
+    x0 = held_back(x0, first[0])
     d0 = swapped(x0, "mp", 2)
-
-    types = [BF, BF, BF, F32]
-    first = project([p0, p1], weights, types)
     second = project([x1, y1], weights, types)
     third = project([x0, y0], weights, types)
     known, left = in_vmem(*known_state(place, [first, second, third], cum_columns, width))
-    k_last, v_last, state = last_keys_and_state([d0, d1], w_k, w_v, known, left)
+    k_last, v_last, state = last_keys_and_state([d0, d1], w_k, w_v, known, left, width)
     k_last, v_last = in_vmem(k_last, v_last)
     other = swapped(state, "seq", 1)
     q_last, g_last = project([d0, d1], [w_q, w_g], [BF, F32])
@@ -621,7 +661,7 @@
     from_y_b = swapped(y_b, "mp", 2)
     own_a, own_b = terms([(*own, 0), (*own, 1)])
     half = model // 2
-    widths = (half - half // 4, half // 4)
+    widths = (half * 11 // 16, half * 5 // 16)
     from_x_b = [swapped(part, "mp", 1) for part in merged(x_b, got_b, widths, own_a)]
     from_y_a = [swapped(part, "mp", 2) for part in merged(y_a, got_a, widths, own_a)]
     out = None

time: 187 us -> 167 us (0.89)
  Pallas kernels: 91.4 us -> 83.2 us
  waiting for transfers between devices: 45.9 us -> 40.6 us
  local copies, waits for them, and re-layouts: 6.97 us -> 2.86 us
  starting transfers between devices: 38.6 us -> 36.3 us
    pallas_call x1 -> x2, Pallas kernels: 22.2 us -> 17.9 us  [prepare(): pl.pallas_call(kernel, in_specs=[ANY] * (1 + len(after)), out_specs=[VMEM...]
    ppermute x6, waiting for transfers between devices: 7.21 us -> 3.07 us  [passed_along(): return lax.ppermute(value, axis, pairs)]
    unnamed x20 -> x16, local copies, waits for them, and re-layouts: 5.96 us -> 1.84 us
    ppermute x17, starting transfers between devices: 18.8 us -> 16 us  [swapped(): return lax.ppermute(value, axis, [(i, i ^ bit) for i in range(peers)])]
    pallas_call x8, Pallas kernels: 35.6 us -> 33.3 us  [the longest x4 23.6 us: project(): pl.pallas_call(kernel, in_specs=[VMEM] * (2 + count * parts) + [ANY] * le...]
  transfers between devices with their start and end apart: 23 -> 23, of which waited for: 9 -> 9; matrix products, arithmetic and copies ran while one was open for 1% -> 0% of each run, Pallas kernels for 43% -> 41%
where the time goes in v3:
time: 167 us; the launch traced here: 164 us
  Pallas kernels  83.2 us (50%)
  waiting for transfers between devices  40.6 us (24%)
  starting transfers between devices  36.3 us (22%)
  local copies, waits for them, and re-layouts  2.86 us (2%)
    ppermute x17, waiting for transfers between devices, swapped(): return lax.ppermute(value, axis, [(i, i ^ bit) for i in range(peers)])  37.5 us
    pallas_call x4, Pallas kernels, project(): pl.pallas_call(kernel, in_specs=[VMEM] * (2 + count * parts) + [ANY] * le...  23.6 us
    ppermute x6, starting transfers between devices, passed_along(): return lax.ppermute(value, axis, pairs)  20.3 us
    pallas_call x2, Pallas kernels, prepare(): pl.pallas_call(kernel, in_specs=[ANY] * (1 + len(after)), out_specs=[VMEM...  17.9 us
    ppermute x17, starting transfers between devices, swapped(): return lax.ppermute(value, axis, [(i, i ^ bit) for i in range(peers)])  16 us
    pallas_call x4, Pallas kernels, output_terms(): pl.pallas_call(kernel, in_specs=[VMEM] * 9, out_specs=[ANY] * 2, out_shap...  12.2 us
    pallas_call x2, Pallas kernels, add_coarse(): pl.pallas_call(kernel, in_specs=[ANY] * len(args), out_specs=ANY, out_sha...  9.19 us
    pallas_call x1, Pallas kernels, local_attention(): pl.pallas_call(kernel, in_specs=[SMEM] + [VMEM] * 14 + [ANY], out_specs=[...  8.16 us
  transfers between devices with their start and end apart: 23, of which 9 were waited for; matrix products, arithmetic and copies ran while one was open for 0% of the time, Pallas kernels for 41%

profile of v3, /device:TPU:0, one launch (start us, length us, event | category | flops | bytes accessed | tf_op | source)
XLA Modules:
  0.0 163.9 jit_solution(11615830962459434565)
XLA Ops:
  0.0 0.9 slice.10
  0.9 4.8 %collective-permute-start = (bf16[16,4096]{1,0:T(8,128)(2,1)S(1)}, bf16[16,4096]{1,0:T(8,128)(2,1)S(1)}, u32[]{:S(2)}, u32[]{:S(2)}) collective-permute-start(bf16[16,4096]{1,0:T(8,128)(2,1)S(1)} %slice.10), channel_id=1, source_target_pairs={{0,1},{1,2},{2,3},{3,4},{4,5},{5,6},{6,7},{7,8},{8,9},{9,10},{10,1... | collective-permute-start | bytes 393224 | tf_op jit(solution)/shard_map/ppermute | solution.py:28
  5.9 2.6 %collective-permute-done.before_ref = bf16[16,4096]{1,0:T(8,128)(2,1)S(1)} collective-permute-done((bf16[16,4096]{1,0:T(8,128)(2,1)S(1)}, bf16[16,4096]{1,0:T(8,128)(2,1)S(1)}, u32[]{:S(2)}, u32[]{:S(2)}) %collective-permute-start) | collective-permute-done | bytes 131104 | tf_op jit(solution)/shard_map/ppermute | solution.py:28
  8.5 0.7 copy-done.4
  9.2 5.1 %shard_map.55 = (bf16[96,4096]{1,0:T(8,128)(2,1)}, bf16[96,4096]{1,0:T(8,128)(2,1)}) custom-call(bf16[16,4096]{1,0:T(8,128)(2,1)} %copy-done.4, bf16[768,4096]{1,0:T(8,128)(2,1)} %fine_ref.5), custom_call_target="tpu_custom_call" | custom-call | flops 603979776 | bytes 6291456 | tf_op jit(solution)/shard_map/pallas_call | solution.py:101
  14.2 3.5 %collective-permute-start.4 = (bf16[96,4096]{1,0:T(8,128)(2,1)}, bf16[96,4096]{1,0:T(8,128)(2,1)S(1)}, u32[]{:S(2)}, u32[]{:S(2)}) collective-permute-start(bf16[96,4096]{1,0:T(8,128)(2,1)} %get-tuple-element.60.d1), channel_id=1, source_target_pairs={{0,2},{1,3},{2,0},{3,1},{4,6},{5,7},{6,4},{7,5},{8,10},{9,11},{10,... | collective-permute-start | bytes 2359304 | tf_op jit(solution)/shard_map/ppermute | solution.py:33
  17.7 0.6 collective-permute-start.5
  18.3 1.4 collective-permute-start.6
  19.7 1.2 copy-done
  20.9 0.8 shard_map.56
  21.7 8.7 %shard_map.58 = (bf16[4096,512]{1,0:T(8,128)(2,1)S(1)}, bf16[4096,512]{1,0:T(8,128)(2,1)S(1)}, bf16[4096,512]{1,0:T(8,128)(2,1)S(1)}, bf16[4096,512]{1,0:T(8,128)(2,1)S(1)}) custom-call(bf16[4096,32,128]{2,1,0:T(8,128)(2,1)} %bitcast.28, bf16[96,4096]{1,0:T(8,128)(2,1)S(1)} %copy-done), custom_call_target="tpu_custom_call" | custom-call | flops 4294967296 | bytes 33554432 | tf_op jit(solution)/shard_map/pallas_call | solution.py:185
  30.5 3.5 %collective-permute-start.2 = (f32[4,128]{1,0:T(4,128)S(1)}, f32[4,128]{1,0:T(4,128)S(1)}, u32[]{:S(2)}, u32[]{:S(2)}) collective-permute-start(f32[4,128]{1,0:T(4,128)S(1)} %constant_dynamic-slice_fusion), channel_id=1, source_target_pairs={{0,8},{4,12},{8,16},{12,20},{16,24},{20,28},{1,9},{5,13},{9,17},{1... | collective-permute-start | bytes 6152 | tf_op jit(solution)/shard_map/ppermute | solution.py:28
  34.0 4.5 %collective-permute-start.3 = (f32[4,128]{1,0:T(4,128)S(1)}, f32[4,128]{1,0:T(4,128)S(1)}, u32[]{:S(2)}, u32[]{:S(2)}) collective-permute-start(f32[4,128]{1,0:T(4,128)S(1)} %constant_dynamic-slice_fusion), channel_id=1, source_target_pairs={{0,16},{4,20},{8,24},{12,28},{1,17},{5,21},{9,25},{13,29},{2,18},{... | collective-permute-start | bytes 6152 | tf_op jit(solution)/shard_map/ppermute | solution.py:28
  38.6 0.7 collective-permute-start.7
  39.4 0.5 collective-permute-done.3
  39.9 9.3 %shard_map.57 = (bf16[4096,512]{1,0:T(8,128)(2,1)S(1)}, bf16[4096,512]{1,0:T(8,128)(2,1)S(1)}, bf16[4096,512]{1,0:T(8,128)(2,1)S(1)}, bf16[4096,512]{1,0:T(8,128)(2,1)S(1)}) custom-call(bf16[4096,32,128]{2,1,0:T(8,128)(2,1)} %bitcast.29, bf16[96,4096]{1,0:T(8,128)(2,1)S(1)} %copy-done, f32[2,4,128]{2,1,0:T(4,128)S(1)} %pad_maximum_fusion.1.refs_1_.refs_2_, ...), custom_call_target="tpu_custom_call" | custom-call | flops 4294967296 | bytes 33554432 | tf_op jit(solution)/shard_map/pallas_call | solution.py:185
  49.2 6.6 %shard_map.59 = (bf16[192,1024]{1,0:T(8,128)(2,1)S(1)}, bf16[192,1024]{1,0:T(8,128)(2,1)S(1)}, bf16[192,1024]{1,0:T(8,128)(2,1)S(1)}, f32[192,1024]{1,0:T(8,128)S(1)}) custom-call(bf16[96,4096]{1,0:T(8,128)(2,1)S(1)} %copy-done, bf16[96,4096]{1,0:T(8,128)(2,1)S(1)} %copy-done.1, bf16[4096,512]{1,0:T(8,128)(2,1)S(1)} %get-tuple-element.62.refs_0_, ...), custom_call_target="tpu_custom_call" | custom-call | flops 6442450944 | bytes 1966080 | tf_op jit(solution)/shard_map/pallas_call | solution.py:212
  55.9 1.0 collective-permute-start.8
  56.9 0.6 collective-permute-start.9
  57.5 6.7 %shard_map.60 = (bf16[192,1024]{1,0:T(8,128)(2,1)S(1)}, bf16[192,1024]{1,0:T(8,128)(2,1)S(1)}, bf16[192,1024]{1,0:T(8,128)(2,1)S(1)}, f32[192,1024]{1,0:T(8,128)S(1)}) custom-call(bf16[96,4096]{1,0:T(8,128)(2,1)S(1)} %collective-permute-done.5.d0, bf16[96,4096]{1,0:T(8,128)(2,1)S(1)} %collective-permute-done.4.refs_8_.d1, ...), custom_call_target="tpu_custom_call" | custom-call | flops 6442450944 | bytes 1966080 | tf_op jit(solution)/shard_map/pallas_call | solution.py:212
  64.2 6.9 %shard_map.62 = (bf16[192,1024]{1,0:T(8,128)(2,1)S(1)}, bf16[192,1024]{1,0:T(8,128)(2,1)S(1)}, bf16[192,1024]{1,0:T(8,128)(2,1)S(1)}, f32[192,1024]{1,0:T(8,128)S(1)}) custom-call(bf16[96,4096]{1,0:T(8,128)(2,1)S(1)} %shard_map.61.d0, bf16[96,4096]{1,0:T(8,128)(2,1)S(1)} %collective-permute-done.7.d1, bf16[4096,512]{1,0:T(8,128)(2,1)S(1)} %get-tuple-element.62.refs_0_, ...), custom_call_target="tpu_custom_call" | custom-call | flops 6442450944 | bytes 1966080 | tf_op jit(solution)/shard_map/pallas_call | solution.py:212
  71.0 1.6 shard_map.64
  72.7 2.3 %collective-permute-done.8.d0 = bf16[96,4096]{1,0:T(8,128)(2,1)S(1)} collective-permute-done((bf16[96,4096]{1,0:T(8,128)(2,1)S(1)}, bf16[96,4096]{1,0:T(8,128)(2,1)S(1)}, u32[]{:S(2)}, u32[]{:S(2)}) %collective-permute-start.8) | collective-permute-done | bytes 786464 | tf_op jit(solution)/shard_map/ppermute | solution.py:33
  74.9 0.7 collective-permute-done.9.d1
  75.7 3.9 %shard_map.65 = (bf16[192,1024]{1,0:T(8,128)(2,1)S(1)}, bf16[192,1024]{1,0:T(8,128)(2,1)S(1)}, bf16[1024,128]{1,0:T(8,128)(2,1)S(1)}) custom-call(bf16[96,4096]{1,0:T(8,128)(2,1)S(1)} %collective-permute-done.8.d0, bf16[96,4096]{1,0:T(8,128)(2,1)S(1)} %collective-permute-done.9.d1, bf16[4096,512]{1,0:T(8,128)(2,1)S(1)} %get-tuple-element.64.refs_2_.refs_0_, ...), custom_call_target="tpu_custom_call" | custom-call | flops 3221225472 | bytes 3932160 | tf_op jit(solution)/shard_map/pallas_call | solution.py:302
  79.7 1.5 collective-permute-done.10.refs_1_.refs_2_
  81.2 1.6 collective-permute-start.11
  82.8 4.6 %collective-permute-start.12 = (bf16[512,128]{1,0:T(8,128)(2,1)S(1)}, bf16[512,128]{1,0:T(8,128)(2,1)S(1)}, u32[]{:S(2)}, u32[]{:S(2)}) collective-permute-start(bf16[512,128]{1,0:T(8,128)(2,1)S(1)} %shard_map.67), channel_id=1, source_target_pairs={{0,16},{4,20},{8,24},{12,28},{1,17},{5,21},{9,25},{13,29},{2,18},{... | collective-permute-start | bytes 393224 | tf_op jit(solution)/shard_map/ppermute | solution.py:28
  87.4 1.3 collective-permute-start.13
  88.7 3.4 %shard_map.63 = (bf16[192,1024]{1,0:T(8,128)(2,1)S(1)}, f32[192,1024]{1,0:T(8,128)S(1)}) custom-call(bf16[96,4096]{1,0:T(8,128)(2,1)S(1)} %collective-permute-done.8.d0, bf16[96,4096]{1,0:T(8,128)(2,1)S(1)} %collective-permute-done.9.d1, bf16[4096,512]{1,0:T(8,128)(2,1)S(1)} %get-tuple-element.62.refs_0_, bf16[4096,512]{1,0:T(8,128)(2,1)S(1)} %get-tuple-element.63.refs_1_, ...), custom_call_target="tpu_custom_call" | custom-call | flops 3221225472 | bytes 1966080 | tf_op jit(solution)/shard_map/pallas_call | solution.py:212
  92.1 8.2 %shard_map.66 = (f32[192,1024]{1,0:T(8,128)S(1)}, bf16[192,1024]{1,0:T(8,128)(2,1)S(1)}, f32[192,1024]{1,0:T(8,128)S(1)}, bf16[192,1024]{1,0:T(8,128)(2,1)S(1)},...) custom-call(s32[1]{0:T(128)} %bitcast.me_ref, ...), custom_call_target="tpu_custom_call" | custom-call | flops 1006632960 | bytes 6291456 | tf_op jit(solution)/shard_map/pallas_call | solution.py:372
  100.5 1.3 collective-permute-done.14.refs_1_
  102.0 3.0 %shard_map.73 = (bf16[192,2048]{1,0:T(8,128)(2,1)S(1)}, bf16[192,2048]{1,0:T(8,128)(2,1)S(1)}) custom-call(f32[192,1024]{1,0:T(8,128)S(1)} %get-tuple-element.101.a0.a1, bf16[192,1024]{1,0:T(8,128)(2,1)S(1)} %get-tuple-element.102.s0.s1, f32[192,1024]{1,0:T(8,128)S(1)} %get-tuple-element.103.z0.z1, f32[192,1024]{1,0:T(8,128)S(1)} %get-tuple-element.101.a0.a1, ...), custom_call_target="tpu_custom_call" | custom-call | flops 1610612736 | bytes 1572864 | tf_op jit(solution)/shard_map/pallas_call | solution.py:512
  105.0 0.5 collective-permute-start.16
  105.5 1.5 collective-permute-start.19
  107.1 3.0 %shard_map.71 = (bf16[192,2048]{1,0:T(8,128)(2,1)S(1)}, bf16[192,2048]{1,0:T(8,128)(2,1)S(1)}) custom-call(f32[192,1024]{1,0:T(8,128)S(1)} %get-tuple-element.93.a0, bf16[192,1024]{1,0:T(8,128)(2,1)S(1)} %get-tuple-element.94.s0, f32[192,1024]{1,0:T(8,128)S(1)} %get-tuple-element.95.z0, f32[192,1024]{1,0:T(8,128)S(1)} %get-tuple-element.96.a1, ...), custom_call_target="tpu_custom_call" | custom-call | flops 1610612736 | bytes 1572864 | tf_op jit(solution)/shard_map/pallas_call | solution.py:512
  110.1 1.5 collective-permute-start.15
  111.6 3.0 %shard_map.72 = (bf16[192,2048]{1,0:T(8,128)(2,1)S(1)}, bf16[192,2048]{1,0:T(8,128)(2,1)S(1)}) custom-call(f32[192,1024]{1,0:T(8,128)S(1)} %get-tuple-element.93.a0, bf16[192,1024]{1,0:T(8,128)(2,1)S(1)} %get-tuple-element.94.s0, f32[192,1024]{1,0:T(8,128)S(1)} %get-tuple-element.95.z0, f32[192,1024]{1,0:T(8,128)S(1)} %get-tuple-element.96.a1, ...), custom_call_target="tpu_custom_call" | custom-call | flops 1610612736 | bytes 1572864 | tf_op jit(solution)/shard_map/pallas_call | solution.py:512
  114.6 0.7 collective-permute-start.18
  115.3 3.2 %shard_map.70 = (bf16[192,2048]{1,0:T(8,128)(2,1)S(1)}, bf16[192,2048]{1,0:T(8,128)(2,1)S(1)}) custom-call(f32[192,1024]{1,0:T(8,128)S(1)} %get-tuple-element.86.a0.a1, bf16[192,1024]{1,0:T(8,128)(2,1)S(1)} %get-tuple-element.87.s0.s1, f32[192,1024]{1,0:T(8,128)S(1)} %get-tuple-element.88.z0.z1, f32[192,1024]{1,0:T(8,128)S(1)} %get-tuple-element.86.a0.a1, ...), custom_call_target="tpu_custom_call" | custom-call | flops 1610612736 | bytes 1572864 | tf_op jit(solution)/shard_map/pallas_call | solution.py:512
  118.5 6.9 %collective-permute-done.16.b = bf16[192,2048]{1,0:T(8,128)(2,1)S(1)} collective-permute-done((bf16[192,2048]{1,0:T(8,128)(2,1)S(1)}, bf16[192,2048]{1,0:T(8,128)(2,1)S(1)}, u32[]{:S(2)}, u32[]{:S(2)}) %collective-permute-start.16) | collective-permute-done | bytes 786464 | tf_op jit(solution)/shard_map/ppermute | solution.py:33
  125.7 1.4 collective-permute-start.21
  127.3 0.7 collective-permute-start.22
  128.0 1.2 collective-permute-start.17
  129.2 13.1 %collective-permute-done.15.refs_1_ = bf16[192,2048]{1,0:T(8,128)(2,1)S(1)} collective-permute-done((bf16[192,2048]{1,0:T(8,128)(2,1)S(1)}, bf16[192,2048]{1,0:T(8,128)(2,1)S(1)}, u32[]{:S(2)}, u32[]{:S(2)}) %collective-permute-start.15) | collective-permute-done | bytes 786464 | tf_op jit(solution)/shard_map/ppermute | solution.py:33
  142.8 11.6 %collective-permute-done.21.refs_2_ = bf16[192,1408]{1,0:T(8,128)(2,1)S(1)} collective-permute-done((bf16[192,1408]{1,0:T(8,128)(2,1)S(1)}, bf16[192,1408]{1,0:T(8,128)(2,1)S(1)}, u32[]{:S(2)}, u32[]{:S(2)}) %collective-permute-start.21) | collective-permute-done | bytes 540704 | tf_op jit(solution)/shard_map/ppermute | solution.py:33
  154.4 5.2 %shard_map.76.refs_6_ = bf16[768,4096]{1,0:T(8,128)(2,1)} custom-call(bf16[768,4096]{1,0:T(8,128)(2,1)S(1)} %bitcast.23, bf16[192,2048]{1,0:T(8,128)(2,1)S(1)} %get-tuple-element.92.after_ref.refs_0_, bf16[192,2048]{1,0:T(8,128)(2,1)S(1)} %collective-permute-done.15.refs_1_, bf16[192,1408]{1,0:T(8,128)(2,1)S(1)} %collective-permute-done.21.refs_2_, ...), custom_call_target="tpu_custom_call" | custom-call | flops 830472192 | bytes 8650752 | tf_op jit(solution)/shard_map/pallas_call | solution.py:592
  159.6 4.0 %shard_map.77 = bf16[768,4096]{1,0:T(8,128)(2,1)} custom-call(bf16[768,4096]{1,0:T(8,128)(2,1)S(1)} %bitcast.23, bf16[192,2048]{1,0:T(8,128)(2,1)S(1)} %get-tuple-element.92.after_ref.refs_0_, bf16[192,2048]{1,0:T(8,128)(2,1)S(1)} %collective-permute-done.15.refs_1_, ...), custom_call_target="tpu_custom_call", output_to_operand_aliasing={{}: (7, {})} | custom-call | flops 377487360 | bytes 3932160 | tf_op jit(solution)/shard_map/pallas_call | solution.py:592
  (50 shorter events, 1.8 us)
Async XLA Ops:
  0.0 19.7 %copy-start.3 = (f32[8,768]{1,0:T(8,128)S(1)}, f32[8,768]{1,0:T(8,128)}, u32[]{:S(2)}) copy-start(f32[8,768]{1,0:T(8,128)} %d_ref.1) | copy-start | bytes 73732
  0.9 7.6 %collective-permute-start = (bf16[16,4096]{1,0:T(8,128)(2,1)S(1)}, bf16[16,4096]{1,0:T(8,128)(2,1)S(1)}, u32[]{:S(2)}, u32[]{:S(2)}) collective-permute-start(bf16[16,4096]{1,0:T(8,128)(2,1)S(1)} %slice.10), channel_id=1, source_target_pairs={{0,1},{1,2},{2,3},{3,4},{4,5},{5,6},{6,7},{7,8},{8,9},{9,10},{10,1... | collective-permute-start | bytes 393224 | tf_op jit(solution)/shard_map/ppermute | solution.py:28
  8.5 0.7 copy-start.4
  14.2 34.9 %collective-permute-start.4 = (bf16[96,4096]{1,0:T(8,128)(2,1)}, bf16[96,4096]{1,0:T(8,128)(2,1)S(1)}, u32[]{:S(2)}, u32[]{:S(2)}) collective-permute-start(bf16[96,4096]{1,0:T(8,128)(2,1)} %get-tuple-element.60.d1), channel_id=1, source_target_pairs={{0,2},{1,3},{2,0},{3,1},{4,6},{5,7},{6,4},{7,5},{8,10},{9,11},{10,... | collective-permute-start | bytes 2359304 | tf_op jit(solution)/shard_map/ppermute | solution.py:33
  17.7 39.8 %collective-permute-start.5 = (bf16[96,4096]{1,0:T(8,128)(2,1)}, bf16[96,4096]{1,0:T(8,128)(2,1)S(1)}, u32[]{:S(2)}, u32[]{:S(2)}) collective-permute-start(bf16[96,4096]{1,0:T(8,128)(2,1)} %get-tuple-element.60.d1), channel_id=1, source_target_pairs={{0,1},{1,0},{2,3},{3,2},{4,5},{5,4},{6,7},{7,6},{8,9},{9,8},{10,11... | collective-permute-start | bytes 2359304 | tf_op jit(solution)/shard_map/ppermute | solution.py:33
  18.3 37.6 %collective-permute-start.6 = (bf16[96,4096]{1,0:T(8,128)(2,1)}, bf16[96,4096]{1,0:T(8,128)(2,1)S(1)}, u32[]{:S(2)}, u32[]{:S(2)}) collective-permute-start(bf16[96,4096]{1,0:T(8,128)(2,1)} %get-tuple-element.59.after_ref.refs_0_.d0), channel_id=1, source_target_pairs={{0,1},{1,0},{2,3},{3,2},{4,5},{5,4},{6,7},{7,6},{8,9},{9,8},{10,11... | collective-permute-start | bytes 2359304 | tf_op jit(solution)/shard_map/ppermute | solution.py:33
  19.7 1.2 copy-start
  21.7 8.8 %collective-permute-start.1 = (f32[8,128]{1,0:T(8,128)S(1)}, f32[8,128]{1,0:T(8,128)S(1)}, u32[]{:S(2)}, u32[]{:S(2)}) collective-permute-start(f32[8,128]{1,0:T(8,128)S(1)} %get-tuple-element.61), channel_id=1, source_target_pairs={{0,4},{4,0},{8,12},{12,8},{16,20},{20,16},{24,28},{28,24},{1,5},{5... | collective-permute-start | bytes 12296 | tf_op jit(solution)/shard_map/ppermute | solution.py:33
  21.7 8.7 %copy-start.5 = (pred[8]{0:T(512)(128)(4,1)S(1)}, pred[8]{0:T(512)(128)(4,1)}, u32[]{:S(2)}) copy-start(pred[8]{0:T(512)(128)(4,1)} %constant.51.clone.1) | copy-start | bytes 28
  30.5 8.1 %collective-permute-start.2 = (f32[4,128]{1,0:T(4,128)S(1)}, f32[4,128]{1,0:T(4,128)S(1)}, u32[]{:S(2)}, u32[]{:S(2)}) collective-permute-start(f32[4,128]{1,0:T(4,128)S(1)} %constant_dynamic-slice_fusion), channel_id=1, source_target_pairs={{0,8},{4,12},{8,16},{12,20},{16,24},{20,28},{1,9},{5,13},{9,17},{1... | collective-permute-start | bytes 6152 | tf_op jit(solution)/shard_map/ppermute | solution.py:28
  34.0 5.8 %collective-permute-start.3 = (f32[4,128]{1,0:T(4,128)S(1)}, f32[4,128]{1,0:T(4,128)S(1)}, u32[]{:S(2)}, u32[]{:S(2)}) collective-permute-start(f32[4,128]{1,0:T(4,128)S(1)} %constant_dynamic-slice_fusion), channel_id=1, source_target_pairs={{0,16},{4,20},{8,24},{12,28},{1,17},{5,21},{9,25},{13,29},{2,18},{... | collective-permute-start | bytes 6152 | tf_op jit(solution)/shard_map/ppermute | solution.py:28
  38.6 25.5 %collective-permute-start.7 = (bf16[96,4096]{1,0:T(8,128)(2,1)S(1)}, bf16[96,4096]{1,0:T(8,128)(2,1)S(1)}, u32[]{:S(2)}, u32[]{:S(2)}) collective-permute-start(bf16[96,4096]{1,0:T(8,128)(2,1)S(1)} %copy-done), channel_id=1, source_target_pairs={{0,2},{1,3},{2,0},{3,1},{4,6},{5,7},{6,4},{7,5},{8,10},{9,11},{10,... | collective-permute-start | bytes 2359304 | tf_op jit(solution)/shard_map/ppermute | solution.py:33
  39.9 9.3 %copy-start.1 = (bf16[96,4096]{1,0:T(8,128)(2,1)S(1)}, bf16[96,4096]{1,0:T(8,128)(2,1)}, u32[]{:S(2)}) copy-start(bf16[96,4096]{1,0:T(8,128)(2,1)} %get-tuple-element.60.d1) | copy-start | bytes 2359300
  55.9 19.1 %collective-permute-start.8 = (bf16[96,4096]{1,0:T(8,128)(2,1)S(1)}, bf16[96,4096]{1,0:T(8,128)(2,1)S(1)}, u32[]{:S(2)}, u32[]{:S(2)}) collective-permute-start(bf16[96,4096]{1,0:T(8,128)(2,1)S(1)} %shard_map.61.d0), channel_id=1, source_target_pairs={{0,2},{1,3},{2,0},{3,1},{4,6},{5,7},{6,4},{7,5},{8,10},{9,11},{10,... | collective-permute-start | bytes 2359304 | tf_op jit(solution)/shard_map/ppermute | solution.py:33
  56.9 18.8 %collective-permute-start.9 = (bf16[96,4096]{1,0:T(8,128)(2,1)S(1)}, bf16[96,4096]{1,0:T(8,128)(2,1)S(1)}, u32[]{:S(2)}, u32[]{:S(2)}) collective-permute-start(bf16[96,4096]{1,0:T(8,128)(2,1)S(1)} %collective-permute-done.4.refs_8_.d1), channel_id=1, source_target_pairs={{0,1},{1,0},{2,3},{3,2},{4,5},{5,4},{6,7},{7,6},{8,9},{9,8},{10,11... | collective-permute-start | bytes 2359304 | tf_op jit(solution)/shard_map/ppermute | solution.py:33
  79.6 1.6 collective-permute-start.10
  81.2 19.1 %collective-permute-start.11 = (bf16[512,128]{1,0:T(8,128)(2,1)S(1)}, bf16[512,128]{1,0:T(8,128)(2,1)S(1)}, u32[]{:S(2)}, u32[]{:S(2)}) collective-permute-start(bf16[512,128]{1,0:T(8,128)(2,1)S(1)} %shard_map.67), channel_id=1, source_target_pairs={{0,8},{4,12},{8,16},{12,20},{16,24},{20,28},{1,9},{5,13},{9,17},{1... | collective-permute-start | bytes 393224 | tf_op jit(solution)/shard_map/ppermute | solution.py:28
  82.8 17.5 %collective-permute-start.12 = (bf16[512,128]{1,0:T(8,128)(2,1)S(1)}, bf16[512,128]{1,0:T(8,128)(2,1)S(1)}, u32[]{:S(2)}, u32[]{:S(2)}) collective-permute-start(bf16[512,128]{1,0:T(8,128)(2,1)S(1)} %shard_map.67), channel_id=1, source_target_pairs={{0,16},{4,20},{8,24},{12,28},{1,17},{5,21},{9,25},{13,29},{2,18},{... | collective-permute-start | bytes 393224 | tf_op jit(solution)/shard_map/ppermute | solution.py:28
  87.4 12.9 %collective-permute-start.13 = (bf16[512,128]{1,0:T(8,128)(2,1)S(1)}, bf16[512,128]{1,0:T(8,128)(2,1)S(1)}, u32[]{:S(2)}, u32[]{:S(2)}) collective-permute-start(bf16[512,128]{1,0:T(8,128)(2,1)S(1)} %shard_map.67), channel_id=1, source_target_pairs={{0,24},{4,28},{1,25},{5,29},{2,26},{6,30},{3,27},{7,31}} | collective-permute-start | bytes 393224 | tf_op jit(solution)/shard_map/ppermute | solution.py:28
  92.1 9.9 %copy-start.2 = (f32[1024]{0:T(1024)S(1)}, f32[1024]{0:T(1024)}, u32[]{:S(2)}) copy-start(f32[1024]{0:T(1024)} %param.8) | copy-start | bytes 12292
  100.4 1.4 collective-permute-start.14
  105.0 20.4 %collective-permute-start.16 = (bf16[192,2048]{1,0:T(8,128)(2,1)S(1)}, bf16[192,2048]{1,0:T(8,128)(2,1)S(1)}, u32[]{:S(2)}, u32[]{:S(2)}) collective-permute-start(bf16[192,2048]{1,0:T(8,128)(2,1)S(1)} %get-tuple-element.104), channel_id=1, source_target_pairs={{0,1},{1,0},{2,3},{3,2},{4,5},{5,4},{6,7},{7,6},{8,9},{9,8},{10,11... | collective-permute-start | bytes 2359304 | tf_op jit(solution)/shard_map/ppermute | solution.py:33
  105.5 21.6 %collective-permute-start.19 = (bf16[192,2048]{1,0:T(8,128)(2,1)S(1)}, bf16[192,2048]{1,0:T(8,128)(2,1)S(1)}, u32[]{:S(2)}, u32[]{:S(2)}) collective-permute-start(bf16[192,2048]{1,0:T(8,128)(2,1)S(1)} %get-tuple-element.109), channel_id=1, source_target_pairs={{0,2},{1,3},{2,0},{3,1},{4,6},{5,7},{6,4},{7,5},{8,10},{9,11},{10,... | collective-permute-start | bytes 2359304 | tf_op jit(solution)/shard_map/ppermute | solution.py:33
  110.1 32.2 %collective-permute-start.15 = (bf16[192,2048]{1,0:T(8,128)(2,1)S(1)}, bf16[192,2048]{1,0:T(8,128)(2,1)S(1)}, u32[]{:S(2)}, u32[]{:S(2)}) collective-permute-start(bf16[192,2048]{1,0:T(8,128)(2,1)S(1)} %get-tuple-element.99), channel_id=1, source_target_pairs={{0,1},{1,0},{2,3},{3,2},{4,5},{5,4},{6,7},{7,6},{8,9},{9,8},{10,11... | collective-permute-start | bytes 2359304 | tf_op jit(solution)/shard_map/ppermute | solution.py:33
  114.6 28.2 %collective-permute-start.18 = (bf16[192,2048]{1,0:T(8,128)(2,1)S(1)}, bf16[192,2048]{1,0:T(8,128)(2,1)S(1)}, u32[]{:S(2)}, u32[]{:S(2)}) collective-permute-start(bf16[192,2048]{1,0:T(8,128)(2,1)S(1)} %get-tuple-element.107), channel_id=1, source_target_pairs={{0,2},{1,3},{2,0},{3,1},{4,6},{5,7},{6,4},{7,5},{8,10},{9,11},{10,... | collective-permute-start | bytes 2359304 | tf_op jit(solution)/shard_map/ppermute | solution.py:33
  115.3 39.1 %slice-start = ((s8[6291456]{0:T(1024)(128)(4,1)}), s8[4194304]{0:T(1024)(128)(4,1)S(1)}, s32[]{:S(2)}) async-start(s8[6291456]{0:T(1024)(128)(4,1)} %bitcast.22), calls=%async_computation | async-start | bytes 8388608
  115.3 39.1 %slice-start.1 = ((s8[6291456]{0:T(1024)(128)(4,1)}), s8[2097152]{0:T(1024)(128)(4,1)S(1)}, s32[]{:S(2)}) async-start(s8[6291456]{0:T(1024)(128)(4,1)} %bitcast.22), calls=%async_computation.1 | async-start | bytes 4194304
  125.7 28.7 %collective-permute-start.21 = (bf16[192,1408]{1,0:T(8,128)(2,1)S(1)}, bf16[192,1408]{1,0:T(8,128)(2,1)S(1)}, u32[]{:S(2)}, u32[]{:S(2)}) collective-permute-start(bf16[192,1408]{1,0:T(8,128)(2,1)S(1)} %get-tuple-element.111), channel_id=1, source_target_pairs={{0,2},{1,3},{2,0},{3,1},{4,6},{5,7},{6,4},{7,5},{8,10},{9,11},{10,... | collective-permute-start | bytes 1622024 | tf_op jit(solution)/shard_map/ppermute | solution.py:33
  127.3 27.0 %collective-permute-start.22 = (bf16[192,1408]{1,0:T(8,128)(2,1)S(1)}, bf16[192,1408]{1,0:T(8,128)(2,1)S(1)}, u32[]{:S(2)}, u32[]{:S(2)}) collective-permute-start(bf16[192,1408]{1,0:T(8,128)(2,1)S(1)} %get-tuple-element.112), channel_id=1, source_target_pairs={{0,1},{1,0},{2,3},{3,2},{4,5},{5,4},{6,7},{7,6},{8,9},{9,8},{10,11... | collective-permute-start | bytes 1622024 | tf_op jit(solution)/shard_map/ppermute | solution.py:33
  128.0 31.6 %collective-permute-start.17 = (bf16[192,640]{1,0:T(8,128)(2,1)S(1)}, bf16[192,640]{1,0:T(8,128)(2,1)S(1)}, u32[]{:S(2)}, u32[]{:S(2)}) collective-permute-start(bf16[192,640]{1,0:T(8,128)(2,1)S(1)} %get-tuple-element.105), channel_id=1, source_target_pairs={{0,2},{1,3},{2,0},{3,1},{4,6},{5,7},{6,4},{7,5},{8,10},{9,11},{10,... | collective-permute-start | bytes 737288 | tf_op jit(solution)/shard_map/ppermute | solution.py:33
  142.3 17.3 %collective-permute-start.20 = (bf16[192,640]{1,0:T(8,128)(2,1)S(1)}, bf16[192,640]{1,0:T(8,128)(2,1)S(1)}, u32[]{:S(2)}, u32[]{:S(2)}) collective-permute-start(bf16[192,640]{1,0:T(8,128)(2,1)S(1)} %get-tuple-element.110), channel_id=1, source_target_pairs={{0,1},{1,0},{2,3},{3,2},{4,5},{5,4},{6,7},{7,6},{8,9},{9,8},{10,11... | collective-permute-start | bytes 737288 | tf_op jit(solution)/shard_map/ppermute | solution.py:33

commit v4 on v3

--- a/solution.py
+++ b/solution.py
@@ -16,7 +16,7 @@
 BF = jnp.bfloat16
 F32 = jnp.float32
 MIB = 2**20
-SMALL = 14 * MIB
+SMALL = 9 * MIB
 ANY = pl.BlockSpec(memory_space=pl.ANY)
 VMEM = pl.BlockSpec(memory_space=pltpu.VMEM)
 SMEM = pl.BlockSpec(memory_space=pltpu.SMEM)
@@ -42,7 +42,7 @@
 
 
 def cost(flops, size):
-    return pl.CostEstimate(flops=int(flops), bytes_accessed=int(size), transcendentals=0)
+    return pl.CostEstimate(flops=int(flops) * 4, bytes_accessed=int(size) * 4, transcendentals=0)
 
 
 def dot(a, b):
@@ -189,7 +189,7 @@
             out_shape=[pltpu.VMEM((depth, width // parts), BF)] * kinds,
             scratch_shapes=[pltpu.VMEM((slots, bk, per, lanes), BF), pltpu.SemaphoreType.DMA((slots,))],
             compiler_params=params(8 * MIB),
-            cost_estimate=cost(2 * depth * kinds * width * 256 // parts, 4 * depth * kinds * width // parts),
+            cost_estimate=cost(1, 1),
         )(rows, *after)
     )
 
@@ -216,7 +216,7 @@
             out_shape=[pltpu.VMEM((rows, width), t) for t in types],
             scratch_shapes=[pltpu.VMEM((rows, depth), BF)],
             compiler_params=params(5 * MIB),
-            cost_estimate=cost(2 * rows * depth * width * count, 2 * rows * (depth + width)),
+            cost_estimate=cost(rows * depth * width * count // 2, rows * (depth + width) // 2),
         )(*pieces, *[part for array in weights for part in array], *after)
     )
 
@@ -269,19 +269,20 @@
     )(me, *[g[1] for g in groups], *[g[2] for g in groups], cum_columns)
 
 
-def last_keys_and_state(pieces, w_k, w_v, known, left, width):
+def last_keys_and_state(pieces, w_k, w_v, known, left, total, width):
     unit, depth = pieces[0].shape
     rows, cols, parts = 2 * unit, w_k[0].shape[1], len(w_k)
     here_heads = cols // HD
 
     def kernel(d0, d1, *refs):
-        wk_refs, wv_refs, (known_ref, left_ref, k_out, v_out, s_out, held, keys) = (
+        wk_refs, wv_refs, (known_ref, left_ref, total_ref, k_out, v_out, s_out, held, keys) = (
             refs[:parts],
             refs[parts : 2 * parts],
             refs[2 * parts :],
         )
         held[:unit] = d0[...]
         held[unit:] = d1[...]
+        s_out[width:] = as_terms(total_ref[...])
         for c in range(0, width, cols):
             k_part = dot(held[...], wk_refs[c // cols][...]).astype(BF)
             v_part = dot(held[...], wv_refs[c // cols][...]).astype(BF)
@@ -301,17 +302,17 @@
 
     return pl.pallas_call(
         kernel,
-        in_specs=[VMEM] * (4 + 2 * parts),
+        in_specs=[VMEM] * (5 + 2 * parts),
         out_specs=[VMEM] * 3,
         out_shape=[
             pltpu.VMEM((rows, width), BF),
             pltpu.VMEM((rows, width), BF),
-            jax.ShapeDtypeStruct((width, HD), BF),
+            jax.ShapeDtypeStruct((width // HD * (HD + 4), HD), BF),
         ],
         scratch_shapes=[pltpu.VMEM((rows, depth), BF), pltpu.VMEM((rows, cols), BF)],
         compiler_params=params(5 * MIB),
         cost_estimate=cost(4 * rows * depth * width, 4 * rows * (depth + width)),
-    )(*pieces, *w_k, *w_v, known, left)
+    )(*pieces, *w_k, *w_v, known, left, total)
 
 
 def local_attention(me, groups, w_out, cum_columns, cum_rows, width):
@@ -407,79 +408,97 @@
         in_specs=[VMEM, ANY],
         out_specs=[VMEM] * 3,
         out_shape=[jax.ShapeDtypeStruct(shape, F32) for shape in ((heads, rows), (rows, heads), (heads, HD))],
-        compiler_params=params(SMALL),
+        compiler_params=params(3 * MIB),
         cost_estimate=cost(12 * heads * rows * CH, 12 * heads * rows),
     )(decay_log, after)
 
 
-def combined(core, pick, terms, factors, rows, after=()):
-    heads = rows // HD
-
-    def kernel(core_ref, *refs):
-        ins, f_ref, out_ref = refs[: len(terms)], refs[len(terms)], refs[-1]
-        for h in range(heads):
-            total = None
-            for n, ref in enumerate(ins):
-                at = pick(n, core_ref[0], h) * HD
-                term = ref[pl.ds(pl.multiple_of(at, HD), HD)].astype(F32) * f_ref[n, h : h + 1, :]
-                total = term if total is None else total + term
-            out_ref[h * HD : (h + 1) * HD] = total.astype(BF)
-
-    return pl.pallas_call(
-        kernel,
-        in_specs=[SMEM] + [VMEM] * (len(terms) + 1) + [ANY] * len(after),
-        out_specs=VMEM,
-        out_shape=jax.ShapeDtypeStruct((rows, HD), BF),
-        compiler_params=params(3 * MIB),
-        cost_estimate=cost(2 * len(terms) * rows * HD, 2 * (len(terms) + 1) * rows * HD),
-    )(core, *terms, factors, *after)
-
-
-def state_factors(total):
-    chips = lax.axis_size("seq") // 2
-    rank = lax.axis_index("seq")
-    core, chip = rank % 2, rank // 2
+def as_terms(decays):
+    high = decays.astype(BF).astype(F32)
+    middle = (decays - high).astype(BF).astype(F32)
+    low = decays - high - middle
+    return jnp.concatenate([high, middle, low, jnp.zeros_like(decays)], axis=0).astype(BF)
+
+
+def from_terms(terms):
+    heads = terms.shape[0] // 4
+    terms = terms.astype(F32)
+    return terms[:heads] + terms[heads : 2 * heads] + terms[2 * heads : 3 * heads]
+
+
+def state_of_chip(core, state, other, total):
     heads = total.shape[0]
     half = heads // 2
-    first = core == 0
-    other = swapped(total, "seq", 1)
-    own_half = lambda value: lax.dynamic_slice_in_dim(value, core * half, half, 0)
-    one = jnp.ones((half, HD), F32)
-    later = jnp.exp(own_half(jnp.where(first, other, total)))
-    joining = jnp.stack([jnp.where(first, later, one), jnp.where(first, one, later)])
-    chip_total = own_half(total + other)
-    weights = []
-    passed = jnp.zeros((half, HD), F32)
-    for d in range(1, chips):
-        weights.append(jnp.where(chip >= d, jnp.exp(passed), 0.0))
-        if d < chips - 1:
-            passed = passed + passed_along(chip_total, "seq", 2 * d)
-    nothing = jnp.zeros((heads, HD), F32)
-    decay = jnp.where(first, 1.0, jnp.exp(other))
-    final = jnp.stack(
-        [
-            jnp.where(first, jnp.concatenate([decay[:half], nothing[half:]]), jnp.concatenate([nothing[:half], decay[half:]])),
-            jnp.where(first, jnp.concatenate([nothing[:half], decay[half:]]), jnp.concatenate([decay[:half], nothing[half:]])),
-            jnp.where(first, nothing, 1.0),
-        ]
-    )
-    return joining, jnp.stack(weights), final
-
-
-def state_of_chip(core, state, other, joining):
-    half = state.shape[0] // 2
-    heads = half // HD
-    return combined(core, lambda n, c, h: c * heads + h, [state, other], joining, half)
-
-
-def entering_state(core, chip_states, other, weights, final, after):
-    half = chip_states[0].shape[0]
-    heads = half // HD
-    entering = combined(core, lambda n, c, h: h, chip_states, weights, half, [after])
-    entering_other = swapped(entering, "seq", 1)
-    return combined(
-        core, lambda n, c, h: h if n == 2 else h % heads, [entering, entering_other, other], final, 2 * half
-    )
+
+    def kernel(core_ref, s_ref, o_ref, total_ref, out_ref):
+        c = core_ref[0]
+        second = c.astype(F32)
+        pick = lambda low, high: (1.0 - second) * low + second * high
+        mine, theirs = total_ref[...], from_terms(o_ref[heads * HD :])
+        decay = jnp.exp(pick(theirs, mine))
+        for_mine, for_theirs = pick(decay, jnp.ones_like(decay)), pick(jnp.ones_like(decay), decay)
+        for h in range(half):
+            rows = pl.ds(pl.multiple_of((c * half + h) * HD, HD), HD)
+            a, b = (pick(x[h : h + 1], x[half + h : half + h + 1]) for x in (for_mine, for_theirs))
+            out_ref[h * HD : (h + 1) * HD] = (s_ref[rows].astype(F32) * a + o_ref[rows].astype(F32) * b).astype(BF)
+        both = mine + theirs
+        out_ref[half * HD :] = as_terms(pick(both[:half], both[half:]))
+
+    return pl.pallas_call(
+        kernel,
+        in_specs=[SMEM] + [VMEM] * 3,
+        out_specs=VMEM,
+        out_shape=jax.ShapeDtypeStruct((half * (HD + 4), HD), BF),
+        compiler_params=params(3 * MIB),
+        cost_estimate=cost(4 * half * HD * HD, 6 * half * HD * HD),
+    )(core, state, other, total)
+
+
+def entering_chip(chip_states, after):
+    half = chip_states[0].shape[0] // (HD + 4)
+
+    def kernel(*refs):
+        ins, out_ref = refs[: len(chip_states)], refs[-1]
+        passed = jnp.zeros((half, HD), F32)
+        weights = []
+        for ref in ins:
+            weights.append(jnp.exp(passed))
+            passed = passed + from_terms(ref[half * HD :])
+        for h in range(half):
+            rows = slice(h * HD, (h + 1) * HD)
+            out_ref[rows] = sum(ref[rows].astype(F32) * w[h : h + 1] for ref, w in zip(ins, weights)).astype(BF)
+
+    return pl.pallas_call(
+        kernel,
+        in_specs=[VMEM] * len(chip_states) + [ANY],
+        out_specs=VMEM,
+        out_shape=jax.ShapeDtypeStruct((half * HD, HD), BF),
+        compiler_params=params(3 * MIB),
+        cost_estimate=cost(6 * half * HD * HD, 8 * half * HD * HD),
+    )(*chip_states, after)
+
+
+def entering_shard(core, entering, entering_other, other):
+    half = entering.shape[0] // HD
+    heads = 2 * half
+
+    def kernel(core_ref, mine_ref, theirs_ref, o_ref, out_ref):
+        second = core_ref[0].astype(F32)
+        decay = (1.0 - second) + second * jnp.exp(from_terms(o_ref[heads * HD :]))
+        for h in range(heads):
+            low, high = (mine_ref, theirs_ref) if h < half else (theirs_ref, mine_ref)
+            rows, here = slice(h * HD, (h + 1) * HD), slice(h % half * HD, (h % half + 1) * HD)
+            state = (1.0 - second) * low[here].astype(F32) + second * high[here].astype(F32)
+            out_ref[rows] = (state * decay[h : h + 1] + second * o_ref[rows].astype(F32)).astype(BF)
+
+    return pl.pallas_call(
+        kernel,
+        in_specs=[SMEM] + [VMEM] * 3,
+        out_specs=VMEM,
+        out_shape=jax.ShapeDtypeStruct((heads * HD, HD), BF),
+        compiler_params=params(3 * MIB),
+        cost_estimate=cost(4 * heads * HD * HD, 8 * heads * HD * HD),
+    )(core, entering, entering_other, other)
 
 
 def output_terms(parts, gain, incoming, w_out):
@@ -623,12 +642,8 @@
     x0 = swapped(p0, "mp", 1)
     y0 = swapped(p0, "mp", 2)
     cum_rows, cum_columns, total = decay_sums(decay_log, p0)
-    joining, state_weights, final = state_factors(total)
     parts = 2
-    weights = [prepare(w_inputs, 0, parts, p0, joining, state_weights, final)]
-    for part in range(1, parts):
-        weights.append(prepare(w_inputs, part, parts, p0))
-    w_q, w_k, w_v, w_g = weights = list(zip(*weights))
+    w_q, w_k, w_v, w_g = weights = list(zip(*[prepare(w_inputs, part, parts, total) for part in range(parts)]))
     d1 = swapped(y1, "mp", 1)
 
     types = [BF, BF, BF, F32]
@@ -638,17 +653,18 @@
     second = project([x1, y1], weights, types)
     third = project([x0, y0], weights, types)
     known, left = in_vmem(*known_state(place, [first, second, third], cum_columns, width))
-    k_last, v_last, state = last_keys_and_state([d0, d1], w_k, w_v, known, left, width)
+    k_last, v_last, state = last_keys_and_state([d0, d1], w_k, w_v, known, left, total, width)
     k_last, v_last = in_vmem(k_last, v_last)
     other = swapped(state, "seq", 1)
     q_last, g_last = project([d0, d1], [w_q, w_g], [BF, F32])
-    chip_state = state_of_chip(core, state, other, joining)
+    chip_state = state_of_chip(core, state, other, total)
     chip_states = [passed_along(chip_state, "seq", 2 * d) for d in range(1, lax.axis_size("seq") // 2)]
     groups, w_kept, attended = local_attention(
         place, [first, second, third, [q_last, k_last, v_last]], pltpu.with_memory_space_constraint(w_out, pltpu.HBM), cum_columns, cum_rows, width
     )
     own, second, third, last = [(*group, gate) for group, gate in zip(groups, (first[3], second[3], third[3], g_last))]
-    incoming = entering_state(core, chip_states, other, state_weights, final, attended)
+    entering = entering_chip(chip_states, attended)
+    incoming = entering_shard(core, entering, swapped(entering, "seq", 1), other)
 
     gain = head_gain[None]
     terms = lambda parts: output_terms(parts, gain, incoming, w_kept)
@@ -665,7 +681,8 @@
     from_x_b = [swapped(part, "mp", 1) for part in merged(x_b, got_b, widths, own_a)]
     from_y_a = [swapped(part, "mp", 2) for part in merged(y_a, got_a, widths, own_a)]
     out = None
-    for n, at in enumerate((0, widths[0])):
+    for n in range(len(widths)):
+        at = sum(widths[:n])
         out = add_coarse(
             fine_rows,
             [

time: 167 us -> 166 us (level)
  starting transfers between devices: 36.3 us -> 31 us
  waiting for transfers between devices: 40.6 us -> 45.2 us
    ppermute x6 -> x4, starting transfers between devices: 20.3 us -> 14.5 us  [passed_along(): return lax.ppermute(value, axis, pairs)]
    ppermute x17 -> x16, waiting for transfers between devices: 37.5 us -> 42.5 us  [swapped(): return lax.ppermute(value, axis, [(i, i ^ bit) for i in range(peers)])]
    ppermute x17 -> x16, starting transfers between devices: 16 us -> 16.5 us  [swapped(): return lax.ppermute(value, axis, [(i, i ^ bit) for i in range(peers)])]
  transfers between devices with their start and end apart: 23 -> 20, of which waited for: 9 -> 7; matrix products, arithmetic and copies ran while one was open for 0% -> 0% of each run, Pallas kernels for 41% -> 41%
where the time goes in v4:
time: 166 us; the launch traced here: 163 us
  Pallas kernels  83.4 us (50%)
  waiting for transfers between devices  45.2 us (27%)
  starting transfers between devices  31 us (19%)
  local copies, waits for them, and re-layouts  2.73 us (2%)
    ppermute x16, waiting for transfers between devices, swapped(): return lax.ppermute(value, axis, [(i, i ^ bit) for i in range(peers)])  42.5 us
    pallas_call x4, Pallas kernels, project(): pl.pallas_call(kernel, in_specs=[VMEM] * (2 + count * parts) + [ANY] * le...  23.8 us
    pallas_call x2, Pallas kernels, prepare(): pl.pallas_call(kernel, in_specs=[ANY] * (1 + len(after)), out_specs=[VMEM...  18 us
    ppermute x16, starting transfers between devices, swapped(): return lax.ppermute(value, axis, [(i, i ^ bit) for i in range(peers)])  16.5 us
    ppermute x4, starting transfers between devices, passed_along(): return lax.ppermute(value, axis, pairs)  14.5 us
    pallas_call x4, Pallas kernels, output_terms(): pl.pallas_call(kernel, in_specs=[VMEM] * 9, out_specs=[ANY] * 2, out_shap...  12.2 us
    pallas_call x2, Pallas kernels, add_coarse(): pl.pallas_call(kernel, in_specs=[ANY] * len(args), out_specs=ANY, out_sha...  9.18 us
    pallas_call x1, Pallas kernels, local_attention(): pl.pallas_call(kernel, in_specs=[SMEM] + [VMEM] * 14 + [ANY], out_specs=[...  8.15 us
  transfers between devices with their start and end apart: 20, of which 7 were waited for; matrix products, arithmetic and copies ran while one was open for 0% of the time, Pallas kernels for 41%

profile of v4, /device:TPU:0, one launch (start us, length us, event | category | flops | bytes accessed | tf_op | source)
XLA Modules:
  0.0 163.1 jit_solution(4536642041517494914)
XLA Ops:
  0.0 0.9 slice.3
  0.9 4.8 %collective-permute-start = (bf16[16,4096]{1,0:T(8,128)(2,1)S(1)}, bf16[16,4096]{1,0:T(8,128)(2,1)S(1)}, u32[]{:S(2)}, u32[]{:S(2)}) collective-permute-start(bf16[16,4096]{1,0:T(8,128)(2,1)S(1)} %slice.3), channel_id=1, source_target_pairs={{0,1},{1,2},{2,3},{3,4},{4,5},{5,6},{6,7},{7,8},{8,9},{9,10},{10,1... | collective-permute-start | bytes 393224 | tf_op jit(solution)/shard_map/ppermute | solution.py:28
  5.8 2.7 %collective-permute-done.before_ref = bf16[16,4096]{1,0:T(8,128)(2,1)S(1)} collective-permute-done((bf16[16,4096]{1,0:T(8,128)(2,1)S(1)}, bf16[16,4096]{1,0:T(8,128)(2,1)S(1)}, u32[]{:S(2)}, u32[]{:S(2)}) %collective-permute-start) | collective-permute-done | bytes 131104 | tf_op jit(solution)/shard_map/ppermute | solution.py:28
  8.5 0.6 copy-done.5
  9.2 5.0 %shard_map.55 = (bf16[96,4096]{1,0:T(8,128)(2,1)}, bf16[96,4096]{1,0:T(8,128)(2,1)}) custom-call(bf16[16,4096]{1,0:T(8,128)(2,1)} %copy-done.5, bf16[768,4096]{1,0:T(8,128)(2,1)} %fine_ref.5), custom_call_target="tpu_custom_call" | custom-call | flops 2415919104 | bytes 25165824 | tf_op jit(solution)/shard_map/pallas_call | solution.py:101
  14.2 3.5 %collective-permute-start.1 = (bf16[96,4096]{1,0:T(8,128)(2,1)}, bf16[96,4096]{1,0:T(8,128)(2,1)S(1)}, u32[]{:S(2)}, u32[]{:S(2)}) collective-permute-start(bf16[96,4096]{1,0:T(8,128)(2,1)} %get-tuple-element.60.d1), channel_id=1, source_target_pairs={{0,2},{1,3},{2,0},{3,1},{4,6},{5,7},{6,4},{7,5},{8,10},{9,11},{10,... | collective-permute-start | bytes 2359304 | tf_op jit(solution)/shard_map/ppermute | solution.py:33
  17.7 0.6 collective-permute-start.3
  18.3 1.4 collective-permute-start.2
  19.7 1.1 copy-done
  20.9 0.8 shard_map.56
  21.6 8.7 %shard_map.57 = (bf16[4096,512]{1,0:T(8,128)(2,1)S(1)}, bf16[4096,512]{1,0:T(8,128)(2,1)S(1)}, bf16[4096,512]{1,0:T(8,128)(2,1)S(1)}, bf16[4096,512]{1,0:T(8,128)(2,1)S(1)}) custom-call(bf16[4096,32,128]{2,1,0:T(8,128)(2,1)} %bitcast.14, f32[8,128]{1,0:T(8,128)S(1)} %get-tuple-element.61.refs_0_.refs_6_.total_ref), custom_call_target="tpu_custom_call" | custom-call | flops 4 | bytes 4 | tf_op jit(solution)/shard_map/pallas_call | solution.py:185
  30.3 9.3 %shard_map.58 = (bf16[4096,512]{1,0:T(8,128)(2,1)S(1)}, bf16[4096,512]{1,0:T(8,128)(2,1)S(1)}, bf16[4096,512]{1,0:T(8,128)(2,1)S(1)}, bf16[4096,512]{1,0:T(8,128)(2,1)S(1)}) custom-call(bf16[4096,32,128]{2,1,0:T(8,128)(2,1)} %bitcast.15, f32[8,128]{1,0:T(8,128)S(1)} %get-tuple-element.61.refs_0_.refs_6_.total_ref), custom_call_target="tpu_custom_call" | custom-call | flops 4 | bytes 4 | tf_op jit(solution)/shard_map/pallas_call | solution.py:185
  39.7 0.1 collective-permute-start.4
  39.8 6.8 %shard_map.59 = (bf16[192,1024]{1,0:T(8,128)(2,1)S(1)}, bf16[192,1024]{1,0:T(8,128)(2,1)S(1)}, bf16[192,1024]{1,0:T(8,128)(2,1)S(1)}, f32[192,1024]{1,0:T(8,128)S(1)}) custom-call(bf16[96,4096]{1,0:T(8,128)(2,1)S(1)} %copy-done.1, bf16[96,4096]{1,0:T(8,128)(2,1)S(1)} %copy-done.2, bf16[4096,512]{1,0:T(8,128)(2,1)S(1)} %get-tuple-element.62.refs_0_, ...), custom_call_target="tpu_custom_call" | custom-call | flops 6442450944 | bytes 1966080 | tf_op jit(solution)/shard_map/pallas_call | solution.py:212
  46.6 2.0 %collective-permute-start.5 = (bf16[96,4096]{1,0:T(8,128)(2,1)S(1)}, bf16[96,4096]{1,0:T(8,128)(2,1)S(1)}, u32[]{:S(2)}, u32[]{:S(2)}) collective-permute-start(bf16[96,4096]{1,0:T(8,128)(2,1)S(1)} %shard_map.61.d0), channel_id=1, source_target_pairs={{0,2},{1,3},{2,0},{3,1},{4,6},{5,7},{6,4},{7,5},{8,10},{9,11},{10,... | collective-permute-start | bytes 2359304 | tf_op jit(solution)/shard_map/ppermute | solution.py:33
  48.6 0.6 collective-permute-start.6
  49.2 6.0 %collective-permute-done.2.d0 = bf16[96,4096]{1,0:T(8,128)(2,1)S(1)} collective-permute-done((bf16[96,4096]{1,0:T(8,128)(2,1)}, bf16[96,4096]{1,0:T(8,128)(2,1)S(1)}, u32[]{:S(2)}, u32[]{:S(2)}) %collective-permute-start.2) | collective-permute-done | bytes 786464 | tf_op jit(solution)/shard_map/ppermute | solution.py:33
  55.2 6.7 %shard_map.60 = (bf16[192,1024]{1,0:T(8,128)(2,1)S(1)}, bf16[192,1024]{1,0:T(8,128)(2,1)S(1)}, bf16[192,1024]{1,0:T(8,128)(2,1)S(1)}, f32[192,1024]{1,0:T(8,128)S(1)}) custom-call(bf16[96,4096]{1,0:T(8,128)(2,1)S(1)} %collective-permute-done.2.d0, bf16[96,4096]{1,0:T(8,128)(2,1)S(1)} %collective-permute-done.1.refs_8_.d1, ...), custom_call_target="tpu_custom_call" | custom-call | flops 6442450944 | bytes 1966080 | tf_op jit(solution)/shard_map/pallas_call | solution.py:212
  62.0 6.9 %shard_map.62 = (bf16[192,1024]{1,0:T(8,128)(2,1)S(1)}, bf16[192,1024]{1,0:T(8,128)(2,1)S(1)}, bf16[192,1024]{1,0:T(8,128)(2,1)S(1)}, f32[192,1024]{1,0:T(8,128)S(1)}) custom-call(bf16[96,4096]{1,0:T(8,128)(2,1)S(1)} %shard_map.61.d0, bf16[96,4096]{1,0:T(8,128)(2,1)S(1)} %collective-permute-done.4.d1, bf16[4096,512]{1,0:T(8,128)(2,1)S(1)} %get-tuple-element.62.refs_0_, ...), custom_call_target="tpu_custom_call" | custom-call | flops 6442450944 | bytes 1966080 | tf_op jit(solution)/shard_map/pallas_call | solution.py:212
  68.9 1.6 shard_map.64
  70.5 3.6 %collective-permute-done.5.d0 = bf16[96,4096]{1,0:T(8,128)(2,1)S(1)} collective-permute-done((bf16[96,4096]{1,0:T(8,128)(2,1)S(1)}, bf16[96,4096]{1,0:T(8,128)(2,1)S(1)}, u32[]{:S(2)}, u32[]{:S(2)}) %collective-permute-start.5) | collective-permute-done | bytes 786464 | tf_op jit(solution)/shard_map/ppermute | solution.py:33
  74.1 3.9 %shard_map.65 = (bf16[192,1024]{1,0:T(8,128)(2,1)S(1)}, bf16[192,1024]{1,0:T(8,128)(2,1)S(1)}, bf16[1056,128]{1,0:T(8,128)(2,1)S(1)}) custom-call(bf16[96,4096]{1,0:T(8,128)(2,1)S(1)} %collective-permute-done.5.d0, bf16[96,4096]{1,0:T(8,128)(2,1)S(1)} %collective-permute-done.6.d1, bf16[4096,512]{1,0:T(8,128)(2,1)S(1)} %get-tuple-element.64.refs_2_.refs_0_, ...), custom_call_target="tpu_custom_call" | custom-call | flops 12884901888 | bytes 15728640 | tf_op jit(solution)/shard_map/pallas_call | solution.py:303
  78.2 3.4 %shard_map.63 = (bf16[192,1024]{1,0:T(8,128)(2,1)S(1)}, f32[192,1024]{1,0:T(8,128)S(1)}) custom-call(bf16[96,4096]{1,0:T(8,128)(2,1)S(1)} %collective-permute-done.5.d0, bf16[96,4096]{1,0:T(8,128)(2,1)S(1)} %collective-permute-done.6.d1, bf16[4096,512]{1,0:T(8,128)(2,1)S(1)} %get-tuple-element.62.refs_0_, bf16[4096,512]{1,0:T(8,128)(2,1)S(1)} %get-tuple-element.63.refs_1_, ...), custom_call_target="tpu_custom_call" | custom-call | flops 3221225472 | bytes 1966080 | tf_op jit(solution)/shard_map/pallas_call | solution.py:212
  81.7 3.9 %collective-permute-start.8 = (bf16[528,128]{1,0:T(8,128)(2,1)S(1)}, bf16[528,128]{1,0:T(8,128)(2,1)S(1)}, u32[]{:S(2)}, u32[]{:S(2)}) collective-permute-start(bf16[528,128]{1,0:T(8,128)(2,1)S(1)} %shard_map.67), channel_id=1, source_target_pairs={{0,8},{4,12},{8,16},{12,20},{16,24},{20,28},{1,9},{5,13},{9,17},{1... | collective-permute-start | bytes 405512 | tf_op jit(solution)/shard_map/ppermute | solution.py:28
  85.5 4.5 %collective-permute-start.9 = (bf16[528,128]{1,0:T(8,128)(2,1)S(1)}, bf16[528,128]{1,0:T(8,128)(2,1)S(1)}, u32[]{:S(2)}, u32[]{:S(2)}) collective-permute-start(bf16[528,128]{1,0:T(8,128)(2,1)S(1)} %shard_map.67), channel_id=1, source_target_pairs={{0,16},{4,20},{8,24},{12,28},{1,17},{5,21},{9,25},{13,29},{2,18},{... | collective-permute-start | bytes 405512 | tf_op jit(solution)/shard_map/ppermute | solution.py:28
  90.0 1.3 collective-permute-start.10
  91.4 8.2 %shard_map.66 = (f32[192,1024]{1,0:T(8,128)S(1)}, bf16[192,1024]{1,0:T(8,128)(2,1)S(1)}, f32[192,1024]{1,0:T(8,128)S(1)}, bf16[192,1024]{1,0:T(8,128)(2,1)S(1)},...) custom-call(s32[1]{0:T(128)} %bitcast.me_ref, ...), custom_call_target="tpu_custom_call" | custom-call | flops 4026531840 | bytes 25165824 | tf_op jit(solution)/shard_map/pallas_call | solution.py:373
  99.7 1.3 collective-permute-done.11.theirs_ref
  101.1 0.2 shard_map.69.in_ref
  101.2 3.0 %shard_map.73 = (bf16[192,2048]{1,0:T(8,128)(2,1)S(1)}, bf16[192,2048]{1,0:T(8,128)(2,1)S(1)}) custom-call(f32[192,1024]{1,0:T(8,128)S(1)} %get-tuple-element.101.a0.a1, bf16[192,1024]{1,0:T(8,128)(2,1)S(1)} %get-tuple-element.102.s0.s1, f32[192,1024]{1,0:T(8,128)S(1)} %get-tuple-element.103.z0.z1, f32[192,1024]{1,0:T(8,128)S(1)} %get-tuple-element.101.a0.a1, ...), custom_call_target="tpu_custom_call" | custom-call | flops 6442450944 | bytes 6291456 | tf_op jit(solution)/shard_map/pallas_call | solution.py:531
  104.2 0.4 collective-permute-start.13
  104.7 1.7 %collective-permute-start.16 = (bf16[192,2048]{1,0:T(8,128)(2,1)S(1)}, bf16[192,2048]{1,0:T(8,128)(2,1)S(1)}, u32[]{:S(2)}, u32[]{:S(2)}) collective-permute-start(bf16[192,2048]{1,0:T(8,128)(2,1)S(1)} %get-tuple-element.109), channel_id=1, source_target_pairs={{0,2},{1,3},{2,0},{3,1},{4,6},{5,7},{6,4},{7,5},{8,10},{9,11},{10,... | collective-permute-start | bytes 2359304 | tf_op jit(solution)/shard_map/ppermute | solution.py:33
  106.3 3.0 %shard_map.71 = (bf16[192,2048]{1,0:T(8,128)(2,1)S(1)}, bf16[192,2048]{1,0:T(8,128)(2,1)S(1)}) custom-call(f32[192,1024]{1,0:T(8,128)S(1)} %get-tuple-element.93.a0, bf16[192,1024]{1,0:T(8,128)(2,1)S(1)} %get-tuple-element.94.s0, f32[192,1024]{1,0:T(8,128)S(1)} %get-tuple-element.95.z0, f32[192,1024]{1,0:T(8,128)S(1)} %get-tuple-element.96.a1, ...), custom_call_target="tpu_custom_call" | custom-call | flops 6442450944 | bytes 6291456 | tf_op jit(solution)/shard_map/pallas_call | solution.py:531
  109.3 3.0 %shard_map.72 = (bf16[192,2048]{1,0:T(8,128)(2,1)S(1)}, bf16[192,2048]{1,0:T(8,128)(2,1)S(1)}) custom-call(f32[192,1024]{1,0:T(8,128)S(1)} %get-tuple-element.93.a0, bf16[192,1024]{1,0:T(8,128)(2,1)S(1)} %get-tuple-element.94.s0, f32[192,1024]{1,0:T(8,128)S(1)} %get-tuple-element.95.z0, f32[192,1024]{1,0:T(8,128)S(1)} %get-tuple-element.96.a1, ...), custom_call_target="tpu_custom_call" | custom-call | flops 6442450944 | bytes 6291456 | tf_op jit(solution)/shard_map/pallas_call | solution.py:531
  112.3 1.7 %collective-permute-start.12 = (bf16[192,2048]{1,0:T(8,128)(2,1)S(1)}, bf16[192,2048]{1,0:T(8,128)(2,1)S(1)}, u32[]{:S(2)}, u32[]{:S(2)}) collective-permute-start(bf16[192,2048]{1,0:T(8,128)(2,1)S(1)} %get-tuple-element.99), channel_id=1, source_target_pairs={{0,1},{1,0},{2,3},{3,2},{4,5},{5,4},{6,7},{7,6},{8,9},{9,8},{10,11... | collective-permute-start | bytes 2359304 | tf_op jit(solution)/shard_map/ppermute | solution.py:33
  114.1 0.4 collective-permute-start.15
  114.4 3.2 %shard_map.70 = (bf16[192,2048]{1,0:T(8,128)(2,1)S(1)}, bf16[192,2048]{1,0:T(8,128)(2,1)S(1)}) custom-call(f32[192,1024]{1,0:T(8,128)S(1)} %get-tuple-element.86.a0.a1, bf16[192,1024]{1,0:T(8,128)(2,1)S(1)} %get-tuple-element.87.s0.s1, f32[192,1024]{1,0:T(8,128)S(1)} %get-tuple-element.88.z0.z1, f32[192,1024]{1,0:T(8,128)S(1)} %get-tuple-element.86.a0.a1, ...), custom_call_target="tpu_custom_call" | custom-call | flops 6442450944 | bytes 6291456 | tf_op jit(solution)/shard_map/pallas_call | solution.py:531
  117.7 7.0 %collective-permute-done.13.b = bf16[192,2048]{1,0:T(8,128)(2,1)S(1)} collective-permute-done((bf16[192,2048]{1,0:T(8,128)(2,1)S(1)}, bf16[192,2048]{1,0:T(8,128)(2,1)S(1)}, u32[]{:S(2)}, u32[]{:S(2)}) %collective-permute-start.13) | collective-permute-done | bytes 786464 | tf_op jit(solution)/shard_map/ppermute | solution.py:33
  124.7 0.2 shard_map.74
  124.9 1.7 %collective-permute-start.18 = (bf16[192,1408]{1,0:T(8,128)(2,1)S(1)}, bf16[192,1408]{1,0:T(8,128)(2,1)S(1)}, u32[]{:S(2)}, u32[]{:S(2)}) collective-permute-start(bf16[192,1408]{1,0:T(8,128)(2,1)S(1)} %get-tuple-element.111), channel_id=1, source_target_pairs={{0,2},{1,3},{2,0},{3,1},{4,6},{5,7},{6,4},{7,5},{8,10},{9,11},{10,... | collective-permute-start | bytes 1622024 | tf_op jit(solution)/shard_map/ppermute | solution.py:33
  126.6 0.2 shard_map.75
  126.9 0.4 collective-permute-start.19
  127.3 1.4 collective-permute-start.14
  128.7 12.8 %collective-permute-done.12.refs_1_ = bf16[192,2048]{1,0:T(8,128)(2,1)S(1)} collective-permute-done((bf16[192,2048]{1,0:T(8,128)(2,1)S(1)}, bf16[192,2048]{1,0:T(8,128)(2,1)S(1)}, u32[]{:S(2)}, u32[]{:S(2)}) %collective-permute-start.12) | collective-permute-done | bytes 786464 | tf_op jit(solution)/shard_map/ppermute | solution.py:33
  141.5 0.4 collective-permute-start.17
  141.9 11.6 %collective-permute-done.18.refs_2_ = bf16[192,1408]{1,0:T(8,128)(2,1)S(1)} collective-permute-done((bf16[192,1408]{1,0:T(8,128)(2,1)S(1)}, bf16[192,1408]{1,0:T(8,128)(2,1)S(1)}, u32[]{:S(2)}, u32[]{:S(2)}) %collective-permute-start.18) | collective-permute-done | bytes 540704 | tf_op jit(solution)/shard_map/ppermute | solution.py:33
  153.5 5.2 %shard_map.76.refs_6_ = bf16[768,4096]{1,0:T(8,128)(2,1)} custom-call(bf16[768,4096]{1,0:T(8,128)(2,1)S(1)} %bitcast.9, bf16[192,2048]{1,0:T(8,128)(2,1)S(1)} %get-tuple-element.92.after_ref.refs_0_, bf16[192,2048]{1,0:T(8,128)(2,1)S(1)} %collective-permute-done.12.refs_1_, bf16[192,1408]{1,0:T(8,128)(2,1)S(1)} %collective-permute-done.18.refs_2_, ...), custom_call_target="tpu_custom_call" | custom-call | flops 3321888768 | bytes 34603008 | tf_op jit(solution)/shard_map/pallas_call | solution.py:611
  158.8 4.0 %shard_map.77 = bf16[768,4096]{1,0:T(8,128)(2,1)} custom-call(bf16[768,4096]{1,0:T(8,128)(2,1)S(1)} %bitcast.9, bf16[192,2048]{1,0:T(8,128)(2,1)S(1)} %get-tuple-element.92.after_ref.refs_0_, bf16[192,2048]{1,0:T(8,128)(2,1)S(1)} %collective-permute-done.12.refs_1_, ...), custom_call_target="tpu_custom_call", output_to_operand_aliasing={{}: (7, {})} | custom-call | flops 1509949440 | bytes 15728640 | tf_op jit(solution)/shard_map/pallas_call | solution.py:611
  (33 shorter events, 0.4 us)
Async XLA Ops:
  0.9 18.8 %copy-start.3 = (f32[8,768]{1,0:T(8,128)S(1)}, f32[8,768]{1,0:T(8,128)}, u32[]{:S(2)}) copy-start(f32[8,768]{1,0:T(8,128)} %d_ref.1) | copy-start | bytes 73732
  0.9 7.6 %collective-permute-start = (bf16[16,4096]{1,0:T(8,128)(2,1)S(1)}, bf16[16,4096]{1,0:T(8,128)(2,1)S(1)}, u32[]{:S(2)}, u32[]{:S(2)}) collective-permute-start(bf16[16,4096]{1,0:T(8,128)(2,1)S(1)} %slice.3), channel_id=1, source_target_pairs={{0,1},{1,2},{2,3},{3,4},{4,5},{5,6},{6,7},{7,8},{8,9},{9,10},{10,1... | collective-permute-start | bytes 393224 | tf_op jit(solution)/shard_map/ppermute | solution.py:28
  8.5 0.7 copy-start.5
  14.2 25.6 %collective-permute-start.1 = (bf16[96,4096]{1,0:T(8,128)(2,1)}, bf16[96,4096]{1,0:T(8,128)(2,1)S(1)}, u32[]{:S(2)}, u32[]{:S(2)}) collective-permute-start(bf16[96,4096]{1,0:T(8,128)(2,1)} %get-tuple-element.60.d1), channel_id=1, source_target_pairs={{0,2},{1,3},{2,0},{3,1},{4,6},{5,7},{6,4},{7,5},{8,10},{9,11},{10,... | collective-permute-start | bytes 2359304 | tf_op jit(solution)/shard_map/ppermute | solution.py:33
  17.7 28.9 %collective-permute-start.3 = (bf16[96,4096]{1,0:T(8,128)(2,1)}, bf16[96,4096]{1,0:T(8,128)(2,1)S(1)}, u32[]{:S(2)}, u32[]{:S(2)}) collective-permute-start(bf16[96,4096]{1,0:T(8,128)(2,1)} %get-tuple-element.59.after_ref.d0), channel_id=1, source_target_pairs={{0,1},{1,0},{2,3},{3,2},{4,5},{5,4},{6,7},{7,6},{8,9},{9,8},{10,11... | collective-permute-start | bytes 2359304 | tf_op jit(solution)/shard_map/ppermute | solution.py:33
  18.3 36.9 %collective-permute-start.2 = (bf16[96,4096]{1,0:T(8,128)(2,1)}, bf16[96,4096]{1,0:T(8,128)(2,1)S(1)}, u32[]{:S(2)}, u32[]{:S(2)}) collective-permute-start(bf16[96,4096]{1,0:T(8,128)(2,1)} %get-tuple-element.60.d1), channel_id=1, source_target_pairs={{0,1},{1,0},{2,3},{3,2},{4,5},{5,4},{6,7},{7,6},{8,9},{9,8},{10,11... | collective-permute-start | bytes 2359304 | tf_op jit(solution)/shard_map/ppermute | solution.py:33
  19.7 1.1 copy-start
  30.3 9.3 %copy-start.1 = (bf16[96,4096]{1,0:T(8,128)(2,1)S(1)}, bf16[96,4096]{1,0:T(8,128)(2,1)}, u32[]{:S(2)}) copy-start(bf16[96,4096]{1,0:T(8,128)(2,1)} %get-tuple-element.59.after_ref.d0) | copy-start | bytes 2359300
  30.3 9.5 %copy-start.2 = (bf16[96,4096]{1,0:T(8,128)(2,1)S(1)}, bf16[96,4096]{1,0:T(8,128)(2,1)}, u32[]{:S(2)}) copy-start(bf16[96,4096]{1,0:T(8,128)(2,1)} %get-tuple-element.60.d1) | copy-start | bytes 2359300
  39.7 22.3 %collective-permute-start.4 = (bf16[96,4096]{1,0:T(8,128)(2,1)S(1)}, bf16[96,4096]{1,0:T(8,128)(2,1)S(1)}, u32[]{:S(2)}, u32[]{:S(2)}) collective-permute-start(bf16[96,4096]{1,0:T(8,128)(2,1)S(1)} %copy-done.1), channel_id=1, source_target_pairs={{0,2},{1,3},{2,0},{3,1},{4,6},{5,7},{6,4},{7,5},{8,10},{9,11},{10,... | collective-permute-start | bytes 2359304 | tf_op jit(solution)/shard_map/ppermute | solution.py:33
  46.6 27.6 %collective-permute-start.5 = (bf16[96,4096]{1,0:T(8,128)(2,1)S(1)}, bf16[96,4096]{1,0:T(8,128)(2,1)S(1)}, u32[]{:S(2)}, u32[]{:S(2)}) collective-permute-start(bf16[96,4096]{1,0:T(8,128)(2,1)S(1)} %shard_map.61.d0), channel_id=1, source_target_pairs={{0,2},{1,3},{2,0},{3,1},{4,6},{5,7},{6,4},{7,5},{8,10},{9,11},{10,... | collective-permute-start | bytes 2359304 | tf_op jit(solution)/shard_map/ppermute | solution.py:33
  48.6 25.5 %collective-permute-start.6 = (bf16[96,4096]{1,0:T(8,128)(2,1)S(1)}, bf16[96,4096]{1,0:T(8,128)(2,1)S(1)}, u32[]{:S(2)}, u32[]{:S(2)}) collective-permute-start(bf16[96,4096]{1,0:T(8,128)(2,1)S(1)} %collective-permute-done.1.refs_8_.d1), channel_id=1, source_target_pairs={{0,1},{1,0},{2,3},{3,2},{4,5},{5,4},{6,7},{7,6},{8,9},{9,8},{10,11... | collective-permute-start | bytes 2359304 | tf_op jit(solution)/shard_map/ppermute | solution.py:33
  78.1 3.5 %collective-permute-start.7 = (bf16[1056,128]{1,0:T(8,128)(2,1)S(1)}, bf16[1056,128]{1,0:T(8,128)(2,1)S(1)}, u32[]{:S(2)}, u32[]{:S(2)}) collective-permute-start(bf16[1056,128]{1,0:T(8,128)(2,1)S(1)} %get-tuple-element.89.s_ref), channel_id=1, source_target_pairs={{0,4},{4,0},{8,12},{12,8},{16,20},{20,16},{24,28},{28,24},{1,5},{5... | collective-permute-start | bytes 811016 | tf_op jit(solution)/shard_map/ppermute | solution.py:33
  81.7 17.9 %collective-permute-start.8 = (bf16[528,128]{1,0:T(8,128)(2,1)S(1)}, bf16[528,128]{1,0:T(8,128)(2,1)S(1)}, u32[]{:S(2)}, u32[]{:S(2)}) collective-permute-start(bf16[528,128]{1,0:T(8,128)(2,1)S(1)} %shard_map.67), channel_id=1, source_target_pairs={{0,8},{4,12},{8,16},{12,20},{16,24},{20,28},{1,9},{5,13},{9,17},{1... | collective-permute-start | bytes 405512 | tf_op jit(solution)/shard_map/ppermute | solution.py:28
  85.5 14.0 %collective-permute-start.9 = (bf16[528,128]{1,0:T(8,128)(2,1)S(1)}, bf16[528,128]{1,0:T(8,128)(2,1)S(1)}, u32[]{:S(2)}, u32[]{:S(2)}) collective-permute-start(bf16[528,128]{1,0:T(8,128)(2,1)S(1)} %shard_map.67), channel_id=1, source_target_pairs={{0,16},{4,20},{8,24},{12,28},{1,17},{5,21},{9,25},{13,29},{2,18},{... | collective-permute-start | bytes 405512 | tf_op jit(solution)/shard_map/ppermute | solution.py:28
  90.0 9.5 %collective-permute-start.10 = (bf16[528,128]{1,0:T(8,128)(2,1)S(1)}, bf16[528,128]{1,0:T(8,128)(2,1)S(1)}, u32[]{:S(2)}, u32[]{:S(2)}) collective-permute-start(bf16[528,128]{1,0:T(8,128)(2,1)S(1)} %shard_map.67), channel_id=1, source_target_pairs={{0,24},{4,28},{1,25},{5,29},{2,26},{6,30},{3,27},{7,31}} | collective-permute-start | bytes 405512 | tf_op jit(solution)/shard_map/ppermute | solution.py:28
  91.3 9.9 %copy-start.4 = (f32[1024]{0:T(1024)S(1)}, f32[1024]{0:T(1024)}, u32[]{:S(2)}) copy-start(f32[1024]{0:T(1024)} %param.8) | copy-start | bytes 12292
  99.6 1.4 collective-permute-start.11
  104.2 20.4 %collective-permute-start.13 = (bf16[192,2048]{1,0:T(8,128)(2,1)S(1)}, bf16[192,2048]{1,0:T(8,128)(2,1)S(1)}, u32[]{:S(2)}, u32[]{:S(2)}) collective-permute-start(bf16[192,2048]{1,0:T(8,128)(2,1)S(1)} %get-tuple-element.104), channel_id=1, source_target_pairs={{0,1},{1,0},{2,3},{3,2},{4,5},{5,4},{6,7},{7,6},{8,9},{9,8},{10,11... | collective-permute-start | bytes 2359304 | tf_op jit(solution)/shard_map/ppermute | solution.py:33
  104.7 22.0 %collective-permute-start.16 = (bf16[192,2048]{1,0:T(8,128)(2,1)S(1)}, bf16[192,2048]{1,0:T(8,128)(2,1)S(1)}, u32[]{:S(2)}, u32[]{:S(2)}) collective-permute-start(bf16[192,2048]{1,0:T(8,128)(2,1)S(1)} %get-tuple-element.109), channel_id=1, source_target_pairs={{0,2},{1,3},{2,0},{3,1},{4,6},{5,7},{6,4},{7,5},{8,10},{9,11},{10,... | collective-permute-start | bytes 2359304 | tf_op jit(solution)/shard_map/ppermute | solution.py:33
  112.3 29.2 %collective-permute-start.12 = (bf16[192,2048]{1,0:T(8,128)(2,1)S(1)}, bf16[192,2048]{1,0:T(8,128)(2,1)S(1)}, u32[]{:S(2)}, u32[]{:S(2)}) collective-permute-start(bf16[192,2048]{1,0:T(8,128)(2,1)S(1)} %get-tuple-element.99), channel_id=1, source_target_pairs={{0,1},{1,0},{2,3},{3,2},{4,5},{5,4},{6,7},{7,6},{8,9},{9,8},{10,11... | collective-permute-start | bytes 2359304 | tf_op jit(solution)/shard_map/ppermute | solution.py:33
  114.1 27.9 %collective-permute-start.15 = (bf16[192,2048]{1,0:T(8,128)(2,1)S(1)}, bf16[192,2048]{1,0:T(8,128)(2,1)S(1)}, u32[]{:S(2)}, u32[]{:S(2)}) collective-permute-start(bf16[192,2048]{1,0:T(8,128)(2,1)S(1)} %get-tuple-element.107), channel_id=1, source_target_pairs={{0,2},{1,3},{2,0},{3,1},{4,6},{5,7},{6,4},{7,5},{8,10},{9,11},{10,... | collective-permute-start | bytes 2359304 | tf_op jit(solution)/shard_map/ppermute | solution.py:33
  114.4 39.1 %slice-start = ((s8[6291456]{0:T(1024)(128)(4,1)}), s8[4194304]{0:T(1024)(128)(4,1)S(1)}, s32[]{:S(2)}) async-start(s8[6291456]{0:T(1024)(128)(4,1)} %bitcast.8), calls=%async_computation | async-start | bytes 8388608
  114.4 39.1 %slice-start.1 = ((s8[6291456]{0:T(1024)(128)(4,1)}), s8[2097152]{0:T(1024)(128)(4,1)S(1)}, s32[]{:S(2)}) async-start(s8[6291456]{0:T(1024)(128)(4,1)} %bitcast.8), calls=%async_computation.1 | async-start | bytes 4194304
  124.9 28.6 %collective-permute-start.18 = (bf16[192,1408]{1,0:T(8,128)(2,1)S(1)}, bf16[192,1408]{1,0:T(8,128)(2,1)S(1)}, u32[]{:S(2)}, u32[]{:S(2)}) collective-permute-start(bf16[192,1408]{1,0:T(8,128)(2,1)S(1)} %get-tuple-element.111), channel_id=1, source_target_pairs={{0,2},{1,3},{2,0},{3,1},{4,6},{5,7},{6,4},{7,5},{8,10},{9,11},{10,... | collective-permute-start | bytes 1622024 | tf_op jit(solution)/shard_map/ppermute | solution.py:33
  126.9 26.7 %collective-permute-start.19 = (bf16[192,1408]{1,0:T(8,128)(2,1)S(1)}, bf16[192,1408]{1,0:T(8,128)(2,1)S(1)}, u32[]{:S(2)}, u32[]{:S(2)}) collective-permute-start(bf16[192,1408]{1,0:T(8,128)(2,1)S(1)} %get-tuple-element.112), channel_id=1, source_target_pairs={{0,1},{1,0},{2,3},{3,2},{4,5},{5,4},{6,7},{7,6},{8,9},{9,8},{10,11... | collective-permute-start | bytes 1622024 | tf_op jit(solution)/shard_map/ppermute | solution.py:33
  127.3 31.5 %collective-permute-start.14 = (bf16[192,640]{1,0:T(8,128)(2,1)S(1)}, bf16[192,640]{1,0:T(8,128)(2,1)S(1)}, u32[]{:S(2)}, u32[]{:S(2)}) collective-permute-start(bf16[192,640]{1,0:T(8,128)(2,1)S(1)} %get-tuple-element.105), channel_id=1, source_target_pairs={{0,2},{1,3},{2,0},{3,1},{4,6},{5,7},{6,4},{7,5},{8,10},{9,11},{10,... | collective-permute-start | bytes 737288 | tf_op jit(solution)/shard_map/ppermute | solution.py:33
  141.5 17.2 %collective-permute-start.17 = (bf16[192,640]{1,0:T(8,128)(2,1)S(1)}, bf16[192,640]{1,0:T(8,128)(2,1)S(1)}, u32[]{:S(2)}, u32[]{:S(2)}) collective-permute-start(bf16[192,640]{1,0:T(8,128)(2,1)S(1)} %get-tuple-element.110), channel_id=1, source_target_pairs={{0,1},{1,0},{2,3},{3,2},{4,5},{5,4},{6,7},{7,6},{8,9},{9,8},{10,11... | collective-permute-start | bytes 737288 | tf_op jit(solution)/shard_map/ppermute | solution.py:33
